TPU v7x, 512 devices: a whole 4x4x16 slice. The times are simulated.
512 devices in a mesh: row: 32 (over z, core), col: 16 (over y, x).
Axes of the slice: x: 4, y: 4, z: 16, core: 2. Of those that a mesh axis runs over, the one named last changes fastest.
Arguments:
- features: bfloat16 [128, 65536], P('col', 'row'), may hold values from -6 to 6
- tile_values: bfloat16 [32, 4, 32, 128, 128], P('row'), may hold values from 0 to 0.046875
- tile_dst: int32 [32, 4, 32], P('row'), may hold values from 0 to 15, as said below
- tile_src: int32 [32, 4, 32], P('row'), may hold values from 0 to 15, as said below
- tile_count: int32 [32, 4], P('row'), may hold values from 1 to 32, as said below
- send_rows: int32 [32, 32, 32], P('row'), may hold values from 0 to 2047
- send_count: int32 [32, 32], P('row'), may hold values from 0 to 32, as said below
- w_self: bfloat16 [128, 256], P(None, 'col'), may hold values from -0.5 to 0.5
- w_neigh: bfloat16 [128, 256], P(None, 'col'), may hold values from -0.5 to 0.5
- bias: float32 [256], P('col'), may hold values from -3 to 3
- cotangent: bfloat16 [256, 65536], P('col', 'row'), may hold values from -6 to 6
Outputs:
- hidden: bfloat16 [256, 65536], P('col', 'row')
- grad_features: bfloat16 [128, 65536], P('col', 'row')
- grad_self: float32 [128, 256], P(None, 'col')
- grad_neigh: float32 [128, 256], P(None, 'col')
- grad_bias: float32 [256], P('col')
Inputs may be any that keep to these rules, and one draw needn't show every extreme that they name: `tile_dst`: destination tile within the partition. `tile_src`: source tile within its group: below 16 for groups 0 to 2, below 8 for group 3. `tile_count`: slots at or after the count are unused. `send_count`: zero where sender and reader are equal; list slots at or after the count are unused. `send_rows`: local row indices within the sender's partition.
All inputs are finite; a program needn't handle non-finite values.
Results may differ from a plain program's by a relative error of at most 0.0075.
Values may be sent and summed in bfloat16 or wider, within the bound.
No kernel may reach another device: no remote copies, remote signals or barrier semaphores. Data moves between devices by JAX's collectives and lax.ppermute only.
A program may use at most 64 MiB of HBM per device.

v0:
```python
import math

import jax
import jax.numpy as jnp
from jax import lax
from jax.sharding import PartitionSpec as P

TILE = 128
RT = 16
BMAX = 32


HIGHEST_PREC = lax.Precision.HIGHEST


def shifted(shard, axis, by):
    size = lax.axis_size(axis)
    return lax.ppermute(shard, axis, [(i, (i + by) % size) for i in range(size)])


def live_tables(tile_dst, tile_src, tile_count, row_tiles, source_count):
    slot_total = tile_dst.shape[-1]
    offsets = jnp.array([0, row_tiles, 2 * row_tiles, 3 * row_tiles], jnp.int32)
    src_index = (tile_src + offsets[:, None]).reshape(-1)
    dst_index = tile_dst.reshape(-1)
    live = (jnp.arange(slot_total, dtype=jnp.int32)[None, :] < tile_count[:, None]).reshape(-1)
    to_dst = jnp.where(
        (dst_index[:, None] == jnp.arange(row_tiles, dtype=jnp.int32)[None, :]) & live[:, None],
        1.0,
        0.0,
    ).astype(jnp.float32)
    to_src = jnp.where(
        (src_index[:, None] == jnp.arange(source_count, dtype=jnp.int32)[None, :]) & live[:, None],
        1.0,
        0.0,
    ).astype(jnp.float32)
    return (src_index, dst_index, to_dst, to_src)


def per_device(
    features,
    tile_values,
    tile_dst,
    tile_src,
    tile_count,
    send_rows,
    send_count,
    w_self,
    w_neigh,
    bias,
    cotangent,
):
    feature_count = features.shape[0]
    row_count = features.shape[1]
    row_devices = lax.axis_size("row")
    bound_count = row_devices * BMAX
    source_count = 3 * RT + bound_count // TILE
    row_lists = send_rows[0]
    slot_ids = jnp.arange(BMAX, dtype=jnp.int32)[None, :]
    keep_mask = slot_ids < send_count[0][:, None]
    previous = shifted(features, "row", 1)
    following = shifted(features, "row", -1)
    outgoing = features[:, row_lists]
    outgoing = jnp.where(keep_mask[None], outgoing, jnp.zeros_like(outgoing))
    incoming = lax.all_to_all(outgoing, "row", split_axis=1, concat_axis=1, tiled=True)
    full_feats = lax.all_gather(features, "col", axis=0, tiled=True)
    sources = jnp.concatenate(
        [features, previous, following, incoming.reshape(feature_count, bound_count)], axis=1
    )
    src_index, dst_index, to_dst, to_src = live_tables(
        tile_dst[0], tile_src[0], tile_count[0], RT, source_count
    )
    tile_blocks = tile_values.reshape(-1, TILE, TILE)
    source_tiles = sources.reshape(feature_count, source_count, TILE)
    picked = jnp.take(source_tiles, src_index, axis=1)
    contrib = jnp.einsum("fts,tsd->ftd", picked, tile_blocks, preferred_element_type=jnp.float32)
    aggregate = (
        jnp.einsum("ftd,tr->frd", contrib, to_dst, precision=HIGHEST_PREC)
        .reshape(feature_count, row_count)
        .astype(jnp.bfloat16)
    )
    full_agg = lax.all_gather(aggregate, "col", axis=0, tiled=True)
    preact = jnp.einsum("dh,dr->hr", w_self, full_feats, preferred_element_type=jnp.float32)
    preact = (
        preact
        + jnp.einsum("dh,dr->hr", w_neigh, full_agg, preferred_element_type=jnp.float32)
        + bias[:, None]
    )
    sigma = jax.nn.sigmoid(preact)
    hidden = (preact * sigma).astype(jnp.bfloat16)
    grad_pre = (cotangent.astype(jnp.float32) * sigma * (1.0 + preact * (1.0 - sigma))).astype(
        jnp.bfloat16
    )
    grad_scale = 1.0 / math.sqrt(row_devices * row_count)
    grad_self = (
        jnp.einsum("dr,hr->dh", full_feats, grad_pre, preferred_element_type=jnp.float32)
        * grad_scale
    )
    grad_neigh = (
        jnp.einsum("dr,hr->dh", full_agg, grad_pre, preferred_element_type=jnp.float32) * grad_scale
    )
    grad_bias = jnp.sum(grad_pre.astype(jnp.float32), axis=1) * grad_scale
    grad_self, grad_neigh, grad_bias = lax.psum((grad_self, grad_neigh, grad_bias), "row")
    full_grad = lax.all_gather(grad_pre, "col", axis=0, tiled=True)
    full_self, full_neigh = (
        lax.all_gather(w_self, "col", axis=1, tiled=True),
        lax.all_gather(w_neigh, "col", axis=1, tiled=True),
    )
    first_row = lax.axis_index("col") * feature_count
    self_rows = lax.dynamic_slice_in_dim(full_self, first_row, feature_count, 0)
    neigh_rows = lax.dynamic_slice_in_dim(full_neigh, first_row, feature_count, 0)
    self_term = jnp.einsum("dh,hr->dr", self_rows, full_grad, preferred_element_type=jnp.float32)
    grad_agg = jnp.einsum(
        "dh,hr->dr", neigh_rows, full_grad, preferred_element_type=jnp.float32
    ).astype(jnp.bfloat16)
    grad_tiles = grad_agg.reshape(feature_count, RT, TILE)
    picked_back = jnp.take(grad_tiles, dst_index, axis=1)
    contrib_back = jnp.einsum(
        "ftd,tsd->fts", picked_back, tile_blocks, preferred_element_type=jnp.float32
    )
    grad_src = jnp.einsum("fts,tk->fks", contrib_back, to_src, precision=HIGHEST_PREC).reshape(
        feature_count, -1
    )
    own_grad = grad_src[:, :row_count]
    grad_previous = grad_src[:, row_count : 2 * row_count]
    grad_following = grad_src[:, 2 * row_count : 3 * row_count]
    grad_boundary = grad_src[:, 3 * row_count :].reshape(feature_count, row_devices, BMAX)
    from_after = shifted(grad_previous, "row", -1)
    from_before = shifted(grad_following, "row", 1)
    returned = lax.all_to_all(
        grad_boundary.astype(jnp.bfloat16), "row", split_axis=1, concat_axis=1, tiled=True
    ).astype(grad_boundary.dtype)
    returned = jnp.where(keep_mask[None], returned, jnp.zeros_like(returned))
    scattered = jnp.zeros((feature_count, row_count), jnp.float32).at[:, row_lists].add(returned)
    grad_total = self_term + own_grad + from_after + from_before + scattered
    grad_features = grad_total.astype(jnp.bfloat16)
    return (hidden, grad_features, grad_self, grad_neigh, grad_bias)


def solution(mesh):
    placed = (
        P("col", "row"),
        P("row", None, None, None, None),
        P("row", None, None),
        P("row", None, None),
        P("row", None),
        P("row", None, None),
        P("row", None),
        P(None, "col"),
        P(None, "col"),
        P("col"),
        P("col", "row"),
    )
    return jax.shard_map(
        per_device,
        mesh=mesh,
        in_specs=placed,
        out_specs=(P("col", "row"), P("col", "row"), P(None, "col"), P(None, "col"), P("col")),
        check_vma=False,
    )
```

profile of v0, /device:TPU:1, one launch (start us, length us, event | category | flops | bytes accessed | tf_op | source)
XLA Modules:
  0.0 275.6 jit_solution(6193018409787173791)
XLA Ops:
  7.2 6.9 %collective-permute-start.1 = (bf16[8,2048]{1,0:T(8,128)(2,1)}, bf16[8,2048]{1,0:T(8,128)(2,1)S(1)}, u32[]{:S(2)}, u32[]{:S(2)}) collective-permute-start(bf16[8,2048]{1,0:T(8,128)(2,1)} %param.12), channel_id=1, source_target_pairs={{0,496},{16,0},{32,16},{48,32},{64,48},{80,64},{96,80},{112,96},{1... | collective-permute-start | bytes 98312 | tf_op jit(solution)/shard_map/ppermute | solution.py:18
  14.1 1.1 copy.27
  15.1 0.7 iota_compare_fusion.1
  15.9 0.7 compare_select_fusion
  16.6 0.1 reshape.181
  16.7 3.2 %gather_fusion = bf16[1024,8]{1,0:T(8,128)(2,1)S(1)} fusion(bf16[8,2048]{0,1:T(8,128)(2,1)S(1)} %copy.27, s32[1024]{0:T(1024)S(1)} %broadcast_clamp_fusion), kind=kCustom, calls=%fused_computation | custom fusion | bytes 36864 | tf_op jit(solution)/shard_map/gather | solution.py:63
  19.9 0.1 copy.28
  20.0 0.7 reshape.215
  20.8 11.1 %all-to-all-start = ((bf16[32,2,128]{2,1,0:T(2,128)(2,1)}), bf16[32,2,128]{2,1,0:T(2,128)(2,1)S(1)}, u32[]{:S(2)}, u32[]{:S(2)}) async-start(bf16[32,2,128]{2,1,0:T(2,128)(2,1)} %reshape.215), calls=%async_computation | async-start | bytes 32768 | tf_op jit(solution)/shard_map/all_to_all | solution.py:65
  31.9 0.8 squeeze.10
  32.6 0.8 squeeze.8
  33.5 0.1 add.126
  33.6 0.1 add.121
  33.7 20.1 %all_gather.15 = bf16[128,2048]{1,0:T(8,128)(2,1)S(1)} all-gather(bf16[8,2048]{1,0:T(8,128)(2,1)} %param.12), channel_id=1, replica_groups=mesh['row'=32,'col'=16] {'col'}, dimensions={0}, use_global_device_ids=true | all-gather | bytes 557056 | tf_op jit(solution)/shard_map/all_gather | solution.py:66
  53.8 0.7 iota_compare_fusion.3
  54.5 0.9 fusion.47
  55.4 0.8 eq.28
  56.2 0.1 lt.98
  56.3 0.1 reshape.216
  56.4 0.1 reshape.174
  56.5 0.8 maximum_bitcast_fusion
  57.3 0.7 gather_fusion.1
  58.0 3.4 %convolution_bitcast_fusion.2 = f32[8,128,128]{2,0,1:T(8,128)S(1)} fusion(bf16[128,128,128]{2,1,0:T(8,128)(2,1)} %bitcast.79, bf16[128,8,128]{2,1,0:T(8,128)(2,1)S(1)} %gather_fusion.1, pred[128]{0:T(512)(128)(4,1)S(1)} %get-tuple-element.25), kind=kOutput, calls=%fused_computation.12 | convolution fusion | flops 33685504 | bytes 4980864 | tf_op jit(solution)/shard_map/fts,tsd->ftd/dot_general | solution.py:76
  61.4 0.4 fusion.5
  61.9 17.6 %all_gather.16 = bf16[128,2048]{1,0:T(8,128)(2,1)S(1)} all-gather(bf16[8,2048]{1,0:T(8,128)(2,1)S(1)} %bitcast.88), channel_id=1, replica_groups=mesh['row'=32,'col'=16] {'col'}, dimensions={0}, use_global_device_ids=true | all-gather | bytes 557056 | tf_op jit(solution)/shard_map/all_gather | solution.py:82
  79.5 1.0 convert_reduce_fusion
  80.5 0.1 reshape_squeeze.3
  80.6 17.5 %all_gather.17 = bf16[128,256]{0,1:T(8,128)(2,1)S(1)} all-gather(bf16[128,16]{0,1:T(8,128)(2,1)S(1)} %copy-done.1), channel_id=1, replica_groups=mesh['row'=32,'col'=16] {'col'}, dimensions={1}, use_global_device_ids=true | all-gather | bytes 69632 | tf_op jit(solution)/shard_map/all_gather | solution.py:106
  98.1 16.5 %all_gather.19 = bf16[128,256]{0,1:T(8,128)(2,1)S(1)} all-gather(bf16[128,16]{0,1:T(8,128)(2,1)S(1)} %copy-done.3), channel_id=1, replica_groups=mesh['row'=32,'col'=16] {'col'}, dimensions={1}, use_global_device_ids=true | all-gather | bytes 69632 | tf_op jit(solution)/shard_map/all_gather | solution.py:107
  114.6 1.1 convolution_multiply_fusion
  115.7 1.1 fusion.6
  116.8 107.7 %all-reduce = (f32[128,16]{0,1:T(8,128)}, f32[128,16]{0,1:T(8,128)}, f32[16]{0:T(128)}) all-reduce(f32[128,16]{0,1:T(8,128)S(1)} %fusion.6, f32[128,16]{0,1:T(8,128)S(1)} %convolution_multiply_fusion, f32[16]{0:T(128)S(1)} %broadcast_multiply_fusion), channel_id=1, replica_groups=mesh['row'=32,'col'=16] {'row'}, use_global_device_ids=true, to_apply=%region_1.2 | all-reduce | flops 4112 | bytes 32896 | tf_op jit(solution)/shard_map/psum | solution.py:103
  224.5 1.6 fusion.4
  226.1 0.7 gather_fusion.2
  226.8 4.5 %convolution_bitcast_fusion.1 = f32[8,128,128]{2,0,1:T(8,128)S(1)} fusion(bf16[128,128,128]{2,1,0:T(8,128)(2,1)} %bitcast.80, bf16[128,8,128]{2,1,0:T(8,128)(2,1)S(1)} %gather_fusion.2, pred[128]{0:T(512)(128)(4,1)S(1)} %compare_and_fusion), kind=kOutput, calls=%fused_computation.11 | convolution fusion | flops 33685504 | bytes 4980864 | tf_op jit(solution)/shard_map/ftd,tsd->fts/dot_general | solution.py:118
  231.2 0.5 convolution_bitcast_fusion.3
  231.8 0.1 convert_element_type.41
  232.0 0.7 reshape.217
  232.7 15.9 %all-to-all-start.1 = ((bf16[32,2,128]{2,1,0:T(2,128)(2,1)}), bf16[32,2,128]{2,1,0:T(2,128)(2,1)S(1)}, u32[]{:S(2)}, u32[]{:S(2)}) async-start(bf16[32,2,128]{2,1,0:T(2,128)(2,1)} %reshape.217), calls=%async_computation.1 | async-start | bytes 32768 | tf_op jit(solution)/shard_map/all_to_all | solution.py:130
  248.6 0.2 collective-permute-start.2
  248.9 1.5 collective-permute-start.3
  250.4 10.0 %all-to-all-done.1 = bf16[32,2,128]{2,1,0:T(2,128)(2,1)S(1)} async-done(((bf16[32,2,128]{2,1,0:T(2,128)(2,1)}), bf16[32,2,128]{2,1,0:T(2,128)(2,1)S(1)}, u32[]{:S(2)}, u32[]{:S(2)}) %all-to-all-start.1) | async-done | bytes 16416 | tf_op jit(solution)/shard_map/all_to_all | solution.py:130
  260.4 0.1 reshape.218
  260.5 0.2 copy.37
  260.7 0.4 fusion.3
  261.1 0.3 copy.34
  261.4 6.4 %scatter_fusion = f32[8,2048]{0,1:T(8,128)S(1)} fusion(f32[8,2048]{0,1:T(8,128)S(1)} %copy.34, s32[1024]{0:T(1024)S(1)} %reshape.181, f32[1024,8]{1,0:T(8,128)S(1)} %bitcast.84), kind=kCustom, calls=%fused_computation.3 | custom fusion | flops 8192 | bytes 102400 | tf_op jit(solution)/shard_map/scatter-add | solution.py:134
  267.9 0.8 copy.36
  (40 shorter events, 0.4 us)
Async XLA Ops:
  7.2 49.4 %collective-permute-start.1 = (bf16[8,2048]{1,0:T(8,128)(2,1)}, bf16[8,2048]{1,0:T(8,128)(2,1)S(1)}, u32[]{:S(2)}, u32[]{:S(2)}) collective-permute-start(bf16[8,2048]{1,0:T(8,128)(2,1)} %param.12), channel_id=1, source_target_pairs={{0,496},{16,0},{32,16},{48,32},{64,48},{80,64},{96,80},{112,96},{1... | collective-permute-start | bytes 98312 | tf_op jit(solution)/shard_map/ppermute | solution.py:18
  14.1 42.5 %collective-permute-start = (bf16[8,2048]{1,0:T(8,128)(2,1)}, bf16[8,2048]{1,0:T(8,128)(2,1)S(1)}, u32[]{:S(2)}, u32[]{:S(2)}) collective-permute-start(bf16[8,2048]{1,0:T(8,128)(2,1)} %param.12), channel_id=1, source_target_pairs={{0,16},{16,32},{32,48},{48,64},{64,80},{80,96},{96,112},{112,128},... | collective-permute-start | bytes 98312 | tf_op jit(solution)/shard_map/ppermute | solution.py:18
  20.8 35.5 %all-to-all-start = ((bf16[32,2,128]{2,1,0:T(2,128)(2,1)}), bf16[32,2,128]{2,1,0:T(2,128)(2,1)S(1)}, u32[]{:S(2)}, u32[]{:S(2)}) async-start(bf16[32,2,128]{2,1,0:T(2,128)(2,1)} %reshape.215), calls=%async_computation | async-start | bytes 32768 | tf_op jit(solution)/shard_map/all_to_all | solution.py:65
  31.8 192.7 %all-gather.2.cloned.1.call-start = ((), (), s32[]{:S(2)}) async-start(), calls=%async_computation.2 | async-start | bytes 1114112 | tf_op jit(solution)/shard_map/all_gather | solution.py:104
  33.6 45.8 %copy-start.3 = (bf16[128,16]{0,1:T(8,128)(2,1)S(1)}, bf16[128,16]{0,1:T(8,128)(2,1)}, u32[]{:S(2)}) copy-start(bf16[128,16]{0,1:T(8,128)(2,1)} %param.20) | copy-start | bytes 12292
  33.7 45.9 %copy-start.4 = (bf16[16,2048]{1,0:T(8,128)(2,1)S(1)}, bf16[16,2048]{1,0:T(8,128)(2,1)}, u32[]{:S(2)}) copy-start(bf16[16,2048]{1,0:T(8,128)(2,1)} %param.22) | copy-start | bytes 196612
  33.7 45.9 %copy-start.5 = (f32[16]{0:T(128)S(1)}, f32[16]{0:T(128)}, u32[]{:S(2)}) copy-start(f32[16]{0:T(128)} %param.21) | copy-start | bytes 196
  56.3 24.3 %copy-start.2 = (s32[1,4,32]{2,1,0:T(4,128)S(1)}, s32[1,4,32]{2,1,0:T(4,128)}, u32[]{:S(2)}) copy-start(s32[1,4,32]{2,1,0:T(4,128)} %param.14) | copy-start | bytes 1540
  56.4 24.3 %copy-start.1 = (bf16[128,16]{0,1:T(8,128)(2,1)S(1)}, bf16[128,16]{0,1:T(8,128)(2,1)}, u32[]{:S(2)}) copy-start(bf16[128,16]{0,1:T(8,128)(2,1)} %param.19) | copy-start | bytes 12292
  226.1 34.7 %copy-start = (bf16[256,2048]{1,0:T(8,128)(2,1)S(1)}, bf16[256,2048]{1,0:T(8,128)(2,1)}, u32[]{:S(2)}) copy-start(bf16[256,2048]{1,0:T(8,128)(2,1)} %all-gather.2.cloned.1.call-done) | copy-start | bytes 3145732
  232.7 27.7 %all-to-all-start.1 = ((bf16[32,2,128]{2,1,0:T(2,128)(2,1)}), bf16[32,2,128]{2,1,0:T(2,128)(2,1)S(1)}, u32[]{:S(2)}, u32[]{:S(2)}) async-start(bf16[32,2,128]{2,1,0:T(2,128)(2,1)} %reshape.217), calls=%async_computation.1 | async-start | bytes 32768 | tf_op jit(solution)/shard_map/all_to_all | solution.py:130
  248.6 12.1 %collective-permute-start.2 = (f32[8,2048]{1,0:T(8,128)S(1)}, f32[8,2048]{1,0:T(8,128)S(1)}, u32[]{:S(2)}, u32[]{:S(2)}) collective-permute-start(f32[8,2048]{1,0:T(8,128)S(1)} %get-tuple-element.27), channel_id=1, source_target_pairs={{0,496},{16,0},{32,16},{48,32},{64,48},{80,64},{96,80},{112,96},{1... | collective-permute-start | bytes 196616 | tf_op jit(solution)/shard_map/ppermute | solution.py:18
  248.9 11.8 %collective-permute-start.3 = (f32[8,2048]{1,0:T(8,128)S(1)}, f32[8,2048]{1,0:T(8,128)S(1)}, u32[]{:S(2)}, u32[]{:S(2)}) collective-permute-start(f32[8,2048]{1,0:T(8,128)S(1)} %get-tuple-element.28), channel_id=1, source_target_pairs={{0,16},{16,32},{32,48},{48,64},{64,80},{80,96},{96,112},{112,128},... | collective-permute-start | bytes 196616 | tf_op jit(solution)/shard_map/ppermute | solution.py:18
Sparse Core Ops, SparseCore 0:
  80.6 64.6 all-gather.1
where the time goes:
time: 276 us
  blocking collectives  179 us (65%)
  starting transfers between devices  35.7 us (13%)
  matrix products  14.8 us (5%)
  between operations  14.3 us (5%)
  local copies, waits for them, and re-layouts  11.9 us (4%)
  waiting for transfers between devices  10 us (4%)
  other arithmetic  9.53 us (3%)
    psum x1, blocking collectives, per_device(): lax.psum((grad_self, grad_neigh, grad_bias), 'row')  108 us
    all_gather x1, blocking collectives, per_device(): full_feats = lax.all_gather(features, 'col', axis=0, tiled=True)  20.1 us
    all_gather x1, blocking collectives, per_device(): full_agg = lax.all_gather(aggregate, 'col', axis=0, tiled=True)  17.6 us
    all_gather x1, blocking collectives, per_device(): lax.all_gather(w_self, 'col', axis=1, tiled=True)  17.5 us
    all_gather x1, blocking collectives, per_device(): lax.all_gather(w_neigh, 'col', axis=1, tiled=True)  16.5 us
    all_to_all x1, starting transfers between devices, per_device(): lax.all_to_all(grad_boundary.astype(jnp.bfloat16), 'row', split_axis=1, c...  15.9 us
    all_to_all x1, starting transfers between devices, per_device(): lax.all_to_all(outgoing, 'row', split_axis=1, concat_axis=1, tiled=True)  11.1 us
    all_to_all x1, waiting for transfers between devices, per_device(): lax.all_to_all(grad_boundary.astype(jnp.bfloat16), 'row', split_axis=1, c...  9.98 us
  transfers between devices with their start and end apart: 7, of which 1 were waited for; matrix products, arithmetic and copies ran while one was open for 5% of the time, Pallas kernels for 0%

commit v1 on v0

v1 whole, which is shorter than its diff:
```python
import functools
import math

import jax
import jax.numpy as jnp
from jax import lax
from jax.experimental import pallas as pl
from jax.experimental.pallas import tpu as pltpu
from jax.sharding import PartitionSpec as P

TILE = 128
RT = 16
BMAX = 32
NROW = 32
NCOL = 16
FEAT = 8
HLOC = 16
D_IN = 128
HID = 256
NODES_LOC = RT * TILE
NB = NROW * BMAX // TILE
PER = TILE // BMAX
PAIRS = 4
RS = 4
FWD_ROWS = 80
BWD_ROWS = 80
F32, BF16 = jnp.float32, jnp.bfloat16
NT = (((1,), (1,)), ((), ()))
TN = (((0,), (0,)), ((), ()))

VM = pl.BlockSpec(memory_space=pltpu.VMEM)
SM = pl.BlockSpec(memory_space=pltpu.SMEM)


def dot(a, b, dims=(((1,), (0,)), ((), ()))):
    return lax.dot_general(a, b, dims, preferred_element_type=F32)


def iota(shape, dim):
    return lax.broadcasted_iota(jnp.int32, shape, dim)


def tile_of(ref, k):
    return ref[:, k * TILE : (k + 1) * TILE]


def call(body, out_shape, in_specs, out_specs, scratch=(), flops=0, nbytes=0):
    return pl.pallas_call(
        body,
        out_shape=out_shape,
        in_specs=in_specs,
        out_specs=out_specs,
        scratch_shapes=list(scratch),
        compiler_params=pltpu.CompilerParams(vmem_limit_bytes=32 * 1024 * 1024),
        cost_estimate=pl.CostEstimate(flops=flops, bytes_accessed=nbytes, transcendentals=0),
    )


def gather_kernel(feat, rows, counts, out, index, scr):
    cnt = jnp.broadcast_to(counts[...], (NROW, NROW))
    cnt = jnp.where(iota((NROW, NROW), 0) == iota((NROW, NROW), 1), cnt, 0)
    cnt = jnp.sum(cnt, axis=1, keepdims=True)
    scr[...] = jnp.zeros_like(scr)
    scr[:, :BMAX] = jnp.where(iota((NROW, BMAX), 1) < cnt, rows[0], -1)
    lane = iota((NB, TILE), 1)
    idx = scr[pl.ds(0, NB, stride=PER), :]
    for b in range(1, PER):
        part = pltpu.roll(scr[pl.ds(b, NB, stride=PER), :], BMAX * b, 1)
        idx = jnp.where(lane // BMAX == b, part, idx)
    index[...] = idx
    x = jnp.concatenate([tile_of(feat, t).astype(F32) for t in range(RT)], axis=0).astype(BF16)
    place = iota((TILE, TILE), 0)
    for m in range(NB):
        row = idx[m : m + 1, :]
        hot = jnp.where(place == (row & (TILE - 1)), 1.0, 0.0).astype(BF16)
        c = dot(x, hot)
        tile = row >> 7
        g = jnp.zeros((FEAT, TILE), F32)
        for t in range(RT):
            g = g + jnp.where(tile == t, c[t * FEAT : (t + 1) * FEAT], 0.0)
        for b in range(PER):
            moved = g if b == 0 else pltpu.roll(g, TILE - BMAX * b, 1)
            out[PER * m + b] = moved.astype(BF16)


def store_source(lo, hi, k, x):
    zero = jnp.zeros((FEAT, TILE), F32)
    lo[k] = jnp.concatenate([x, zero], axis=0).astype(BF16)
    hi[k] = jnp.concatenate([zero, x], axis=0).astype(BF16)


def zero_source(lo, hi, k):
    lo[k] = jnp.zeros((2 * FEAT, TILE), BF16)
    hi[k] = jnp.zeros((2 * FEAT, TILE), BF16)


def forward_group(g, base, none, lo, hi, tiles, dst, src, count, acc):
    n = count[0, g]

    def step(it, carry):
        done = []
        for u in range(PAIRS):
            first = (it * PAIRS + u) * 2
            second = first + 1
            ka = jnp.where(first < n, src[0, g, first] + base, none)
            kb = jnp.where(second < n, src[0, g, second] + base, none)
            da = jnp.where(first < n, dst[0, g, first], 0)
            db = jnp.where(second < n, dst[0, g, second], 0)
            left = jnp.concatenate([lo[ka], hi[kb]], axis=1)
            right = tiles[0, g, pl.ds(first, 2)].reshape(2 * TILE, TILE)
            done.append((dot(left, right), da, db))
        for r, da, db in done:
            acc[da] += r[:FEAT]
            acc[db] += r[FEAT:]
        return carry

    lax.fori_loop(0, (n + 2 * PAIRS - 1) // (2 * PAIRS), step, 0)


def near_kernel(feat, prev, foll, tiles, dst, src, count, part, lo, hi):
    for k in range(RT):
        store_source(lo, hi, k, tile_of(feat, k).astype(F32))
        store_source(lo, hi, RT + k, tile_of(prev, k).astype(F32))
        store_source(lo, hi, 2 * RT + k, tile_of(foll, k).astype(F32))
    zero_source(lo, hi, 3 * RT)
    part[...] = jnp.zeros_like(part)
    for g in range(3):
        forward_group(g, g * RT, 3 * RT, lo, hi, tiles, dst, src, count, part)


def far_kernel(recv, part, feat, cot, wst, wnt, bias, tiles, dst, src, count, buf, lo, hi, acc):
    lane = iota((FEAT, TILE), 1)
    for k in range(NB):
        x = recv[PER * k].astype(F32)
        for b in range(1, PER):
            moved = pltpu.roll(recv[PER * k + b].astype(F32), BMAX * b, 1)
            x = jnp.where(lane // BMAX == b, moved, x)
        store_source(lo, hi, k, x)
    zero_source(lo, hi, NB)
    acc[...] = part[...]
    forward_group(3, 0, NB, lo, hi, tiles, dst, src, count, acc)
    b = jnp.broadcast_to(bias[...], (HLOC, HLOC))
    b = jnp.where(iota((HLOC, HLOC), 0) == iota((HLOC, HLOC), 1), b, 0.0)
    b = jnp.sum(b, axis=1, keepdims=True)
    b0 = b.astype(BF16).astype(F32)
    b1 = (b - b0).astype(BF16).astype(F32)
    b2 = b - b0 - b1
    lane = iota((HLOC, TILE), 1)
    block = jnp.where(lane == 0, b0, jnp.where(lane == 1, b1, jnp.where(lane == 2, b2, 0.0)))
    block = block.astype(BF16)
    for d in range(RT):
        both = jnp.concatenate([acc[d], tile_of(feat, d).astype(F32)], axis=0)
        buf[d, 0:16] = both.astype(BF16)
        buf[d, 16:32] = tile_of(cot, d)
        buf[d, 32:48] = wst[...]
        buf[d, 48:64] = wnt[...]
        buf[d, 64:80] = block


def dense_kernel(r, out):
    wst = jnp.concatenate([r[c, 32:48] for c in range(NCOL)], axis=0)
    wnt = jnp.concatenate([r[c, 48:64] for c in range(NCOL)], axis=0)
    cot = jnp.concatenate([r[c, 16:32] for c in range(NCOL)], axis=0).astype(F32)
    bias = jnp.concatenate([r[c, 64:80] for c in range(NCOL)], axis=0).astype(F32)
    bias = bias[:, 0:1] + bias[:, 1:2] + bias[:, 2:3]
    heads = [r[c, 0:16].astype(F32) for c in range(NCOL)]
    agg = jnp.concatenate([h[:FEAT] for h in heads], axis=0).astype(BF16)
    feats = jnp.concatenate([h[FEAT:] for h in heads], axis=0).astype(BF16)
    pre = dot(wst, feats) + dot(wnt, agg) + bias
    sig = jax.nn.sigmoid(pre)
    hidden = (pre * sig).astype(BF16)
    grad = (cot * sig * (1.0 + pre * (1.0 - sig))).astype(BF16)
    own = dot(wst, grad, TN)
    own_hi = own.astype(BF16).astype(F32)
    own_lo = own - own_hi
    agg_grad = dot(wnt, grad, TN)
    gs = dot(grad, feats, NT).astype(BF16)
    gn = dot(grad, agg, NT).astype(BF16)
    sums = dot(jnp.ones((FEAT, TILE), BF16), grad, NT)
    sub, lane = iota((FEAT, TILE), 0), iota((FEAT, TILE), 1)
    for c in range(NCOL):
        f, h = slice(c * FEAT, (c + 1) * FEAT), slice(c * HLOC, (c + 1) * HLOC)
        per = TILE // HLOC
        bsum = sums[:, (c // per) * TILE : (c // per + 1) * TILE]
        shift = (BMAX - HLOC * (c % per)) % TILE
        bsum = pltpu.roll(bsum, shift, 1) if shift else bsum
        bsum = jnp.where((lane >= BMAX) & (lane < BMAX + HLOC), bsum, 0.0)
        bhi = bsum.astype(BF16).astype(F32)
        bsum = jnp.where(sub == 0, bhi, jnp.where(sub == 1, bsum - bhi, 0.0))
        out[c, 0:16] = jnp.concatenate([agg_grad[f], own_hi[f]], axis=0).astype(BF16)
        out[c, 16:32] = hidden[h]
        out[c, 32:48] = gs[h]
        out[c, 48:64] = gn[h]
        out[c, 64:80] = jnp.concatenate([own_lo[f], bsum], axis=0).astype(BF16)


def weights_kernel(r, out, bsum):
    total = r[0, 32:64].astype(F32)
    tail = r[0, 64:80].astype(F32)[FEAT:]
    for d in range(1, RT):
        total = total + r[d, 32:64].astype(F32)
        tail = tail + r[d, 64:80].astype(F32)[FEAT:]
    for s in range(RS):
        out[s] = total[s * 8 : (s + 1) * 8]
    both = tail[0:1] + tail[1:2]
    hi = both.astype(BF16).astype(F32)
    sub = iota((FEAT, TILE), 0)
    bsum[...] = jnp.where(sub == 0, hi, jnp.where(sub == 1, both - hi, 0.0))


def backward_group(g, base, none, lo, hi, tiles, dst, src, count, acc):
    n = count[0, g]

    def step(it, carry):
        done = []
        for u in range(PAIRS):
            first = (it * PAIRS + u) * 2
            second = first + 1
            da = jnp.where(first < n, dst[0, g, first], none)
            db = jnp.where(second < n, dst[0, g, second], none)
            ka = jnp.where(first < n, src[0, g, first] + base, base)
            kb = jnp.where(second < n, src[0, g, second] + base, base)
            res = dot(lo[da], tiles[0, g, first], NT) + dot(hi[db], tiles[0, g, second], NT)
            done.append((res, ka, kb))
        for res, ka, kb in done:
            acc[ka] += res[:FEAT]
            acc[kb] += res[FEAT:]
        return carry

    lax.fori_loop(0, (n + 2 * PAIRS - 1) // (2 * PAIRS), step, 0)


def load_grads(r, lo, hi):
    for d in range(RT):
        store_source(lo, hi, d, r[d, 0:16].astype(F32)[:FEAT])
    zero_source(lo, hi, RT)


def back_far_kernel(r, tiles, dst, src, count, acc, lo, hi):
    load_grads(r, lo, hi)
    acc[...] = jnp.zeros_like(acc)
    backward_group(3, 0, RT, lo, hi, tiles, dst, src, count, acc)


def pack_kernel(far, bsum, piece, out):
    mine = piece[0]
    for s in range(1, RS):
        mine = mine + piece[s]
    extra = bsum[...]
    lane = iota((FEAT, TILE), 1)
    for k in range(NB):
        x = far[k]
        for b in range(PER):
            moved = pltpu.roll(x, TILE - BMAX * b, 1) if b else x
            moved = jnp.where(lane < BMAX, moved, extra)
            out[PER * k + b] = jnp.concatenate([moved, mine], axis=0).astype(BF16)


def back_near_kernel(r, tiles, dst, src, count, own, prev, foll, hidden, lo, hi, acc):
    load_grads(r, lo, hi)
    acc[...] = jnp.zeros_like(acc)
    for g in range(3):
        backward_group(g, g * RT, RT, lo, hi, tiles, dst, src, count, acc)
    for k in range(RT):
        cols = slice(k * TILE, (k + 1) * TILE)
        own[:, cols] = (
            acc[k] + r[k, 0:16].astype(F32)[FEAT:] + r[k, 64:80].astype(F32)[:FEAT]
        )
        prev[:, cols] = acc[RT + k]
        foll[:, cols] = acc[2 * RT + k]
        hidden[:, cols] = r[k, 16:32]


def final_kernel(recv, index, own, after, before, grad, gs, gn, gb, *, scale):
    lane = iota((FEAT, TILE), 1)
    place = iota((TILE, TILE), 0)
    lefts, rights = [], []
    pieces = [jnp.zeros((8, TILE), F32) for _ in range(RS)]
    bsum = jnp.zeros((FEAT, TILE), F32)
    for k in range(NB):
        row = index[k : k + 1, :]
        tile = row >> 7
        x = jnp.zeros((FEAT, TILE), F32)
        for b in range(PER):
            p = PER * k + b
            block = recv[p].astype(F32)
            head = block[:FEAT]
            bsum = bsum + head
            pieces[p % RS] = pieces[p % RS] + block[FEAT:]
            moved = pltpu.roll(head, BMAX * b, 1) if b else head
            x = jnp.where(lane // BMAX == b, moved, x)
        lefts.append(
            jnp.concatenate([jnp.where(tile == t, x, 0.0) for t in range(RT)], axis=0).astype(BF16)
        )
        rights.append(jnp.where(place == (row & (TILE - 1)), 1.0, 0.0).astype(BF16))
    spread = dot(jnp.concatenate(lefts, axis=1), jnp.concatenate(rights, axis=1), NT)
    for t in range(RT):
        cols = slice(t * TILE, (t + 1) * TILE)
        total = own[:, cols] + after[:, cols] + before[:, cols]
        grad[:, cols] = (total + spread[t * FEAT : (t + 1) * FEAT]).astype(BF16)
    weights = jnp.concatenate(pieces, axis=0) * scale
    gs[...] = weights[:HLOC]
    gn[...] = weights[HLOC:]
    bias = pltpu.roll((bsum[0:1] + bsum[1:2]) * scale, TILE - BMAX, 1)
    gb[...] = bias[:, :HLOC]


def shifted(shard, by):
    return lax.ppermute(shard, "row", [(i, (i + by) % NROW) for i in range(NROW)])


def swap(x, axis, groups=None):
    return lax.all_to_all(x, axis, 0, 0, axis_index_groups=groups, tiled=True)


def per_device(
    features,
    tile_values,
    tile_dst,
    tile_src,
    tile_count,
    send_rows,
    send_count,
    w_self,
    w_neigh,
    bias,
    cotangent,
):
    sds = jax.ShapeDtypeStruct
    tables = (tile_dst, tile_src, tile_count)
    previous = shifted(features, 1)
    following = shifted(features, -1)
    outgoing, index = call(
        gather_kernel,
        (sds((NROW, FEAT, TILE), BF16), sds((NB, TILE), jnp.int32)),
        [VM] * 3,
        (VM, VM),
        [pltpu.VMEM((NROW, TILE), jnp.int32)],
        flops=2 * TILE * TILE * NROW * BMAX,
    )(features, send_rows, send_count)
    incoming = swap(outgoing, "row")
    near = 3 * RT + 1
    part = call(
        near_kernel,
        sds((RT, FEAT, TILE), F32),
        [VM] * 4 + [SM] * 3,
        VM,
        [pltpu.VMEM((near, 2 * FEAT, TILE), BF16)] * 2,
        flops=2 * 16 * TILE * TILE * 96,
        nbytes=4 << 20,
    )(features, previous, following, tile_values, *tables)
    buf = call(
        far_kernel,
        sds((NCOL, FWD_ROWS, TILE), BF16),
        [VM] * 8 + [SM] * 3,
        VM,
        [pltpu.VMEM((NB + 1, 2 * FEAT, TILE), BF16)] * 2 + [pltpu.VMEM((RT, FEAT, TILE), F32)],
        flops=2 * 16 * TILE * TILE * 32,
        nbytes=1 << 20,
    )(
        incoming,
        part,
        features,
        cotangent,
        w_self.T,
        w_neigh.T,
        bias.reshape(1, HLOC),
        tile_values,
        *tables,
    )
    by_node = swap(buf, "col")
    sent = call(
        dense_kernel,
        sds((NCOL, BWD_ROWS, TILE), BF16),
        [VM],
        VM,
        flops=2 * D_IN * HID * TILE * 6,
    )(by_node)
    back = swap(sent, "col")
    weights, bsum = call(
        weights_kernel,
        (sds((RS, 8, TILE), F32), sds((FEAT, TILE), F32)),
        [VM],
        (VM, VM),
    )(back)
    groups = [[i + k for k in range(RS)] for i in range(0, NROW, RS)]
    pieces = swap(weights, "row", groups)
    grads = [pltpu.VMEM((RT + 1, 2 * FEAT, TILE), BF16)] * 2
    far = call(
        back_far_kernel,
        sds((NB, FEAT, TILE), F32),
        [VM] * 2 + [SM] * 3,
        VM,
        grads,
        flops=2 * 16 * TILE * TILE * 32,
        nbytes=1 << 20,
    )(back, tile_values, *tables)
    returning = call(pack_kernel, sds((NROW, 2 * FEAT, TILE), BF16), [VM] * 3, VM)(
        far, bsum, pieces
    )
    returned = swap(returning, "row")
    own, to_previous, to_following, hidden = call(
        back_near_kernel,
        (sds((FEAT, NODES_LOC), F32),) * 3 + (sds((HLOC, NODES_LOC), BF16),),
        [VM] * 2 + [SM] * 3,
        (VM,) * 4,
        grads + [pltpu.VMEM((3 * RT, FEAT, TILE), F32)],
        flops=2 * 16 * TILE * TILE * 96,
        nbytes=3 << 20,
    )(back, tile_values, *tables)
    after = shifted(to_previous, -1)
    before = shifted(to_following, 1)
    grad_features, grad_self, grad_neigh, grad_bias = call(
        functools.partial(final_kernel, scale=1.0 / math.sqrt(NROW * NODES_LOC)),
        (
            sds((FEAT, NODES_LOC), BF16),
            sds((HLOC, D_IN), F32),
            sds((HLOC, D_IN), F32),
            sds((1, HLOC), F32),
        ),
        [VM] * 5,
        (VM,) * 4,
    )(returned, index, own, after, before)
    return (hidden, grad_features, grad_self.T, grad_neigh.T, grad_bias.reshape(HLOC))


def solution(mesh):
    placed = (
        P("col", "row"),
        P("row", None, None, None, None),
        P("row", None, None),
        P("row", None, None),
        P("row", None),
        P("row", None, None),
        P("row", None),
        P(None, "col"),
        P(None, "col"),
        P("col"),
        P("col", "row"),
    )
    return jax.shard_map(
        per_device,
        mesh=mesh,
        in_specs=placed,
        out_specs=(P("col", "row"), P("col", "row"), P(None, "col"), P(None, "col"), P("col")),
        check_vma=False,
    )
```

time: 276 us -> 103 us (0.37)
  blocking collectives: 179 us -> 25.2 us
  matrix products: 14.8 us -> 0 us
  between operations: 14.3 us -> 0.79 us
  Pallas kernels: 0 us -> 10.1 us
  other arithmetic: 9.53 us -> 0 us
  waiting for transfers between devices: 10 us -> 14.1 us
  starting transfers between devices: 35.7 us -> 38.5 us
    psum x1 -> x0, blocking collectives: 108 us -> none  [per_device(): lax.psum((grad_self, grad_neigh, grad_bias), 'row')]
    all_gather x4 -> x0, blocking collectives: 71.7 us -> none  [the longest x1 20.1 us: per_device(): full_feats = lax.all_gather(features, 'col', axis=0, tiled=True)]
    all_to_all x0 -> x2, blocking collectives: none -> 25.2 us  [swap(): return lax.all_to_all(x, axis, 0, 0, axis_index_groups=groups, tiled=True)]
    dot_general x10 -> x0, matrix products: 14.8 us -> none  [the longest x1 4.47 us: per_device(): jnp.einsum('ftd,tsd->fts', picked_back, tile_blocks, preferred_element_ty...]
    unnamed x20 -> x38, local copies, waits for them, and re-layouts: 3.54 us -> 13.7 us
    pallas_call x0 -> x9, Pallas kernels: none -> 10.1 us  [the longest x1 2.56 us: per_device(): call(back_near_kernel, (sds((FEAT, NODES_LOC), F32),) * 3 + (sds((HLOC, N...]
    all_to_all x2 -> x3, starting transfers between devices: 27 us -> 34.8 us  [swap(): return lax.all_to_all(x, axis, 0, 0, axis_index_groups=groups, tiled=True)]
    scatter-add x1 -> x0, other arithmetic: 6.43 us -> none  [per_device(): jnp.zeros((feature_count, row_count), jnp.float32).at[:, row_lists]]
  transfers between devices with their start and end apart: 7 -> 7, of which waited for: 1 -> 4; matrix products, arithmetic and copies ran while one was open for 5% -> 0% of each run, Pallas kernels for 0% -> 5%
where the time goes in v1:
time: 103 us; the launch traced here: 102 us
  starting transfers between devices  38.5 us (37%)
  blocking collectives  25.2 us (24%)
  waiting for transfers between devices  14.1 us (14%)
  local copies, waits for them, and re-layouts  13.7 us (13%)
  Pallas kernels  10.1 us (10%)
    all_to_all x3, starting transfers between devices, swap(): return lax.all_to_all(x, axis, 0, 0, axis_index_groups=groups, tiled=True)  34.8 us
    all_to_all x2, blocking collectives, swap(): return lax.all_to_all(x, axis, 0, 0, axis_index_groups=groups, tiled=True)  25.2 us
    unnamed x38, local copies, waits for them, and re-layouts  13.7 us
    all_to_all x3, waiting for transfers between devices, swap(): return lax.all_to_all(x, axis, 0, 0, axis_index_groups=groups, tiled=True)  8.56 us
    ppermute x4, waiting for transfers between devices, shifted(): lax.ppermute(shard, 'row', [(i, (i + by) % NROW) for i in range(NROW)])  5.54 us
    ppermute x4, starting transfers between devices, shifted(): lax.ppermute(shard, 'row', [(i, (i + by) % NROW) for i in range(NROW)])  3.65 us
    pallas_call x1, Pallas kernels, per_device(): call(back_near_kernel, (sds((FEAT, NODES_LOC), F32),) * 3 + (sds((HLOC, N...  2.56 us
  transfers between devices with their start and end apart: 7, of which 4 were waited for; matrix products, arithmetic and copies ran while one was open for 0% of the time, Pallas kernels for 5%

profile of v1, /device:TPU:1, one launch (start us, length us, event | category | flops | bytes accessed | tf_op | source)
XLA Modules:
  0.0 102.3 jit_solution(13441468243647275342)
XLA Ops:
  0.6 0.0 copy-start.4
  0.6 0.7 copy-done.4
  1.4 0.7 copy-done.17
  2.1 0.7 copy-done.18
  2.8 0.0 copy-start.13
  2.8 0.0 copy-start.14
  2.8 0.0 copy-start.15
  2.8 0.0 copy-start.16
  2.8 1.1 %shard_map.146 = (bf16[32,8,128]{2,1,0:T(8,128)(2,1)}, s32[8,128]{1,0:T(8,128)S(1)}) custom-call(bf16[8,2048]{1,0:T(8,128)(2,1)S(1)} %copy-done.4, s32[1,32,32]{2,1,0:T(8,128)S(1)} %copy-done.17, s32[1,32]{1,0:T(1,128)S(1)} %copy-done.18), custom_call_target="tpu_custom_call" | custom-call | flops 33554432 | tf_op jit(solution)/shard_map/pallas_call | solution.py:333
  3.9 16.8 %all-to-all-start = ((bf16[32,8,128]{2,1,0:T(8,128)(2,1)}), bf16[32,8,128]{2,1,0:T(8,128)(2,1)S(1)}, u32[]{:S(2)}, u32[]{:S(2)}) async-start(bf16[32,8,128]{2,1,0:T(8,128)(2,1)} %get-tuple-element.17), calls=%async_computation | async-start | bytes 131072 | tf_op jit(solution)/shard_map/all_to_all | solution.py:313
  20.7 0.2 collective-permute-start.1
  20.9 1.5 %collective-permute-start = (bf16[8,2048]{1,0:T(8,128)(2,1)}, bf16[8,2048]{1,0:T(8,128)(2,1)S(1)}, u32[]{:S(2)}, u32[]{:S(2)}) collective-permute-start(bf16[8,2048]{1,0:T(8,128)(2,1)} %feat.5), channel_id=1, source_target_pairs={{0,16},{16,32},{32,48},{48,64},{64,80},{80,96},{96,112},{112,128},... | collective-permute-start | bytes 98312 | tf_op jit(solution)/shard_map/ppermute | solution.py:309
  22.4 2.7 %collective-permute-done.1.foll = bf16[8,2048]{1,0:T(8,128)(2,1)S(1)} collective-permute-done((bf16[8,2048]{1,0:T(8,128)(2,1)}, bf16[8,2048]{1,0:T(8,128)(2,1)S(1)}, u32[]{:S(2)}, u32[]{:S(2)}) %collective-permute-start.1) | collective-permute-done | bytes 32800 | tf_op jit(solution)/shard_map/ppermute | solution.py:309
  25.2 0.0 collective-permute-done.prev
  25.2 2.2 %copy-done = bf16[1,4,32,128,128]{4,3,2,1,0:T(8,128)(2,1)S(1)} copy-done((bf16[1,4,32,128,128]{4,3,2,1,0:T(8,128)(2,1)S(1)}, bf16[1,4,32,128,128]{4,3,2,1,0:T(8,128)(2,1)}, u32[]{:S(2)}) %copy-start) | copy-done | bytes 4194328
  27.4 0.8 copy-done.5
  28.1 0.7 copy-done.8
  28.8 0.7 copy-done.10
  29.5 0.7 copy-done.12
  30.1 1.5 %shard_map.147.part = f32[16,8,128]{2,1,0:T(8,128)S(1)} custom-call(bf16[8,2048]{1,0:T(8,128)(2,1)S(1)} %copy-done.5, bf16[8,2048]{1,0:T(8,128)(2,1)S(1)} %collective-permute-done.prev, bf16[8,2048]{1,0:T(8,128)(2,1)S(1)} %collective-permute-done.1.foll, bf16[1,4,32,128,128]{4,3,2,1,0:T(8,128)(2,1)S(1)} %copy-done, s32[1,4,32]{2,1,0:T(4,128)S(1)} %copy-done.8, ...), custom_call_target="tpu_custom_call" | custom-call | flops 50331648 | bytes 4194304 | tf_op jit(solution)/shard_map/pallas_call | solution.py:343
  31.6 2.2 %all-to-all-done.recv = bf16[32,8,128]{2,1,0:T(8,128)(2,1)S(1)} async-done(((bf16[32,8,128]{2,1,0:T(8,128)(2,1)}), bf16[32,8,128]{2,1,0:T(8,128)(2,1)S(1)}, u32[]{:S(2)}, u32[]{:S(2)}) %all-to-all-start) | async-done | bytes 65568 | tf_op jit(solution)/shard_map/all_to_all | solution.py:313
  33.8 0.0 copy-done.6
  33.8 0.0 copy-done.7
  33.8 0.0 copy-done.9
  33.8 0.0 copy-done.11
  33.8 0.0 copy-done.13
  33.8 0.0 copy-start.1
  33.8 2.2 %copy-done.1 = bf16[1,4,32,128,128]{4,3,2,1,0:T(8,128)(2,1)S(1)} copy-done((bf16[1,4,32,128,128]{4,3,2,1,0:T(8,128)(2,1)S(1)}, bf16[1,4,32,128,128]{4,3,2,1,0:T(8,128)(2,1)}, u32[]{:S(2)}) %copy-start.1) | copy-done | bytes 4194328
  36.0 1.1 %shard_map.148 = bf16[16,80,128]{2,1,0:T(8,128)(2,1)S(1)} custom-call(bf16[32,8,128]{2,1,0:T(8,128)(2,1)S(1)} %all-to-all-done.recv, f32[16,8,128]{2,1,0:T(8,128)S(1)} %shard_map.147.part, bf16[8,2048]{1,0:T(8,128)(2,1)S(1)} %copy-done.6, bf16[16,2048]{1,0:T(8,128)(2,1)S(1)} %copy-done.7, bf16[16,128]{1,0:T(8,128)(2,1)S(1)} %bitcast.6, ...), custom_call_target="tpu_custom_call" | custom-call | flops 16777216 | bytes 1048576 | tf_op jit(solution)/shard_map/pallas_call | solution.py:352
  37.1 14.5 %all_to_all.25.r = bf16[16,80,128]{2,1,0:T(8,128)(2,1)S(1)} all-to-all(bf16[16,80,128]{2,1,0:T(8,128)(2,1)S(1)} %shard_map.148), channel_id=1, replica_groups=mesh['row'=32,'col'=16] {'col'}, dimensions={0} | all-to-all | bytes 655360 | tf_op jit(solution)/shard_map/all_to_all | solution.py:313
  51.7 0.4 shard_map.149
  52.1 10.6 %all_to_all.26.r = bf16[16,80,128]{2,1,0:T(8,128)(2,1)S(1)} all-to-all(bf16[16,80,128]{2,1,0:T(8,128)(2,1)S(1)} %shard_map.149), channel_id=1, replica_groups=mesh['row'=32,'col'=16] {'col'}, dimensions={0} | all-to-all | bytes 655360 | tf_op jit(solution)/shard_map/all_to_all | solution.py:313
  62.7 0.6 shard_map.152
  63.4 7.6 %all-to-all-start.3 = ((f32[4,8,128]{2,1,0:T(8,128)}), f32[4,8,128]{2,1,0:T(8,128)S(1)}, u32[]{:S(2)}, u32[]{:S(2)}) async-start(f32[4,8,128]{2,1,0:T(8,128)} %get-tuple-element.20), calls=%async_computation.3 | async-start | bytes 32768 | tf_op jit(solution)/shard_map/all_to_all | solution.py:313
  71.0 2.2 %copy-done.2 = bf16[1,4,32,128,128]{4,3,2,1,0:T(8,128)(2,1)S(1)} copy-done((bf16[1,4,32,128,128]{4,3,2,1,0:T(8,128)(2,1)S(1)}, bf16[1,4,32,128,128]{4,3,2,1,0:T(8,128)(2,1)}, u32[]{:S(2)}) %copy-start.2) | copy-done | bytes 4194328
  73.2 1.1 %shard_map.151.far = f32[8,8,128]{2,1,0:T(8,128)S(1)} custom-call(bf16[16,80,128]{2,1,0:T(8,128)(2,1)S(1)} %all_to_all.26.r, bf16[1,4,32,128,128]{4,3,2,1,0:T(8,128)(2,1)S(1)} %copy-done.2, s32[1,4,32]{2,1,0:T(4,128)S(1)} %copy-done.9, s32[1,4,32]{2,1,0:T(4,128)S(1)} %copy-done.11, s32[1,4]{1,0:T(1,128)S(1)} %copy-done.13), custom_call_target="tpu_custom_call" | custom-call | flops 16777216 | bytes 1048576 | tf_op jit(solution)/shard_map/pallas_call | solution.py:389
  74.3 0.0 all-to-all-done.3.piece
  74.3 0.8 shard_map.153
  75.1 10.4 %all-to-all-start.4 = ((bf16[32,16,128]{2,1,0:T(8,128)(2,1)}), bf16[32,16,128]{2,1,0:T(8,128)(2,1)S(1)}, u32[]{:S(2)}, u32[]{:S(2)}) async-start(bf16[32,16,128]{2,1,0:T(8,128)(2,1)} %shard_map.153), calls=%async_computation.4 | async-start | bytes 262144 | tf_op jit(solution)/shard_map/all_to_all | solution.py:313
  85.5 0.0 copy-start.3
  85.5 2.2 %copy-done.3 = bf16[1,4,32,128,128]{4,3,2,1,0:T(8,128)(2,1)S(1)} copy-done((bf16[1,4,32,128,128]{4,3,2,1,0:T(8,128)(2,1)S(1)}, bf16[1,4,32,128,128]{4,3,2,1,0:T(8,128)(2,1)}, u32[]{:S(2)}) %copy-start.3) | copy-done | bytes 4194328
  87.7 2.6 %shard_map.150 = (f32[8,2048]{1,0:T(8,128)S(1)}, f32[8,2048]{1,0:T(8,128)S(1)}, f32[8,2048]{1,0:T(8,128)S(1)}, bf16[16,2048]{1,0:T(8,128)(2,1)}) custom-call(bf16[16,80,128]{2,1,0:T(8,128)(2,1)S(1)} %all_to_all.26.r, bf16[1,4,32,128,128]{4,3,2,1,0:T(8,128)(2,1)S(1)} %copy-done.3, s32[1,4,32]{2,1,0:T(4,128)S(1)} %copy-done.9, s32[1,4,32]{2,1,0:T(4,128)S(1)} %copy-done.11, ...), custom_call_target="tpu_custom_call" | custom-call | flops 50331648 | bytes 3145728 | tf_op jit(solution)/shard_map/pallas_call | solution.py:402
  90.3 0.8 collective-permute-start.2
  91.0 1.1 %collective-permute-start.3 = (f32[8,2048]{1,0:T(8,128)S(1)}, f32[8,2048]{1,0:T(8,128)S(1)}, u32[]{:S(2)}, u32[]{:S(2)}) collective-permute-start(f32[8,2048]{1,0:T(8,128)S(1)} %get-tuple-element.24), channel_id=1, source_target_pairs={{0,16},{16,32},{32,48},{48,64},{64,80},{80,96},{96,112},{112,128},... | collective-permute-start | bytes 196616 | tf_op jit(solution)/shard_map/ppermute | solution.py:309
  92.2 2.8 %collective-permute-done.2.after = f32[8,2048]{1,0:T(8,128)S(1)} collective-permute-done((f32[8,2048]{1,0:T(8,128)S(1)}, f32[8,2048]{1,0:T(8,128)S(1)}, u32[]{:S(2)}, u32[]{:S(2)}) %collective-permute-start.2) | collective-permute-done | bytes 65568 | tf_op jit(solution)/shard_map/ppermute | solution.py:309
  94.9 0.0 collective-permute-done.3.before
  95.0 6.4 %all-to-all-done.4.recv = bf16[32,16,128]{2,1,0:T(8,128)(2,1)S(1)} async-done(((bf16[32,16,128]{2,1,0:T(8,128)(2,1)}), bf16[32,16,128]{2,1,0:T(8,128)(2,1)S(1)}, u32[]{:S(2)}, u32[]{:S(2)}) %all-to-all-start.4) | async-done | bytes 131104 | tf_op jit(solution)/shard_map/all_to_all | solution.py:313
  101.4 0.9 shard_map.154
  (15 shorter events, 0.0 us)
Async XLA Ops:
  0.6 0.8 copy-start.4
  1.4 0.7 copy-start.17
  2.1 0.7 copy-start.18
  2.8 31.0 %copy-start.6 = (bf16[8,2048]{1,0:T(8,128)(2,1)S(1)}, bf16[8,2048]{1,0:T(8,128)(2,1)}, u32[]{:S(2)}) copy-start(bf16[8,2048]{1,0:T(8,128)(2,1)} %feat.5) | copy-start | bytes 98308
  2.8 31.0 %copy-start.7 = (bf16[16,2048]{1,0:T(8,128)(2,1)S(1)}, bf16[16,2048]{1,0:T(8,128)(2,1)}, u32[]{:S(2)}) copy-start(bf16[16,2048]{1,0:T(8,128)(2,1)} %cot.1) | copy-start | bytes 196612
  2.8 31.0 %copy-start.9 = (s32[1,4,32]{2,1,0:T(4,128)S(1)}, s32[1,4,32]{2,1,0:T(4,128)}, u32[]{:S(2)}) copy-start(s32[1,4,32]{2,1,0:T(4,128)} %dst.7) | copy-start | bytes 1540
  2.8 31.0 %copy-start.11 = (s32[1,4,32]{2,1,0:T(4,128)S(1)}, s32[1,4,32]{2,1,0:T(4,128)}, u32[]{:S(2)}) copy-start(s32[1,4,32]{2,1,0:T(4,128)} %src.7) | copy-start | bytes 1540
  2.8 31.0 %copy-start.13 = (s32[1,4]{1,0:T(1,128)S(1)}, s32[1,4]{1,0:T(1,128)}, u32[]{:S(2)}) copy-start(s32[1,4]{1,0:T(1,128)} %count.7) | copy-start | bytes 52
  2.8 31.0 %copy-start.14 = (bf16[128,16]{0,1:T(8,128)(2,1)S(1)}, bf16[128,16]{0,1:T(8,128)(2,1)}, u32[]{:S(2)}) copy-start(bf16[128,16]{0,1:T(8,128)(2,1)} %param.18) | copy-start | bytes 12292
  2.8 31.0 %copy-start.15 = (bf16[128,16]{0,1:T(8,128)(2,1)S(1)}, bf16[128,16]{0,1:T(8,128)(2,1)}, u32[]{:S(2)}) copy-start(bf16[128,16]{0,1:T(8,128)(2,1)} %param.19) | copy-start | bytes 12292
  2.8 31.0 %copy-start.16 = (f32[16]{0:T(128)S(1)}, f32[16]{0:T(128)}, u32[]{:S(2)}) copy-start(f32[16]{0:T(128)} %param.20) | copy-start | bytes 196
  3.9 29.8 %all-to-all-start = ((bf16[32,8,128]{2,1,0:T(8,128)(2,1)}), bf16[32,8,128]{2,1,0:T(8,128)(2,1)S(1)}, u32[]{:S(2)}, u32[]{:S(2)}) async-start(bf16[32,8,128]{2,1,0:T(8,128)(2,1)} %get-tuple-element.17), calls=%async_computation | async-start | bytes 131072 | tf_op jit(solution)/shard_map/all_to_all | solution.py:313
  20.7 4.5 %collective-permute-start.1 = (bf16[8,2048]{1,0:T(8,128)(2,1)}, bf16[8,2048]{1,0:T(8,128)(2,1)S(1)}, u32[]{:S(2)}, u32[]{:S(2)}) collective-permute-start(bf16[8,2048]{1,0:T(8,128)(2,1)} %feat.5), channel_id=1, source_target_pairs={{0,496},{16,0},{32,16},{48,32},{64,48},{80,64},{96,80},{112,96},{1... | collective-permute-start | bytes 98312 | tf_op jit(solution)/shard_map/ppermute | solution.py:309
  20.9 4.2 %collective-permute-start = (bf16[8,2048]{1,0:T(8,128)(2,1)}, bf16[8,2048]{1,0:T(8,128)(2,1)S(1)}, u32[]{:S(2)}, u32[]{:S(2)}) collective-permute-start(bf16[8,2048]{1,0:T(8,128)(2,1)} %feat.5), channel_id=1, source_target_pairs={{0,16},{16,32},{32,48},{48,64},{64,80},{80,96},{96,112},{112,128},... | collective-permute-start | bytes 98312 | tf_op jit(solution)/shard_map/ppermute | solution.py:309
  25.2 2.2 %copy-start = (bf16[1,4,32,128,128]{4,3,2,1,0:T(8,128)(2,1)S(1)}, bf16[1,4,32,128,128]{4,3,2,1,0:T(8,128)(2,1)}, u32[]{:S(2)}) copy-start(bf16[1,4,32,128,128]{4,3,2,1,0:T(8,128)(2,1)} %tiles.7) | copy-start | bytes 12582916
  27.4 0.8 copy-start.5
  28.1 0.7 copy-start.8
  28.8 0.7 copy-start.10
  29.5 0.7 copy-start.12
  33.8 2.2 %copy-start.1 = (bf16[1,4,32,128,128]{4,3,2,1,0:T(8,128)(2,1)S(1)}, bf16[1,4,32,128,128]{4,3,2,1,0:T(8,128)(2,1)}, u32[]{:S(2)}) copy-start(bf16[1,4,32,128,128]{4,3,2,1,0:T(8,128)(2,1)} %tiles.7) | copy-start | bytes 12582916
  63.4 10.9 %all-to-all-start.3 = ((f32[4,8,128]{2,1,0:T(8,128)}), f32[4,8,128]{2,1,0:T(8,128)S(1)}, u32[]{:S(2)}, u32[]{:S(2)}) async-start(f32[4,8,128]{2,1,0:T(8,128)} %get-tuple-element.20), calls=%async_computation.3 | async-start | bytes 32768 | tf_op jit(solution)/shard_map/all_to_all | solution.py:313
  71.0 2.2 %copy-start.2 = (bf16[1,4,32,128,128]{4,3,2,1,0:T(8,128)(2,1)S(1)}, bf16[1,4,32,128,128]{4,3,2,1,0:T(8,128)(2,1)}, u32[]{:S(2)}) copy-start(bf16[1,4,32,128,128]{4,3,2,1,0:T(8,128)(2,1)} %tiles.7) | copy-start | bytes 12582916
  75.1 26.3 %all-to-all-start.4 = ((bf16[32,16,128]{2,1,0:T(8,128)(2,1)}), bf16[32,16,128]{2,1,0:T(8,128)(2,1)S(1)}, u32[]{:S(2)}, u32[]{:S(2)}) async-start(bf16[32,16,128]{2,1,0:T(8,128)(2,1)} %shard_map.153), calls=%async_computation.4 | async-start | bytes 262144 | tf_op jit(solution)/shard_map/all_to_all | solution.py:313
  85.5 2.2 %copy-start.3 = (bf16[1,4,32,128,128]{4,3,2,1,0:T(8,128)(2,1)S(1)}, bf16[1,4,32,128,128]{4,3,2,1,0:T(8,128)(2,1)}, u32[]{:S(2)}) copy-start(bf16[1,4,32,128,128]{4,3,2,1,0:T(8,128)(2,1)} %tiles.7) | copy-start | bytes 12582916
  90.3 4.7 %collective-permute-start.2 = (f32[8,2048]{1,0:T(8,128)S(1)}, f32[8,2048]{1,0:T(8,128)S(1)}, u32[]{:S(2)}, u32[]{:S(2)}) collective-permute-start(f32[8,2048]{1,0:T(8,128)S(1)} %get-tuple-element.23), channel_id=1, source_target_pairs={{0,496},{16,0},{32,16},{48,32},{64,48},{80,64},{96,80},{112,96},{1... | collective-permute-start | bytes 196616 | tf_op jit(solution)/shard_map/ppermute | solution.py:309
  91.0 3.9 %collective-permute-start.3 = (f32[8,2048]{1,0:T(8,128)S(1)}, f32[8,2048]{1,0:T(8,128)S(1)}, u32[]{:S(2)}, u32[]{:S(2)}) collective-permute-start(f32[8,2048]{1,0:T(8,128)S(1)} %get-tuple-element.24), channel_id=1, source_target_pairs={{0,16},{16,32},{32,48},{48,64},{64,80},{80,96},{96,112},{112,128},... | collective-permute-start | bytes 196616 | tf_op jit(solution)/shard_map/ppermute | solution.py:309

commit v2 on v1

--- a/solution.py
+++ b/solution.py
@@ -20,7 +20,6 @@
 NODES_LOC = RT * TILE
 NB = NROW * BMAX // TILE
 PER = TILE // BMAX
-PAIRS = 4
 RS = 4
 FWD_ROWS = 80
 BWD_ROWS = 80
@@ -29,7 +28,14 @@
 TN = (((0,), (0,)), ((), ()))
 
 VM = pl.BlockSpec(memory_space=pltpu.VMEM)
-SM = pl.BlockSpec(memory_space=pltpu.SMEM)
+HB = pl.BlockSpec(memory_space=pltpu.HBM)
+CHUNK = 8
+NCHUNK = 4
+TABLES = [
+    pltpu.SMEM((1, 4, 32), jnp.int32),
+    pltpu.SMEM((1, 4, 32), jnp.int32),
+    pltpu.SMEM((1, 4), jnp.int32),
+]
 
 
 def dot(a, b, dims=(((1,), (0,)), ((), ()))):
@@ -51,12 +57,47 @@
         in_specs=in_specs,
         out_specs=out_specs,
         scratch_shapes=list(scratch),
-        compiler_params=pltpu.CompilerParams(vmem_limit_bytes=32 * 1024 * 1024),
+        compiler_params=pltpu.CompilerParams(vmem_limit_bytes=16 * 1024 * 1024),
         cost_estimate=pl.CostEstimate(flops=flops, bytes_accessed=nbytes, transcendentals=0),
     )
 
 
-def gather_kernel(feat, rows, counts, out, index, scr):
+def start_all(sources, targets, sems):
+    copies = [
+        pltpu.make_async_copy(a, b, sems.at[i]) for i, (a, b) in enumerate(zip(sources, targets))
+    ]
+    for c in copies:
+        c.start()
+    return copies
+
+
+def wait_all(copies):
+    for c in copies:
+        c.wait()
+
+
+def chunk_copy(tiles, held, g, c, slot, sems):
+    return pltpu.make_async_copy(
+        tiles.at[0, g, pl.ds(c * CHUNK, CHUNK)],
+        held.at[slot, pl.ds(c * CHUNK, CHUNK)],
+        sems.at[slot, c],
+    )
+
+
+def start_chunks(tiles, held, groups, count, sems, first, last):
+    for slot, g in enumerate(groups):
+        for c in range(first, last):
+            if c == 0:
+                chunk_copy(tiles, held, g, c, slot, sems).start()
+            else:
+
+                @pl.when(count[0, g] > c * CHUNK)
+                def _():
+                    chunk_copy(tiles, held, g, c, slot, sems).start()
+
+
+def gather_kernel(feat_hbm, rows_hbm, counts_hbm, out, index, feat, rows, counts, scr, sems):
+    wait_all(start_all((rows_hbm, counts_hbm, feat_hbm), (rows, counts, feat), sems))
     cnt = jnp.broadcast_to(counts[...], (NROW, NROW))
     cnt = jnp.where(iota((NROW, NROW), 0) == iota((NROW, NROW), 1), cnt, 0)
     cnt = jnp.sum(cnt, axis=1, keepdims=True)
@@ -94,41 +135,95 @@
     hi[k] = jnp.zeros((2 * FEAT, TILE), BF16)
 
 
-def forward_group(g, base, none, lo, hi, tiles, dst, src, count, acc):
-    n = count[0, g]
-
-    def step(it, carry):
-        done = []
-        for u in range(PAIRS):
-            first = (it * PAIRS + u) * 2
-            second = first + 1
-            ka = jnp.where(first < n, src[0, g, first] + base, none)
-            kb = jnp.where(second < n, src[0, g, second] + base, none)
-            da = jnp.where(first < n, dst[0, g, first], 0)
-            db = jnp.where(second < n, dst[0, g, second], 0)
-            left = jnp.concatenate([lo[ka], hi[kb]], axis=1)
-            right = tiles[0, g, pl.ds(first, 2)].reshape(2 * TILE, TILE)
-            done.append((dot(left, right), da, db))
-        for r, da, db in done:
-            acc[da] += r[:FEAT]
-            acc[db] += r[FEAT:]
-        return carry
-
-    lax.fori_loop(0, (n + 2 * PAIRS - 1) // (2 * PAIRS), step, 0)
-
-
-def near_kernel(feat, prev, foll, tiles, dst, src, count, part, lo, hi):
+def forward_step(it, g, base, none, lo, hi, tile_at, dst, src, n, acc):
+    done = []
+    for u in range(CHUNK // 2):
+        first = it * CHUNK + 2 * u
+        second = first + 1
+        ka = jnp.where(first < n, src[0, g, first] + base, none)
+        kb = jnp.where(second < n, src[0, g, second] + base, none)
+        da = jnp.where(first < n, dst[0, g, first], 0)
+        db = jnp.where(second < n, dst[0, g, second], 0)
+        left = jnp.concatenate([lo[ka], hi[kb]], axis=1)
+        right = tile_at(first).reshape(2 * TILE, TILE)
+        done.append((dot(left, right), da, db))
+    for r, da, db in done:
+        acc[da] += r[:FEAT]
+        acc[db] += r[FEAT:]
+
+
+def steps(n):
+    return (n + CHUNK - 1) // CHUNK
+
+
+def own_kernel(
+    feat_hbm, tiles, dst_hbm, src_hbm, count_hbm, part, kept, feat, dst, src, count, held, lo, hi,
+    sems, chunk_sems, kept_sems,
+):
+    copies = start_all(
+        (count_hbm, dst_hbm, src_hbm, feat_hbm), (count, dst, src, feat), sems
+    )
+    start_chunks(tiles, held, [0], count, chunk_sems, 0, 1)
+    start_chunks(tiles, kept, [3], count, kept_sems, 0, 1)
+    copies[0].wait()
+    start_chunks(tiles, held, [0], count, chunk_sems, 1, NCHUNK)
+    start_chunks(tiles, kept, [3], count, kept_sems, 1, NCHUNK)
+    wait_all(copies[1:])
     for k in range(RT):
         store_source(lo, hi, k, tile_of(feat, k).astype(F32))
-        store_source(lo, hi, RT + k, tile_of(prev, k).astype(F32))
-        store_source(lo, hi, 2 * RT + k, tile_of(foll, k).astype(F32))
-    zero_source(lo, hi, 3 * RT)
+    zero_source(lo, hi, RT)
     part[...] = jnp.zeros_like(part)
-    for g in range(3):
-        forward_group(g, g * RT, 3 * RT, lo, hi, tiles, dst, src, count, part)
-
-
-def far_kernel(recv, part, feat, cot, wst, wnt, bias, tiles, dst, src, count, buf, lo, hi, acc):
+    n = count[0, 0]
+
+    def step(it, carry):
+        chunk_copy(tiles, held, 0, it, 0, chunk_sems).wait()
+        forward_step(
+            it, 0, 0, RT, lo, hi, lambda i: held[0, pl.ds(i, 2)], dst, src, n, part
+        )
+        return carry
+
+    lax.fori_loop(0, steps(n), step, 0)
+
+    def kept_wait(it, carry):
+        chunk_copy(tiles, kept, 3, it, 0, kept_sems).wait()
+        return carry
+
+    lax.fori_loop(0, steps(count[0, 3]), kept_wait, 0)
+
+
+def near_kernel(
+    prev, foll, before, tiles, dst_hbm, src_hbm, count_hbm, part, dst, src, count, held, lo, hi,
+    sems, chunk_sems,
+):
+    copies = start_all((count_hbm, dst_hbm, src_hbm), (count, dst, src), sems)
+    start_chunks(tiles, held, [1, 2], count, chunk_sems, 0, 1)
+    for k in range(RT):
+        store_source(lo, hi, k, tile_of(prev, k).astype(F32))
+        store_source(lo, hi, RT + k, tile_of(foll, k).astype(F32))
+    zero_source(lo, hi, 2 * RT)
+    part[...] = before[...]
+    copies[0].wait()
+    start_chunks(tiles, held, [1, 2], count, chunk_sems, 1, NCHUNK)
+    wait_all(copies[1:])
+    for slot, g in enumerate([1, 2]):
+        n = count[0, g]
+
+        def step(it, carry):
+            chunk_copy(tiles, held, g, it, slot, chunk_sems).wait()
+            forward_step(
+                it, g, slot * RT, 2 * RT, lo, hi,
+                lambda i: held[slot, pl.ds(i, 2)], dst, src, n, part,
+            )
+            return carry
+
+        lax.fori_loop(0, steps(n), step, 0)
+
+
+def far_kernel(
+    recv, part, feat, cot, wst, wnt, bias, kept, dst_hbm, src_hbm, count_hbm, buf, dst, src, count,
+    lo, hi, acc, sems,
+):
+    copies = start_all((count_hbm, dst_hbm, src_hbm), (count, dst, src), sems)
     lane = iota((FEAT, TILE), 1)
     for k in range(NB):
         x = recv[PER * k].astype(F32)
@@ -138,7 +233,16 @@
         store_source(lo, hi, k, x)
     zero_source(lo, hi, NB)
     acc[...] = part[...]
-    forward_group(3, 0, NB, lo, hi, tiles, dst, src, count, acc)
+    wait_all(copies)
+    n = count[0, 3]
+
+    def step(it, carry):
+        forward_step(
+            it, 3, 0, NB, lo, hi, lambda i: kept[0, pl.ds(i, 2)], dst, src, n, acc
+        )
+        return carry
+
+    lax.fori_loop(0, steps(n), step, 0)
     b = jnp.broadcast_to(bias[...], (HLOC, HLOC))
     b = jnp.where(iota((HLOC, HLOC), 0) == iota((HLOC, HLOC), 1), b, 0.0)
     b = jnp.sum(b, axis=1, keepdims=True)
@@ -208,26 +312,20 @@
     bsum[...] = jnp.where(sub == 0, hi, jnp.where(sub == 1, both - hi, 0.0))
 
 
-def backward_group(g, base, none, lo, hi, tiles, dst, src, count, acc):
-    n = count[0, g]
-
-    def step(it, carry):
-        done = []
-        for u in range(PAIRS):
-            first = (it * PAIRS + u) * 2
-            second = first + 1
-            da = jnp.where(first < n, dst[0, g, first], none)
-            db = jnp.where(second < n, dst[0, g, second], none)
-            ka = jnp.where(first < n, src[0, g, first] + base, base)
-            kb = jnp.where(second < n, src[0, g, second] + base, base)
-            res = dot(lo[da], tiles[0, g, first], NT) + dot(hi[db], tiles[0, g, second], NT)
-            done.append((res, ka, kb))
-        for res, ka, kb in done:
-            acc[ka] += res[:FEAT]
-            acc[kb] += res[FEAT:]
-        return carry
-
-    lax.fori_loop(0, (n + 2 * PAIRS - 1) // (2 * PAIRS), step, 0)
+def backward_step(it, g, base, none, lo, hi, tile_at, dst, src, n, acc):
+    done = []
+    for u in range(CHUNK // 2):
+        first = it * CHUNK + 2 * u
+        second = first + 1
+        da = jnp.where(first < n, dst[0, g, first], none)
+        db = jnp.where(second < n, dst[0, g, second], none)
+        ka = jnp.where(first < n, src[0, g, first] + base, base)
+        kb = jnp.where(second < n, src[0, g, second] + base, base)
+        res = dot(lo[da], tile_at(first), NT) + dot(hi[db], tile_at(second), NT)
+        done.append((res, ka, kb))
+    for res, ka, kb in done:
+        acc[ka] += res[:FEAT]
+        acc[kb] += res[FEAT:]
 
 
 def load_grads(r, lo, hi):
@@ -236,10 +334,18 @@
     zero_source(lo, hi, RT)
 
 
-def back_far_kernel(r, tiles, dst, src, count, acc, lo, hi):
+def back_far_kernel(r, kept, dst_hbm, src_hbm, count_hbm, acc, dst, src, count, lo, hi, sems):
+    copies = start_all((count_hbm, dst_hbm, src_hbm), (count, dst, src), sems)
     load_grads(r, lo, hi)
     acc[...] = jnp.zeros_like(acc)
-    backward_group(3, 0, RT, lo, hi, tiles, dst, src, count, acc)
+    wait_all(copies)
+    n = count[0, 3]
+
+    def step(it, carry):
+        backward_step(it, 3, 0, RT, lo, hi, lambda i: kept[0, i], dst, src, n, acc)
+        return carry
+
+    lax.fori_loop(0, steps(n), step, 0)
 
 
 def pack_kernel(far, bsum, piece, out):
@@ -256,18 +362,45 @@
             out[PER * k + b] = jnp.concatenate([moved, mine], axis=0).astype(BF16)
 
 
-def back_near_kernel(r, tiles, dst, src, count, own, prev, foll, hidden, lo, hi, acc):
+def back_groups(
+    groups, r, tiles, dst_hbm, src_hbm, count_hbm, dst, src, count, held, lo, hi, acc, sems, chunk_sems
+):
+    copies = start_all((count_hbm, dst_hbm, src_hbm), (count, dst, src), sems)
+    start_chunks(tiles, held, groups, count, chunk_sems, 0, 1)
     load_grads(r, lo, hi)
     acc[...] = jnp.zeros_like(acc)
-    for g in range(3):
-        backward_group(g, g * RT, RT, lo, hi, tiles, dst, src, count, acc)
+    copies[0].wait()
+    start_chunks(tiles, held, groups, count, chunk_sems, 1, NCHUNK)
+    wait_all(copies[1:])
+    for slot, g in enumerate(groups):
+        n = count[0, g]
+
+        def step(it, carry):
+            chunk_copy(tiles, held, g, it, slot, chunk_sems).wait()
+            backward_step(
+                it, g, slot * RT, RT, lo, hi, lambda i: held[slot, i], dst, src, n, acc
+            )
+            return carry
+
+        lax.fori_loop(0, steps(n), step, 0)
+
+
+def back_near_kernel(r, tiles, dst_hbm, src_hbm, count_hbm, prev, foll, *scratch):
+    back_groups([1, 2], r, tiles, dst_hbm, src_hbm, count_hbm, *scratch)
+    acc = scratch[6]
     for k in range(RT):
         cols = slice(k * TILE, (k + 1) * TILE)
-        own[:, cols] = (
-            acc[k] + r[k, 0:16].astype(F32)[FEAT:] + r[k, 64:80].astype(F32)[:FEAT]
-        )
-        prev[:, cols] = acc[RT + k]
-        foll[:, cols] = acc[2 * RT + k]
+        prev[:, cols] = acc[k]
+        foll[:, cols] = acc[RT + k]
+
+
+def back_own_kernel(r, tiles, dst_hbm, src_hbm, count_hbm, own, hidden, *scratch):
+    back_groups([0], r, tiles, dst_hbm, src_hbm, count_hbm, *scratch)
+    acc = scratch[6]
+    for k in range(RT):
+        cols = slice(k * TILE, (k + 1) * TILE)
+        tail = r[k, 64:80].astype(F32)
+        own[:, cols] = acc[k] + r[k, 0:16].astype(F32)[FEAT:] + tail[:FEAT]
         hidden[:, cols] = r[k, 16:32]
 
 
@@ -305,6 +438,25 @@
     gb[...] = bias[:, :HLOC]
 
 
+def held(groups):
+    return pltpu.VMEM((groups, 32, TILE, TILE), BF16)
+
+
+def sources(tiles):
+    return [pltpu.VMEM((tiles + 1, 2 * FEAT, TILE), BF16)] * 2
+
+
+def back_scratch(groups):
+    return [
+        *TABLES,
+        held(groups),
+        *sources(RT),
+        pltpu.VMEM((groups * RT, FEAT, TILE), F32),
+        pltpu.SemaphoreType.DMA((3,)),
+        pltpu.SemaphoreType.DMA((groups, NCHUNK)),
+    ]
+
+
 def shifted(shard, by):
     return lax.ppermute(shard, "row", [(i, (i + by) % NROW) for i in range(NROW)])
 
@@ -327,34 +479,69 @@
     cotangent,
 ):
     sds = jax.ShapeDtypeStruct
-    tables = (tile_dst, tile_src, tile_count)
+    in_hbm = lambda x: pltpu.with_memory_space_constraint(x, pltpu.HBM)
+    tables = tuple(in_hbm(x) for x in (tile_dst, tile_src, tile_count))
+    tiles = in_hbm(tile_values)
     previous = shifted(features, 1)
     following = shifted(features, -1)
     outgoing, index = call(
         gather_kernel,
         (sds((NROW, FEAT, TILE), BF16), sds((NB, TILE), jnp.int32)),
-        [VM] * 3,
+        [HB] * 3,
         (VM, VM),
-        [pltpu.VMEM((NROW, TILE), jnp.int32)],
+        [
+            pltpu.VMEM((FEAT, NODES_LOC), BF16),
+            pltpu.VMEM((1, NROW, BMAX), jnp.int32),
+            pltpu.VMEM((1, NROW), jnp.int32),
+            pltpu.VMEM((NROW, TILE), jnp.int32),
+            pltpu.SemaphoreType.DMA((3,)),
+        ],
         flops=2 * TILE * TILE * NROW * BMAX,
-    )(features, send_rows, send_count)
+    )(in_hbm(features), in_hbm(send_rows), in_hbm(send_count))
     incoming = swap(outgoing, "row")
-    near = 3 * RT + 1
+    part, kept = call(
+        own_kernel,
+        (sds((RT, FEAT, TILE), F32), sds((1, 32, TILE, TILE), BF16)),
+        [HB] * 5,
+        (VM, VM),
+        [
+            pltpu.VMEM((FEAT, NODES_LOC), BF16),
+            *TABLES,
+            held(1),
+            *sources(RT),
+            pltpu.SemaphoreType.DMA((4,)),
+            pltpu.SemaphoreType.DMA((1, NCHUNK)),
+            pltpu.SemaphoreType.DMA((1, NCHUNK)),
+        ],
+        flops=2 * 16 * TILE * TILE * 32,
+        nbytes=2 << 20,
+    )(in_hbm(features), tiles, *tables)
     part = call(
         near_kernel,
         sds((RT, FEAT, TILE), F32),
-        [VM] * 4 + [SM] * 3,
+        [VM] * 3 + [HB] * 4,
         VM,
-        [pltpu.VMEM((near, 2 * FEAT, TILE), BF16)] * 2,
-        flops=2 * 16 * TILE * TILE * 96,
-        nbytes=4 << 20,
-    )(features, previous, following, tile_values, *tables)
+        [
+            *TABLES,
+            held(2),
+            *sources(2 * RT),
+            pltpu.SemaphoreType.DMA((3,)),
+            pltpu.SemaphoreType.DMA((2, NCHUNK)),
+        ],
+        flops=2 * 16 * TILE * TILE * 64,
+        nbytes=2 << 20,
+    )(previous, following, part, tiles, *tables)
     buf = call(
         far_kernel,
         sds((NCOL, FWD_ROWS, TILE), BF16),
-        [VM] * 8 + [SM] * 3,
+        [VM] * 8 + [HB] * 3,
         VM,
-        [pltpu.VMEM((NB + 1, 2 * FEAT, TILE), BF16)] * 2 + [pltpu.VMEM((RT, FEAT, TILE), F32)],
+        [
+            *TABLES,
+            *sources(NB),
+            pltpu.VMEM((RT, FEAT, TILE), F32),
+            pltpu.SemaphoreType.DMA((3,)),
+        ],
         flops=2 * 16 * TILE * TILE * 32,
         nbytes=1 << 20,
     )(
@@ -365,7 +552,7 @@
         w_self.T,
         w_neigh.T,
         bias.reshape(1, HLOC),
-        tile_values,
+        kept,
         *tables,
     )
     by_node = swap(buf, "col")
@@ -385,31 +572,39 @@
     )(back)
     groups = [[i + k for k in range(RS)] for i in range(0, NROW, RS)]
     pieces = swap(weights, "row", groups)
-    grads = [pltpu.VMEM((RT + 1, 2 * FEAT, TILE), BF16)] * 2
     far = call(
         back_far_kernel,
         sds((NB, FEAT, TILE), F32),
-        [VM] * 2 + [SM] * 3,
+        [VM] * 2 + [HB] * 3,
         VM,
-        grads,
+        [*TABLES, *sources(RT), pltpu.SemaphoreType.DMA((3,))],
         flops=2 * 16 * TILE * TILE * 32,
         nbytes=1 << 20,
-    )(back, tile_values, *tables)
+    )(back, kept, *tables)
     returning = call(pack_kernel, sds((NROW, 2 * FEAT, TILE), BF16), [VM] * 3, VM)(
         far, bsum, pieces
     )
     returned = swap(returning, "row")
-    own, to_previous, to_following, hidden = call(
+    to_previous, to_following = call(
         back_near_kernel,
-        (sds((FEAT, NODES_LOC), F32),) * 3 + (sds((HLOC, NODES_LOC), BF16),),
-        [VM] * 2 + [SM] * 3,
-        (VM,) * 4,
-        grads + [pltpu.VMEM((3 * RT, FEAT, TILE), F32)],
-        flops=2 * 16 * TILE * TILE * 96,
-        nbytes=3 << 20,
-    )(back, tile_values, *tables)
+        (sds((FEAT, NODES_LOC), F32),) * 2,
+        [VM] + [HB] * 4,
+        (VM, VM),
+        back_scratch(2),
+        flops=2 * 16 * TILE * TILE * 64,
+        nbytes=2 << 20,
+    )(back, tiles, *tables)
     after = shifted(to_previous, -1)
     before = shifted(to_following, 1)
+    own, hidden = call(
+        back_own_kernel,
+        (sds((FEAT, NODES_LOC), F32), sds((HLOC, NODES_LOC), BF16)),
+        [VM] + [HB] * 4,
+        (VM, VM),
+        back_scratch(1),
+        flops=2 * 16 * TILE * TILE * 32,
+        nbytes=1 << 20,
+    )(back, tiles, *tables)
     grad_features, grad_self, grad_neigh, grad_bias = call(
         functools.partial(final_kernel, scale=1.0 / math.sqrt(NROW * NODES_LOC)),
         (

time: 103 us -> 94.8 us (0.920)
  local copies, waits for them, and re-layouts: 13.7 us -> 0.03 us
  Pallas kernels: 10.1 us -> 15.6 us
  starting transfers between devices: 38.5 us -> 34 us
  waiting for transfers between devices: 14.1 us -> 18.4 us
    unnamed x38 -> x10, local copies, waits for them, and re-layouts: 13.7 us -> 0.03 us
    all_to_all x3, waiting for transfers between devices: 8.56 us -> 17 us  [swap(): return lax.all_to_all(x, axis, 0, 0, axis_index_groups=groups, tiled=True)]
    pallas_call x4 -> x6, Pallas kernels: 6.23 us -> 11 us  [the longest x1 2.6 us: per_device(): call(back_own_kernel, (sds((FEAT, NODES_LOC), F32), sds((HLOC, NODES_LOC)...]
    all_to_all x3, starting transfers between devices: 34.8 us -> 30.3 us  [swap(): return lax.all_to_all(x, axis, 0, 0, axis_index_groups=groups, tiled=True)]
    ppermute x4, waiting for transfers between devices: 5.54 us -> 1.44 us  [shifted(): lax.ppermute(shard, 'row', [(i, (i + by) % NROW) for i in range(NROW)])]
  transfers between devices with their start and end apart: 7 -> 7, of which waited for: 4 -> 5; matrix products, arithmetic and copies ran while one was open for 0% -> 0% of each run, Pallas kernels for 5% -> 10%
where the time goes in v2:
time: 94.8 us; the launch traced here: 94.2 us
  starting transfers between devices  34 us (36%)
  blocking collectives  25.3 us (27%)
  waiting for transfers between devices  18.4 us (19%)
  Pallas kernels  15.6 us (16%)
    all_to_all x3, starting transfers between devices, swap(): return lax.all_to_all(x, axis, 0, 0, axis_index_groups=groups, tiled=True)  30.3 us
    all_to_all x2, blocking collectives, swap(): return lax.all_to_all(x, axis, 0, 0, axis_index_groups=groups, tiled=True)  25.3 us
    all_to_all x3, waiting for transfers between devices, swap(): return lax.all_to_all(x, axis, 0, 0, axis_index_groups=groups, tiled=True)  17 us
    ppermute x4, starting transfers between devices, shifted(): lax.ppermute(shard, 'row', [(i, (i + by) % NROW) for i in range(NROW)])  3.68 us
    pallas_call x1, Pallas kernels, per_device(): call(back_own_kernel, (sds((FEAT, NODES_LOC), F32), sds((HLOC, NODES_LOC)...  2.6 us
    pallas_call x1, Pallas kernels, per_device(): call(back_near_kernel, (sds((FEAT, NODES_LOC), F32),) * 2, [VM] + [HB] *...  2.03 us
    pallas_call x1, Pallas kernels, per_device(): call(own_kernel, (sds((RT, FEAT, TILE), F32), sds((1, 32, TILE, TILE), BF...  1.94 us
    pallas_call x1, Pallas kernels, per_device(): call(near_kernel, sds((RT, FEAT, TILE), F32), [VM] * 3 + [HB] * 4, VM, [*...  1.92 us
  transfers between devices with their start and end apart: 7, of which 5 were waited for; matrix products, arithmetic and copies ran while one was open for 0% of the time, Pallas kernels for 10%

profile of v2, /device:TPU:1, one launch (start us, length us, event | category | flops | bytes accessed | tf_op | source)
XLA Modules:
  0.0 94.2 jit_solution(3519039277820900538)
XLA Ops:
  0.6 1.9 %shard_map.146 = (bf16[32,8,128]{2,1,0:T(8,128)(2,1)}, s32[8,128]{1,0:T(8,128)S(1)}) custom-call(bf16[8,2048]{1,0:T(8,128)(2,1)} %feat.1, s32[1,32,32]{2,1,0:T(8,128)} %rows_hbm.1, s32[1,32]{1,0:T(1,128)} %counts_hbm.1), custom_call_target="tpu_custom_call" | custom-call | flops 33554432 | tf_op jit(solution)/shard_map/pallas_call | solution.py:487
  2.6 16.8 %all-to-all-start = ((bf16[32,8,128]{2,1,0:T(8,128)(2,1)}), bf16[32,8,128]{2,1,0:T(8,128)(2,1)S(1)}, u32[]{:S(2)}, u32[]{:S(2)}) async-start(bf16[32,8,128]{2,1,0:T(8,128)(2,1)} %get-tuple-element.19), calls=%async_computation | async-start | bytes 131072 | tf_op jit(solution)/shard_map/all_to_all | solution.py:465
  19.3 0.0 copy-start
  19.3 0.0 copy-start.1
  19.3 0.0 copy-start.2
  19.4 0.0 copy-start.3
  19.4 0.0 copy-start.4
  19.4 0.2 collective-permute-start.1
  19.6 1.5 %collective-permute-start = (bf16[8,2048]{1,0:T(8,128)(2,1)}, bf16[8,2048]{1,0:T(8,128)(2,1)S(1)}, u32[]{:S(2)}, u32[]{:S(2)}) collective-permute-start(bf16[8,2048]{1,0:T(8,128)(2,1)} %feat.1), channel_id=1, source_target_pairs={{0,16},{16,32},{32,48},{48,64},{64,80},{80,96},{96,112},{112,128},... | collective-permute-start | bytes 98312 | tf_op jit(solution)/shard_map/ppermute | solution.py:461
  21.1 1.9 %shard_map.147 = (f32[16,8,128]{2,1,0:T(8,128)S(1)}, bf16[1,32,128,128]{3,2,1,0:T(8,128)(2,1)S(1)}) custom-call(bf16[8,2048]{1,0:T(8,128)(2,1)} %feat.1, bf16[1,4,32,128,128]{4,3,2,1,0:T(8,128)(2,1)} %tiles.7, s32[1,4,32]{2,1,0:T(4,128)} %dst_hbm.11, s32[1,4,32]{2,1,0:T(4,128)} %src_hbm.11, s32[1,4]{1,0:T(1,128)} %count_hbm.11), custom_call_target="tpu_custom_call" | custom-call | flops 16777216 | bytes 2097152 | tf_op jit(solution)/shard_map/pallas_call | solution.py:502
  23.1 0.7 collective-permute-done.1.foll
  23.8 0.0 collective-permute-done.prev
  23.8 1.9 %shard_map.148.part = f32[16,8,128]{2,1,0:T(8,128)S(1)} custom-call(bf16[8,2048]{1,0:T(8,128)(2,1)S(1)} %collective-permute-done.prev, bf16[8,2048]{1,0:T(8,128)(2,1)S(1)} %collective-permute-done.1.foll, f32[16,8,128]{2,1,0:T(8,128)S(1)} %get-tuple-element.20.before, bf16[1,4,32,128,128]{4,3,2,1,0:T(8,128)(2,1)} %tiles.7, s32[1,4,32]{2,1,0:T(4,128)} %dst_hbm.11, ...), custom_call_target="tpu_custom_call" | custom-call | flops 33554432 | bytes 2097152 | tf_op jit(solution)/shard_map/pallas_call | solution.py:519
  25.7 6.7 %all-to-all-done.recv = bf16[32,8,128]{2,1,0:T(8,128)(2,1)S(1)} async-done(((bf16[32,8,128]{2,1,0:T(8,128)(2,1)}), bf16[32,8,128]{2,1,0:T(8,128)(2,1)S(1)}, u32[]{:S(2)}, u32[]{:S(2)}) %all-to-all-start) | async-done | bytes 65568 | tf_op jit(solution)/shard_map/all_to_all | solution.py:465
  32.4 0.0 copy-done
  32.4 0.0 copy-done.1
  32.4 0.0 copy-done.2
  32.4 0.0 copy-done.3
  32.4 0.0 copy-done.4
  32.4 1.2 %shard_map.149 = bf16[16,80,128]{2,1,0:T(8,128)(2,1)S(1)} custom-call(bf16[32,8,128]{2,1,0:T(8,128)(2,1)S(1)} %all-to-all-done.recv, f32[16,8,128]{2,1,0:T(8,128)S(1)} %shard_map.148.part, bf16[8,2048]{1,0:T(8,128)(2,1)S(1)} %copy-done, bf16[16,2048]{1,0:T(8,128)(2,1)S(1)} %copy-done.1, bf16[16,128]{1,0:T(8,128)(2,1)S(1)} %bitcast.6, ...), custom_call_target="tpu_custom_call" | custom-call | flops 16777216 | bytes 1048576 | tf_op jit(solution)/shard_map/pallas_call | solution.py:534
  33.7 14.6 %all_to_all.25.r = bf16[16,80,128]{2,1,0:T(8,128)(2,1)S(1)} all-to-all(bf16[16,80,128]{2,1,0:T(8,128)(2,1)S(1)} %shard_map.149), channel_id=1, replica_groups=mesh['row'=32,'col'=16] {'col'}, dimensions={0} | all-to-all | bytes 655360 | tf_op jit(solution)/shard_map/all_to_all | solution.py:465
  48.2 0.4 shard_map.150
  48.7 10.8 %all_to_all.26.r = bf16[16,80,128]{2,1,0:T(8,128)(2,1)S(1)} all-to-all(bf16[16,80,128]{2,1,0:T(8,128)(2,1)S(1)} %shard_map.150), channel_id=1, replica_groups=mesh['row'=32,'col'=16] {'col'}, dimensions={0} | all-to-all | bytes 655360 | tf_op jit(solution)/shard_map/all_to_all | solution.py:465
  59.4 0.6 shard_map.153
  60.1 7.2 %all-to-all-start.3 = ((f32[4,8,128]{2,1,0:T(8,128)}), f32[4,8,128]{2,1,0:T(8,128)S(1)}, u32[]{:S(2)}, u32[]{:S(2)}) async-start(f32[4,8,128]{2,1,0:T(8,128)} %get-tuple-element.24), calls=%async_computation.3 | async-start | bytes 32768 | tf_op jit(solution)/shard_map/all_to_all | solution.py:465
  67.3 1.3 %shard_map.152.far = f32[8,8,128]{2,1,0:T(8,128)S(1)} custom-call(bf16[16,80,128]{2,1,0:T(8,128)(2,1)S(1)} %all_to_all.26.r, bf16[1,32,128,128]{3,2,1,0:T(8,128)(2,1)S(1)} %get-tuple-element.21.kept, s32[1,4,32]{2,1,0:T(4,128)} %dst_hbm.11, s32[1,4,32]{2,1,0:T(4,128)} %src_hbm.11, s32[1,4]{1,0:T(1,128)} %count_hbm.11), custom_call_target="tpu_custom_call" | custom-call | flops 16777216 | bytes 1048576 | tf_op jit(solution)/shard_map/pallas_call | solution.py:575
  68.6 1.8 %all-to-all-done.3.piece = f32[4,8,128]{2,1,0:T(8,128)S(1)} async-done(((f32[4,8,128]{2,1,0:T(8,128)}), f32[4,8,128]{2,1,0:T(8,128)S(1)}, u32[]{:S(2)}, u32[]{:S(2)}) %all-to-all-start.3) | async-done | bytes 16416 | tf_op jit(solution)/shard_map/all_to_all | solution.py:465
  70.4 0.7 shard_map.154
  71.1 6.3 %all-to-all-start.4 = ((bf16[32,16,128]{2,1,0:T(8,128)(2,1)}), bf16[32,16,128]{2,1,0:T(8,128)(2,1)S(1)}, u32[]{:S(2)}, u32[]{:S(2)}) async-start(bf16[32,16,128]{2,1,0:T(8,128)(2,1)} %shard_map.154), calls=%async_computation.4 | async-start | bytes 262144 | tf_op jit(solution)/shard_map/all_to_all | solution.py:465
  77.5 2.0 %shard_map.155 = (f32[8,2048]{1,0:T(8,128)S(1)}, f32[8,2048]{1,0:T(8,128)S(1)}) custom-call(bf16[16,80,128]{2,1,0:T(8,128)(2,1)S(1)} %all_to_all.26.r, bf16[1,4,32,128,128]{4,3,2,1,0:T(8,128)(2,1)} %tiles.7, s32[1,4,32]{2,1,0:T(4,128)} %dst_hbm.11, s32[1,4,32]{2,1,0:T(4,128)} %src_hbm.11, s32[1,4]{1,0:T(1,128)} %count_hbm.11), custom_call_target="tpu_custom_call" | custom-call | flops 33554432 | bytes 2097152 | tf_op jit(solution)/shard_map/pallas_call | solution.py:588
  79.5 0.2 collective-permute-start.2
  79.8 1.7 %collective-permute-start.3 = (f32[8,2048]{1,0:T(8,128)S(1)}, f32[8,2048]{1,0:T(8,128)S(1)}, u32[]{:S(2)}, u32[]{:S(2)}) collective-permute-start(f32[8,2048]{1,0:T(8,128)S(1)} %get-tuple-element.28), channel_id=1, source_target_pairs={{0,16},{16,32},{32,48},{48,64},{64,80},{80,96},{96,112},{112,128},... | collective-permute-start | bytes 196616 | tf_op jit(solution)/shard_map/ppermute | solution.py:461
  81.4 2.6 %shard_map.151 = (f32[8,2048]{1,0:T(8,128)S(1)}, bf16[16,2048]{1,0:T(8,128)(2,1)}) custom-call(bf16[16,80,128]{2,1,0:T(8,128)(2,1)S(1)} %all_to_all.26.r, bf16[1,4,32,128,128]{4,3,2,1,0:T(8,128)(2,1)} %tiles.7, s32[1,4,32]{2,1,0:T(4,128)} %dst_hbm.11, s32[1,4,32]{2,1,0:T(4,128)} %src_hbm.11, s32[1,4]{1,0:T(1,128)} %count_hbm.11), custom_call_target="tpu_custom_call" | custom-call | flops 16777216 | bytes 1048576 | tf_op jit(solution)/shard_map/pallas_call | solution.py:599
  84.0 0.7 collective-permute-done.2.after
  84.8 0.0 collective-permute-done.3.before
  84.8 8.5 %all-to-all-done.4.recv = bf16[32,16,128]{2,1,0:T(8,128)(2,1)S(1)} async-done(((bf16[32,16,128]{2,1,0:T(8,128)(2,1)}), bf16[32,16,128]{2,1,0:T(8,128)(2,1)S(1)}, u32[]{:S(2)}, u32[]{:S(2)}) %all-to-all-start.4) | async-done | bytes 131104 | tf_op jit(solution)/shard_map/all_to_all | solution.py:465
  93.3 0.9 shard_map.156
Async XLA Ops:
  2.6 29.8 %all-to-all-start = ((bf16[32,8,128]{2,1,0:T(8,128)(2,1)}), bf16[32,8,128]{2,1,0:T(8,128)(2,1)S(1)}, u32[]{:S(2)}, u32[]{:S(2)}) async-start(bf16[32,8,128]{2,1,0:T(8,128)(2,1)} %get-tuple-element.19), calls=%async_computation | async-start | bytes 131072 | tf_op jit(solution)/shard_map/all_to_all | solution.py:465
  19.3 13.1 %copy-start = (bf16[8,2048]{1,0:T(8,128)(2,1)S(1)}, bf16[8,2048]{1,0:T(8,128)(2,1)}, u32[]{:S(2)}) copy-start(bf16[8,2048]{1,0:T(8,128)(2,1)} %feat.1) | copy-start | bytes 98308
  19.3 13.1 %copy-start.1 = (bf16[16,2048]{1,0:T(8,128)(2,1)S(1)}, bf16[16,2048]{1,0:T(8,128)(2,1)}, u32[]{:S(2)}) copy-start(bf16[16,2048]{1,0:T(8,128)(2,1)} %cot.1) | copy-start | bytes 196612
  19.3 13.1 %copy-start.2 = (bf16[128,16]{0,1:T(8,128)(2,1)S(1)}, bf16[128,16]{0,1:T(8,128)(2,1)}, u32[]{:S(2)}) copy-start(bf16[128,16]{0,1:T(8,128)(2,1)} %param.18) | copy-start | bytes 12292
  19.4 13.1 %copy-start.3 = (bf16[128,16]{0,1:T(8,128)(2,1)S(1)}, bf16[128,16]{0,1:T(8,128)(2,1)}, u32[]{:S(2)}) copy-start(bf16[128,16]{0,1:T(8,128)(2,1)} %param.19) | copy-start | bytes 12292
  19.4 13.1 %copy-start.4 = (f32[16]{0:T(128)S(1)}, f32[16]{0:T(128)}, u32[]{:S(2)}) copy-start(f32[16]{0:T(128)} %param.20) | copy-start | bytes 196
  19.4 4.4 %collective-permute-start.1 = (bf16[8,2048]{1,0:T(8,128)(2,1)}, bf16[8,2048]{1,0:T(8,128)(2,1)S(1)}, u32[]{:S(2)}, u32[]{:S(2)}) collective-permute-start(bf16[8,2048]{1,0:T(8,128)(2,1)} %feat.1), channel_id=1, source_target_pairs={{0,496},{16,0},{32,16},{48,32},{64,48},{80,64},{96,80},{112,96},{1... | collective-permute-start | bytes 98312 | tf_op jit(solution)/shard_map/ppermute | solution.py:461
  19.6 4.2 %collective-permute-start = (bf16[8,2048]{1,0:T(8,128)(2,1)}, bf16[8,2048]{1,0:T(8,128)(2,1)S(1)}, u32[]{:S(2)}, u32[]{:S(2)}) collective-permute-start(bf16[8,2048]{1,0:T(8,128)(2,1)} %feat.1), channel_id=1, source_target_pairs={{0,16},{16,32},{32,48},{48,64},{64,80},{80,96},{96,112},{112,128},... | collective-permute-start | bytes 98312 | tf_op jit(solution)/shard_map/ppermute | solution.py:461
  60.1 10.3 %all-to-all-start.3 = ((f32[4,8,128]{2,1,0:T(8,128)}), f32[4,8,128]{2,1,0:T(8,128)S(1)}, u32[]{:S(2)}, u32[]{:S(2)}) async-start(f32[4,8,128]{2,1,0:T(8,128)} %get-tuple-element.24), calls=%async_computation.3 | async-start | bytes 32768 | tf_op jit(solution)/shard_map/all_to_all | solution.py:465
  71.1 22.1 %all-to-all-start.4 = ((bf16[32,16,128]{2,1,0:T(8,128)(2,1)}), bf16[32,16,128]{2,1,0:T(8,128)(2,1)S(1)}, u32[]{:S(2)}, u32[]{:S(2)}) async-start(bf16[32,16,128]{2,1,0:T(8,128)(2,1)} %shard_map.154), calls=%async_computation.4 | async-start | bytes 262144 | tf_op jit(solution)/shard_map/all_to_all | solution.py:465
  79.5 5.2 %collective-permute-start.2 = (f32[8,2048]{1,0:T(8,128)S(1)}, f32[8,2048]{1,0:T(8,128)S(1)}, u32[]{:S(2)}, u32[]{:S(2)}) collective-permute-start(f32[8,2048]{1,0:T(8,128)S(1)} %get-tuple-element.27), channel_id=1, source_target_pairs={{0,496},{16,0},{32,16},{48,32},{64,48},{80,64},{96,80},{112,96},{1... | collective-permute-start | bytes 196616 | tf_op jit(solution)/shard_map/ppermute | solution.py:461
  79.8 5.0 %collective-permute-start.3 = (f32[8,2048]{1,0:T(8,128)S(1)}, f32[8,2048]{1,0:T(8,128)S(1)}, u32[]{:S(2)}, u32[]{:S(2)}) collective-permute-start(f32[8,2048]{1,0:T(8,128)S(1)} %get-tuple-element.28), channel_id=1, source_target_pairs={{0,16},{16,32},{32,48},{48,64},{64,80},{80,96},{96,112},{112,128},... | collective-permute-start | bytes 196616 | tf_op jit(solution)/shard_map/ppermute | solution.py:461

commit v3 on v2

--- a/solution.py
+++ b/solution.py
@@ -20,9 +20,11 @@
 NODES_LOC = RT * TILE
 NB = NROW * BMAX // TILE
 PER = TILE // BMAX
-RS = 4
+RET = 5
 FWD_ROWS = 80
 BWD_ROWS = 80
+FIRST_ROW = 20
+FIRST_COL = 11
 F32, BF16 = jnp.float32, jnp.bfloat16
 NT = (((1,), (1,)), ((), ()))
 TN = (((0,), (0,)), ((), ()))
@@ -40,6 +42,14 @@
 
 def dot(a, b, dims=(((1,), (0,)), ((), ()))):
     return lax.dot_general(a, b, dims, preferred_element_type=F32)
+
+
+def row_at(p):
+    return (p - FIRST_ROW) % NROW
+
+
+def col_at(c):
+    return (c - FIRST_COL) % NCOL
 
 
 def iota(shape, dim):
@@ -94,6 +104,46 @@
                 @pl.when(count[0, g] > c * CHUNK)
                 def _():
                     chunk_copy(tiles, held, g, c, slot, sems).start()
+
+
+def by_row(k, parts):
+    out = parts[0]
+    for i in range(1, PER):
+        out = jnp.where(k == i, parts[i], out)
+    return out
+
+
+def in_place():
+    shape = (NROW * FEAT, TILE)
+    return iota(shape, 1) // BMAX == iota(shape, 0) % PER
+
+
+def compact(groups):
+    k = iota((FEAT, TILE), 0) % PER
+    moved = []
+    for g in groups:
+        turned = [g] + [pltpu.roll(g, BMAX * c, 1) for c in range(1, PER)]
+        for b in range(PER):
+            moved.append(by_row(k, [turned[(i - b) % PER] for i in range(PER)]))
+    rows = jnp.where(in_place(), jnp.concatenate(moved, axis=0), 0.0).astype(BF16)
+    shape = (NROW * 2, NROW * FEAT)
+    pick = jnp.where(iota(shape, 0) == iota(shape, 1) // PER, 1.0, 0.0).astype(BF16)
+    return dot(pick, rows)
+
+
+def spread_out(rows):
+    shape = (NROW * FEAT, NROW * 2)
+    pick = jnp.where(iota(shape, 1) == iota(shape, 0) // PER, 1.0, 0.0).astype(BF16)
+    wide = jnp.where(in_place(), dot(pick, rows), 0.0)
+    k = iota((FEAT, TILE), 0) % PER
+    out = []
+    for m in range(NB):
+        parts = [wide[p * FEAT : (p + 1) * FEAT] for p in range(PER * m, PER * m + PER)]
+        x = by_row(k, parts)
+        for c in range(1, PER):
+            x = x + pltpu.roll(by_row(k, [parts[(i + c) % PER] for i in range(PER)]), BMAX * c, 1)
+        out.append(x)
+    return out
 
 
 def gather_kernel(feat_hbm, rows_hbm, counts_hbm, out, index, feat, rows, counts, scr, sems):
@@ -111,6 +161,7 @@
     index[...] = idx
     x = jnp.concatenate([tile_of(feat, t).astype(F32) for t in range(RT)], axis=0).astype(BF16)
     place = iota((TILE, TILE), 0)
+    groups = []
     for m in range(NB):
         row = idx[m : m + 1, :]
         hot = jnp.where(place == (row & (TILE - 1)), 1.0, 0.0).astype(BF16)
@@ -119,9 +170,10 @@
         g = jnp.zeros((FEAT, TILE), F32)
         for t in range(RT):
             g = g + jnp.where(tile == t, c[t * FEAT : (t + 1) * FEAT], 0.0)
-        for b in range(PER):
-            moved = g if b == 0 else pltpu.roll(g, TILE - BMAX * b, 1)
-            out[PER * m + b] = moved.astype(BF16)
+        groups.append(g)
+    rows2 = compact(groups).astype(BF16)
+    for p in range(NROW):
+        out[row_at(p)] = rows2[2 * p : 2 * p + 2]
 
 
 def store_source(lo, hi, k, x):
@@ -157,18 +209,21 @@
 
 
 def own_kernel(
-    feat_hbm, tiles, dst_hbm, src_hbm, count_hbm, part, kept, feat, dst, src, count, held, lo, hi,
-    sems, chunk_sems, kept_sems,
+    feat_hbm, tiles, dst_hbm, src_hbm, count_hbm, part, near, far, dst_out, src_out, count_out,
+    feat, dst, src, count, held, lo, hi, sems, own_sems, near_sems, far_sems,
 ):
     copies = start_all(
-        (count_hbm, dst_hbm, src_hbm, feat_hbm), (count, dst, src, feat), sems
+        (count_hbm, dst_hbm, src_hbm, feat_hbm, dst_hbm, src_hbm, count_hbm),
+        (count, dst, src, feat, dst_out, src_out, count_out),
+        sems,
     )
-    start_chunks(tiles, held, [0], count, chunk_sems, 0, 1)
-    start_chunks(tiles, kept, [3], count, kept_sems, 0, 1)
+    work = ((held, [0], own_sems), (near, [1, 2], near_sems), (far, [3], far_sems))
+    for place, groups, place_sems in work:
+        start_chunks(tiles, place, groups, count, place_sems, 0, 1)
     copies[0].wait()
-    start_chunks(tiles, held, [0], count, chunk_sems, 1, NCHUNK)
-    start_chunks(tiles, kept, [3], count, kept_sems, 1, NCHUNK)
-    wait_all(copies[1:])
+    for place, groups, place_sems in work:
+        start_chunks(tiles, place, groups, count, place_sems, 1, NCHUNK)
+    wait_all(copies[1:4])
     for k in range(RT):
         store_source(lo, hi, k, tile_of(feat, k).astype(F32))
     zero_source(lo, hi, RT)
@@ -176,43 +231,37 @@
     n = count[0, 0]
 
     def step(it, carry):
-        chunk_copy(tiles, held, 0, it, 0, chunk_sems).wait()
-        forward_step(
-            it, 0, 0, RT, lo, hi, lambda i: held[0, pl.ds(i, 2)], dst, src, n, part
-        )
+        chunk_copy(tiles, held, 0, it, 0, own_sems).wait()
+        forward_step(it, 0, 0, RT, lo, hi, lambda i: held[0, pl.ds(i, 2)], dst, src, n, part)
         return carry
 
     lax.fori_loop(0, steps(n), step, 0)
-
-    def kept_wait(it, carry):
-        chunk_copy(tiles, kept, 3, it, 0, kept_sems).wait()
-        return carry
-
-    lax.fori_loop(0, steps(count[0, 3]), kept_wait, 0)
-
-
-def near_kernel(
-    prev, foll, before, tiles, dst_hbm, src_hbm, count_hbm, part, dst, src, count, held, lo, hi,
-    sems, chunk_sems,
-):
-    copies = start_all((count_hbm, dst_hbm, src_hbm), (count, dst, src), sems)
-    start_chunks(tiles, held, [1, 2], count, chunk_sems, 0, 1)
+    for place, groups, place_sems in work[1:]:
+        for slot, g in enumerate(groups):
+
+            def arrived(it, carry):
+                chunk_copy(tiles, place, g, it, slot, place_sems).wait()
+                return carry
+
+            lax.fori_loop(0, steps(count[0, g]), arrived, 0)
+    wait_all(copies[4:])
+
+
+def near_kernel(prev, foll, before, near, dst_in, src_in, count_in, part, dst, src, count, lo, hi, sems):
+    copies = start_all((count_in, dst_in, src_in), (count, dst, src), sems)
     for k in range(RT):
         store_source(lo, hi, k, tile_of(prev, k).astype(F32))
         store_source(lo, hi, RT + k, tile_of(foll, k).astype(F32))
     zero_source(lo, hi, 2 * RT)
     part[...] = before[...]
-    copies[0].wait()
-    start_chunks(tiles, held, [1, 2], count, chunk_sems, 1, NCHUNK)
-    wait_all(copies[1:])
+    wait_all(copies)
     for slot, g in enumerate([1, 2]):
         n = count[0, g]
 
         def step(it, carry):
-            chunk_copy(tiles, held, g, it, slot, chunk_sems).wait()
             forward_step(
                 it, g, slot * RT, 2 * RT, lo, hi,
-                lambda i: held[slot, pl.ds(i, 2)], dst, src, n, part,
+                lambda i: near[slot, pl.ds(i, 2)], dst, src, n, part,
             )
             return carry
 
@@ -224,12 +273,8 @@
     lo, hi, acc, sems,
 ):
     copies = start_all((count_hbm, dst_hbm, src_hbm), (count, dst, src), sems)
-    lane = iota((FEAT, TILE), 1)
-    for k in range(NB):
-        x = recv[PER * k].astype(F32)
-        for b in range(1, PER):
-            moved = pltpu.roll(recv[PER * k + b].astype(F32), BMAX * b, 1)
-            x = jnp.where(lane // BMAX == b, moved, x)
+    rows = jnp.concatenate([recv[row_at(p)].astype(F32) for p in range(NROW)], axis=0).astype(BF16)
+    for k, x in enumerate(spread_out(rows)):
         store_source(lo, hi, k, x)
     zero_source(lo, hi, NB)
     acc[...] = part[...]
@@ -254,20 +299,21 @@
     block = block.astype(BF16)
     for d in range(RT):
         both = jnp.concatenate([acc[d], tile_of(feat, d).astype(F32)], axis=0)
-        buf[d, 0:16] = both.astype(BF16)
-        buf[d, 16:32] = tile_of(cot, d)
-        buf[d, 32:48] = wst[...]
-        buf[d, 48:64] = wnt[...]
-        buf[d, 64:80] = block
+        at = col_at(d)
+        buf[at, 0:16] = both.astype(BF16)
+        buf[at, 16:32] = tile_of(cot, d)
+        buf[at, 32:48] = wst[...]
+        buf[at, 48:64] = wnt[...]
+        buf[at, 64:80] = block
 
 
 def dense_kernel(r, out):
-    wst = jnp.concatenate([r[c, 32:48] for c in range(NCOL)], axis=0)
-    wnt = jnp.concatenate([r[c, 48:64] for c in range(NCOL)], axis=0)
-    cot = jnp.concatenate([r[c, 16:32] for c in range(NCOL)], axis=0).astype(F32)
-    bias = jnp.concatenate([r[c, 64:80] for c in range(NCOL)], axis=0).astype(F32)
+    wst = jnp.concatenate([r[col_at(c), 32:48] for c in range(NCOL)], axis=0)
+    wnt = jnp.concatenate([r[col_at(c), 48:64] for c in range(NCOL)], axis=0)
+    cot = jnp.concatenate([r[col_at(c), 16:32] for c in range(NCOL)], axis=0).astype(F32)
+    bias = jnp.concatenate([r[col_at(c), 64:80] for c in range(NCOL)], axis=0).astype(F32)
     bias = bias[:, 0:1] + bias[:, 1:2] + bias[:, 2:3]
-    heads = [r[c, 0:16].astype(F32) for c in range(NCOL)]
+    heads = [r[col_at(c), 0:16].astype(F32) for c in range(NCOL)]
     agg = jnp.concatenate([h[:FEAT] for h in heads], axis=0).astype(BF16)
     feats = jnp.concatenate([h[FEAT:] for h in heads], axis=0).astype(BF16)
     pre = dot(wst, feats) + dot(wnt, agg) + bias
@@ -291,25 +337,27 @@
         bsum = jnp.where((lane >= BMAX) & (lane < BMAX + HLOC), bsum, 0.0)
         bhi = bsum.astype(BF16).astype(F32)
         bsum = jnp.where(sub == 0, bhi, jnp.where(sub == 1, bsum - bhi, 0.0))
-        out[c, 0:16] = jnp.concatenate([agg_grad[f], own_hi[f]], axis=0).astype(BF16)
-        out[c, 16:32] = hidden[h]
-        out[c, 32:48] = gs[h]
-        out[c, 48:64] = gn[h]
-        out[c, 64:80] = jnp.concatenate([own_lo[f], bsum], axis=0).astype(BF16)
-
-
-def weights_kernel(r, out, bsum):
+        out[col_at(c), 0:16] = jnp.concatenate([agg_grad[f], own_hi[f]], axis=0).astype(BF16)
+        out[col_at(c), 16:32] = hidden[h]
+        out[col_at(c), 32:48] = gs[h]
+        out[col_at(c), 48:64] = gn[h]
+        out[col_at(c), 64:80] = jnp.concatenate([own_lo[f], bsum], axis=0).astype(BF16)
+
+
+def weights_kernel(r, kept, given, bsum):
     total = r[0, 32:64].astype(F32)
     tail = r[0, 64:80].astype(F32)[FEAT:]
     for d in range(1, RT):
         total = total + r[d, 32:64].astype(F32)
         tail = tail + r[d, 64:80].astype(F32)[FEAT:]
-    for s in range(RS):
-        out[s] = total[s * 8 : (s + 1) * 8]
+    first = lax.axis_index("row") % 2 == 0
+    kept[...] = jnp.where(first, total[:HLOC], total[HLOC:])
+    given[...] = jnp.where(first, total[HLOC:], total[:HLOC])
     both = tail[0:1] + tail[1:2]
     hi = both.astype(BF16).astype(F32)
-    sub = iota((FEAT, TILE), 0)
-    bsum[...] = jnp.where(sub == 0, hi, jnp.where(sub == 1, both - hi, 0.0))
+    lo = pltpu.roll(jnp.broadcast_to(both - hi, (FEAT, TILE)), HLOC, 1)[0:1]
+    lane = iota((1, TILE), 1)
+    bsum[...] = jnp.where(lane < BMAX + HLOC, hi, lo)
 
 
 def backward_step(it, g, base, none, lo, hi, tile_at, dst, src, n, acc):
@@ -330,11 +378,11 @@
 
 def load_grads(r, lo, hi):
     for d in range(RT):
-        store_source(lo, hi, d, r[d, 0:16].astype(F32)[:FEAT])
+        store_source(lo, hi, d, r[col_at(d), 0:16].astype(F32)[:FEAT])
     zero_source(lo, hi, RT)
 
 
-def back_far_kernel(r, kept, dst_hbm, src_hbm, count_hbm, acc, dst, src, count, lo, hi, sems):
+def back_far_kernel(r, kept, dst_hbm, src_hbm, count_hbm, out, dst, src, count, lo, hi, acc, sems):
     copies = start_all((count_hbm, dst_hbm, src_hbm), (count, dst, src), sems)
     load_grads(r, lo, hi)
     acc[...] = jnp.zeros_like(acc)
@@ -346,20 +394,19 @@
         return carry
 
     lax.fori_loop(0, steps(n), step, 0)
-
-
-def pack_kernel(far, bsum, piece, out):
-    mine = piece[0]
-    for s in range(1, RS):
-        mine = mine + piece[s]
-    extra = bsum[...]
-    lane = iota((FEAT, TILE), 1)
-    for k in range(NB):
-        x = far[k]
-        for b in range(PER):
-            moved = pltpu.roll(x, TILE - BMAX * b, 1) if b else x
-            moved = jnp.where(lane < BMAX, moved, extra)
-            out[PER * k + b] = jnp.concatenate([moved, mine], axis=0).astype(BF16)
+    rows = compact([acc[k] for k in range(NB)]).astype(BF16)
+    for p in range(NROW):
+        out[p] = rows[2 * p : 2 * p + 2]
+
+
+def pack_kernel(far, bsum, kept, got, out):
+    mine = (kept[...] + got[...]).astype(BF16)
+    extra = jnp.broadcast_to(bsum[...], (2, TILE))
+    for p in range(NROW):
+        at = RET * row_at(p)
+        out[at] = jnp.concatenate([far[p].astype(F32), extra], axis=0).astype(BF16)
+        for i in range(4):
+            out[at + 1 + i] = mine[4 * i : 4 * i + 4]
 
 
 def back_groups(
@@ -390,8 +437,8 @@
     acc = scratch[6]
     for k in range(RT):
         cols = slice(k * TILE, (k + 1) * TILE)
-        prev[:, cols] = acc[k]
-        foll[:, cols] = acc[RT + k]
+        prev[:, cols] = acc[k].astype(BF16)
+        foll[:, cols] = acc[RT + k].astype(BF16)
 
 
 def back_own_kernel(r, tiles, dst_hbm, src_hbm, count_hbm, own, hidden, *scratch):
@@ -399,29 +446,33 @@
     acc = scratch[6]
     for k in range(RT):
         cols = slice(k * TILE, (k + 1) * TILE)
-        tail = r[k, 64:80].astype(F32)
-        own[:, cols] = acc[k] + r[k, 0:16].astype(F32)[FEAT:] + tail[:FEAT]
-        hidden[:, cols] = r[k, 16:32]
+        at = col_at(k)
+        tail = r[at, 64:80].astype(F32)
+        own[:, cols] = acc[k] + r[at, 0:16].astype(F32)[FEAT:] + tail[:FEAT]
+        hidden[:, cols] = r[at, 16:32]
 
 
 def final_kernel(recv, index, own, after, before, grad, gs, gn, gb, *, scale):
-    lane = iota((FEAT, TILE), 1)
     place = iota((TILE, TILE), 0)
     lefts, rights = [], []
-    pieces = [jnp.zeros((8, TILE), F32) for _ in range(RS)]
-    bsum = jnp.zeros((FEAT, TILE), F32)
-    for k in range(NB):
+    heads = [recv[RET * row_at(p)].astype(F32) for p in range(NROW)]
+    rows = jnp.concatenate([h[:2] for h in heads], axis=0).astype(BF16)
+    bsum = heads[0]
+    for h in heads[1:]:
+        bsum = bsum + h
+    bsum = bsum[2:3]
+    halves = []
+    for half in range(2):
+        quarters = []
+        for i in range(4):
+            q = recv[RET * row_at(half) + 1 + i].astype(F32)
+            for p in range(half + 2, NROW, 2):
+                q = q + recv[RET * row_at(p) + 1 + i].astype(F32)
+            quarters.append(q)
+        halves.append(jnp.concatenate(quarters, axis=0) * scale)
+    for k, x in enumerate(spread_out(rows)):
         row = index[k : k + 1, :]
         tile = row >> 7
-        x = jnp.zeros((FEAT, TILE), F32)
-        for b in range(PER):
-            p = PER * k + b
-            block = recv[p].astype(F32)
-            head = block[:FEAT]
-            bsum = bsum + head
-            pieces[p % RS] = pieces[p % RS] + block[FEAT:]
-            moved = pltpu.roll(head, BMAX * b, 1) if b else head
-            x = jnp.where(lane // BMAX == b, moved, x)
         lefts.append(
             jnp.concatenate([jnp.where(tile == t, x, 0.0) for t in range(RT)], axis=0).astype(BF16)
         )
@@ -429,13 +480,14 @@
     spread = dot(jnp.concatenate(lefts, axis=1), jnp.concatenate(rights, axis=1), NT)
     for t in range(RT):
         cols = slice(t * TILE, (t + 1) * TILE)
-        total = own[:, cols] + after[:, cols] + before[:, cols]
+        total = own[:, cols] + (after[:, cols].astype(F32) + before[:, cols].astype(F32))
         grad[:, cols] = (total + spread[t * FEAT : (t + 1) * FEAT]).astype(BF16)
-    weights = jnp.concatenate(pieces, axis=0) * scale
-    gs[...] = weights[:HLOC]
-    gn[...] = weights[HLOC:]
-    bias = pltpu.roll((bsum[0:1] + bsum[1:2]) * scale, TILE - BMAX, 1)
-    gb[...] = bias[:, :HLOC]
+    gs[...] = halves[0]
+    gn[...] = halves[1]
+    bsum = jnp.broadcast_to(bsum * scale, (FEAT, TILE))
+    hi = pltpu.roll(bsum, TILE - BMAX, 1)
+    lo = pltpu.roll(bsum, TILE - BMAX - HLOC, 1)
+    gb[...] = (hi + lo)[0:1, :HLOC]
 
 
 def held(groups):
@@ -461,8 +513,10 @@
     return lax.ppermute(shard, "row", [(i, (i + by) % NROW) for i in range(NROW)])
 
 
-def swap(x, axis, groups=None):
-    return lax.all_to_all(x, axis, 0, 0, axis_index_groups=groups, tiled=True)
+def swap(x, axis, first):
+    size = lax.axis_size(axis)
+    group = [(first + i) % size for i in range(size)]
+    return lax.all_to_all(x, axis, 0, 0, axis_index_groups=[group], tiled=True)
 
 
 def per_device(
@@ -486,7 +540,7 @@
     following = shifted(features, -1)
     outgoing, index = call(
         gather_kernel,
-        (sds((NROW, FEAT, TILE), BF16), sds((NB, TILE), jnp.int32)),
+        (sds((NROW, 2, TILE), BF16), sds((NB, TILE), jnp.int32)),
         [HB] * 3,
         (VM, VM),
         [
@@ -498,43 +552,45 @@
         ],
         flops=2 * TILE * TILE * NROW * BMAX,
     )(in_hbm(features), in_hbm(send_rows), in_hbm(send_count))
-    incoming = swap(outgoing, "row")
-    part, kept = call(
+    incoming = swap(outgoing, "row", FIRST_ROW)
+    part, near, kept, *here = call(
         own_kernel,
-        (sds((RT, FEAT, TILE), F32), sds((1, 32, TILE, TILE), BF16)),
+        (
+            sds((RT, FEAT, TILE), F32),
+            sds((2, 32, TILE, TILE), BF16),
+            sds((1, 32, TILE, TILE), BF16),
+            sds((1, 4, 32), jnp.int32),
+            sds((1, 4, 32), jnp.int32),
+            sds((1, 4), jnp.int32),
+        ),
         [HB] * 5,
-        (VM, VM),
+        (VM,) * 6,
         [
             pltpu.VMEM((FEAT, NODES_LOC), BF16),
             *TABLES,
             held(1),
             *sources(RT),
-            pltpu.SemaphoreType.DMA((4,)),
+            pltpu.SemaphoreType.DMA((7,)),
             pltpu.SemaphoreType.DMA((1, NCHUNK)),
+            pltpu.SemaphoreType.DMA((2, NCHUNK)),
             pltpu.SemaphoreType.DMA((1, NCHUNK)),
         ],
         flops=2 * 16 * TILE * TILE * 32,
-        nbytes=2 << 20,
+        nbytes=4 << 20,
     )(in_hbm(features), tiles, *tables)
     part = call(
         near_kernel,
         sds((RT, FEAT, TILE), F32),
-        [VM] * 3 + [HB] * 4,
+        [VM] * 7,
         VM,
-        [
-            *TABLES,
-            held(2),
-            *sources(2 * RT),
-            pltpu.SemaphoreType.DMA((3,)),
-            pltpu.SemaphoreType.DMA((2, NCHUNK)),
-        ],
+        [*TABLES, *sources(2 * RT), pltpu.SemaphoreType.DMA((3,))],
         flops=2 * 16 * TILE * TILE * 64,
         nbytes=2 << 20,
-    )(previous, following, part, tiles, *tables)
+    )(previous, following, part, near, *here)
     buf = call(
         far_kernel,
         sds((NCOL, FWD_ROWS, TILE), BF16),
-        [VM] * 8 + [HB] * 3,
+        [VM] * 11,
         VM,
         [
             *TABLES,
@@ -553,9 +609,9 @@
         w_neigh.T,
         bias.reshape(1, HLOC),
         kept,
-        *tables,
+        *here,
     )
-    by_node = swap(buf, "col")
+    by_node = swap(buf, "col", FIRST_COL)
     sent = call(
         dense_kernel,
         sds((NCOL, BWD_ROWS, TILE), BF16),
@@ -563,48 +619,50 @@
         VM,
         flops=2 * D_IN * HID * TILE * 6,
     )(by_node)
-    back = swap(sent, "col")
-    weights, bsum = call(
-        weights_kernel,
-        (sds((RS, 8, TILE), F32), sds((FEAT, TILE), F32)),
-        [VM],
-        (VM, VM),
+    back = swap(sent, "col", FIRST_COL)
+    half = sds((HLOC, TILE), F32)
+    kept_half, given_half, bsum = call(
+        weights_kernel, (half, half, sds((1, TILE), F32)), [VM], (VM, VM, VM)
     )(back)
-    groups = [[i + k for k in range(RS)] for i in range(0, NROW, RS)]
-    pieces = swap(weights, "row", groups)
+    got_half = lax.ppermute(given_half, "row", [(i, i ^ 1) for i in range(NROW)])
     far = call(
         back_far_kernel,
-        sds((NB, FEAT, TILE), F32),
-        [VM] * 2 + [HB] * 3,
+        sds((NROW, 2, TILE), BF16),
+        [VM] * 5,
         VM,
-        [*TABLES, *sources(RT), pltpu.SemaphoreType.DMA((3,))],
+        [
+            *TABLES,
+            *sources(RT),
+            pltpu.VMEM((NB, FEAT, TILE), F32),
+            pltpu.SemaphoreType.DMA((3,)),
+        ],
         flops=2 * 16 * TILE * TILE * 32,
         nbytes=1 << 20,
-    )(back, kept, *tables)
-    returning = call(pack_kernel, sds((NROW, 2 * FEAT, TILE), BF16), [VM] * 3, VM)(
-        far, bsum, pieces
+    )(back, kept, *here)
+    returning = call(pack_kernel, sds((NROW * RET, 4, TILE), BF16), [VM] * 4, VM)(
+        far, bsum, kept_half, got_half
     )
-    returned = swap(returning, "row")
+    returned = swap(returning, "row", FIRST_ROW)
     to_previous, to_following = call(
         back_near_kernel,
-        (sds((FEAT, NODES_LOC), F32),) * 2,
-        [VM] + [HB] * 4,
+        (sds((FEAT, NODES_LOC), BF16),) * 2,
+        [VM, HB] + [VM] * 3,
         (VM, VM),
         back_scratch(2),
         flops=2 * 16 * TILE * TILE * 64,
         nbytes=2 << 20,
-    )(back, tiles, *tables)
+    )(back, tiles, *here)
     after = shifted(to_previous, -1)
     before = shifted(to_following, 1)
     own, hidden = call(
         back_own_kernel,
         (sds((FEAT, NODES_LOC), F32), sds((HLOC, NODES_LOC), BF16)),
-        [VM] + [HB] * 4,
+        [VM, HB] + [VM] * 3,
         (VM, VM),
         back_scratch(1),
         flops=2 * 16 * TILE * TILE * 32,
         nbytes=1 << 20,
-    )(back, tiles, *tables)
+    )(back, tiles, *here)
     grad_features, grad_self, grad_neigh, grad_bias = call(
         functools.partial(final_kernel, scale=1.0 / math.sqrt(NROW * NODES_LOC)),
         (

time: 94.8 us -> 83.2 us (0.88)
  waiting for transfers between devices: 18.4 us -> 4.68 us
  starting transfers between devices: 34 us -> 38.8 us
  blocking collectives: 25.3 us -> 23.1 us
    all_to_all x3 -> x2, waiting for transfers between devices: 17 us -> 1.79 us  [swap(): return lax.all_to_all(x, axis, 0, 0, axis_index_groups=[group], tiled=True)]
    ppermute x0 -> x1, starting transfers between devices: none -> 5.46 us  [per_device(): lax.ppermute(given_half, 'row', [(i, i ^ 1) for i in range(NROW)])]
    all_to_all x2, blocking collectives: 25.3 us -> 23.1 us  [swap(): return lax.all_to_all(x, axis, 0, 0, axis_index_groups=[group], tiled=True)]
    ppermute x4, waiting for transfers between devices: 1.44 us -> 2.89 us  [shifted(): lax.ppermute(shard, 'row', [(i, (i + by) % NROW) for i in range(NROW)])]
    all_to_all x3 -> x2, starting transfers between devices: 30.3 us -> 30.2 us  [swap(): return lax.all_to_all(x, axis, 0, 0, axis_index_groups=[group], tiled=True)]
  transfers between devices with their start and end apart: 7 -> 7, of which waited for: 5 -> 3; matrix products, arithmetic and copies ran while one was open for 0% -> 0% of each run, Pallas kernels for 10% -> 12%
where the time goes in v3:
time: 83.2 us; the launch traced here: 82.7 us
  starting transfers between devices  38.8 us (47%)
  blocking collectives  23.1 us (28%)
  Pallas kernels  15.3 us (18%)
  waiting for transfers between devices  4.68 us (6%)
    all_to_all x2, starting transfers between devices, swap(): return lax.all_to_all(x, axis, 0, 0, axis_index_groups=[group], tiled=True)  30.2 us
    all_to_all x2, blocking collectives, swap(): return lax.all_to_all(x, axis, 0, 0, axis_index_groups=[group], tiled=True)  23.1 us
    ppermute x1, starting transfers between devices, per_device(): lax.ppermute(given_half, 'row', [(i, i ^ 1) for i in range(NROW)])  5.46 us
    ppermute x4, starting transfers between devices, shifted(): lax.ppermute(shard, 'row', [(i, (i + by) % NROW) for i in range(NROW)])  3.2 us
    ppermute x4, waiting for transfers between devices, shifted(): lax.ppermute(shard, 'row', [(i, (i + by) % NROW) for i in range(NROW)])  2.89 us
    pallas_call x1, Pallas kernels, per_device(): call(back_own_kernel, (sds((FEAT, NODES_LOC), F32), sds((HLOC, NODES_LOC)...  2.48 us
    pallas_call x1, Pallas kernels, per_device(): call(back_near_kernel, (sds((FEAT, NODES_LOC), BF16),) * 2, [VM, HB] + [V...  2.42 us
    pallas_call x1, Pallas kernels, per_device(): call(own_kernel, (sds((RT, FEAT, TILE), F32), sds((2, 32, TILE, TILE), BF...  2.2 us
  transfers between devices with their start and end apart: 7, of which 3 were waited for; matrix products, arithmetic and copies ran while one was open for 0% of the time, Pallas kernels for 12%

profile of v3, /device:TPU:1, one launch (start us, length us, event | category | flops | bytes accessed | tf_op | source)
XLA Modules:
  0.0 82.7 jit_solution(16918714948747988123)
XLA Ops:
  0.6 0.0 copy-start
  0.6 0.0 copy-start.2
  0.7 0.0 copy-start.3
  0.7 0.0 copy-start.4
  0.7 0.0 copy-start.1
  0.7 2.1 %shard_map.146 = (bf16[32,2,128]{2,1,0:T(2,128)(2,1)}, s32[8,128]{1,0:T(8,128)S(1)}) custom-call(bf16[8,2048]{1,0:T(8,128)(2,1)} %feat.1, s32[1,32,32]{2,1,0:T(8,128)} %rows_hbm.1, s32[1,32]{1,0:T(1,128)} %counts_hbm.1), custom_call_target="tpu_custom_call" | custom-call | flops 33554432 | tf_op jit(solution)/shard_map/pallas_call | solution.py:541
  2.8 18.4 %all-to-all-start = ((bf16[32,2,128]{2,1,0:T(2,128)(2,1)}), bf16[32,2,128]{2,1,0:T(2,128)(2,1)S(1)}, u32[]{:S(2)}, u32[]{:S(2)}) async-start(bf16[32,2,128]{2,1,0:T(2,128)(2,1)} %get-tuple-element.24), calls=%async_computation | async-start | bytes 32768 | tf_op jit(solution)/shard_map/all_to_all | solution.py:519
  21.1 1.4 %collective-permute-start = (bf16[8,2048]{1,0:T(8,128)(2,1)}, bf16[8,2048]{1,0:T(8,128)(2,1)S(1)}, u32[]{:S(2)}, u32[]{:S(2)}) collective-permute-start(bf16[8,2048]{1,0:T(8,128)(2,1)} %feat.1), channel_id=1, source_target_pairs={{0,16},{16,32},{32,48},{48,64},{64,80},{80,96},{96,112},{112,128},... | collective-permute-start | bytes 98312 | tf_op jit(solution)/shard_map/ppermute | solution.py:513
  22.6 0.0 collective-permute-start.1
  22.6 2.2 %shard_map.147 = (f32[16,8,128]{2,1,0:T(8,128)S(1)}, bf16[2,32,128,128]{3,2,1,0:T(8,128)(2,1)S(1)}, bf16[1,32,128,128]{3,2,1,0:T(8,128)(2,1)S(1)}, s32[1,4,32]{2...) custom-call(bf16[8,2048]{1,0:T(8,128)(2,1)} %feat.1, bf16[1,4,32,128,128]{4,3,2,1,0:T(8,128)(2,1)} %tiles.5, ...), custom_call_target="tpu_custom_call" | custom-call | flops 16777216 | bytes 4194304 | tf_op jit(solution)/shard_map/pallas_call | solution.py:556
  24.8 0.0 collective-permute-done.prev
  24.8 1.3 %collective-permute-done.1.foll = bf16[8,2048]{1,0:T(8,128)(2,1)S(1)} collective-permute-done((bf16[8,2048]{1,0:T(8,128)(2,1)}, bf16[8,2048]{1,0:T(8,128)(2,1)S(1)}, u32[]{:S(2)}, u32[]{:S(2)}) %collective-permute-start.1) | collective-permute-done | bytes 32800 | tf_op jit(solution)/shard_map/ppermute | solution.py:513
  26.1 1.3 %shard_map.148.part = f32[16,8,128]{2,1,0:T(8,128)S(1)} custom-call(bf16[8,2048]{1,0:T(8,128)(2,1)S(1)} %collective-permute-done.prev, bf16[8,2048]{1,0:T(8,128)(2,1)S(1)} %collective-permute-done.1.foll, f32[16,8,128]{2,1,0:T(8,128)S(1)} %get-tuple-element.25.before, bf16[2,32,128,128]{3,2,1,0:T(8,128)(2,1)S(1)} %get-tuple-element.26.near, ...), custom_call_target="tpu_custom_call" | custom-call | flops 33554432 | bytes 2097152 | tf_op jit(solution)/shard_map/pallas_call | solution.py:581
  27.4 0.0 all-to-all-done.recv
  27.5 0.0 copy-done
  27.5 0.0 copy-done.2
  27.5 0.0 copy-done.3
  27.5 0.0 copy-done.4
  27.5 0.0 copy-done.1
  27.5 1.1 %shard_map.149 = bf16[16,80,128]{2,1,0:T(8,128)(2,1)S(1)} custom-call(bf16[32,2,128]{2,1,0:T(2,128)(2,1)S(1)} %all-to-all-done.recv, f32[16,8,128]{2,1,0:T(8,128)S(1)} %shard_map.148.part, bf16[8,2048]{1,0:T(8,128)(2,1)S(1)} %copy-done, bf16[16,2048]{1,0:T(8,128)(2,1)S(1)} %copy-done.1, bf16[16,128]{1,0:T(8,128)(2,1)S(1)} %bitcast.6, ...), custom_call_target="tpu_custom_call" | custom-call | flops 16777216 | bytes 1048576 | tf_op jit(solution)/shard_map/pallas_call | solution.py:590
  28.6 12.4 %all_to_all.20.r = bf16[16,80,128]{2,1,0:T(8,128)(2,1)S(1)} all-to-all(bf16[16,80,128]{2,1,0:T(8,128)(2,1)S(1)} %shard_map.149), channel_id=1, replica_groups={{11,12,13,14,15,0,1,2,3,4,5,6,7,8,9,10},{27,28,29,30,31,16,17,18,19,20,..., dimensions={0} | all-to-all | bytes 655360 | tf_op jit(solution)/shard_map/all_to_all | solution.py:519
  41.0 0.4 shard_map.150
  41.5 10.7 %all_to_all.21.r = bf16[16,80,128]{2,1,0:T(8,128)(2,1)S(1)} all-to-all(bf16[16,80,128]{2,1,0:T(8,128)(2,1)S(1)} %shard_map.150), channel_id=1, replica_groups={{11,12,13,14,15,0,1,2,3,4,5,6,7,8,9,10},{27,28,29,30,31,16,17,18,19,20,..., dimensions={0} | all-to-all | bytes 655360 | tf_op jit(solution)/shard_map/all_to_all | solution.py:519
  52.1 0.1 shard_map.153
  52.2 5.5 %collective-permute-start.2 = (f32[16,128]{1,0:T(8,128)S(1)}, f32[16,128]{1,0:T(8,128)S(1)}, u32[]{:S(2)}, u32[]{:S(2)}) collective-permute-start(f32[16,128]{1,0:T(8,128)S(1)} %get-tuple-element.34), channel_id=1, source_target_pairs={{0,16},{16,0},{32,48},{48,32},{64,80},{80,64},{96,112},{112,96},{1... | collective-permute-start | bytes 24584 | tf_op jit(solution)/shard_map/ppermute | solution.py:627
  57.7 1.4 %shard_map.152.far = bf16[32,2,128]{2,1,0:T(2,128)(2,1)S(1)} custom-call(bf16[16,80,128]{2,1,0:T(8,128)(2,1)S(1)} %all_to_all.21.r, bf16[1,32,128,128]{3,2,1,0:T(8,128)(2,1)S(1)} %get-tuple-element.30.kept, s32[1,4,32]{2,1,0:T(4,128)S(1)} %get-tuple-element.27.dst_in.dst_hbm, s32[1,4,32]{2,1,0:T(4,128)S(1)} %get-tuple-element.28.src_in.src_hbm, ...), custom_call_target="tpu_custom_call" | custom-call | flops 16777216 | bytes 1048576 | tf_op jit(solution)/shard_map/pallas_call | solution.py:628
  59.1 0.0 collective-permute-done.2.got
  59.1 0.7 shard_map.154
  59.8 11.8 %all-to-all-start.3 = ((bf16[160,4,128]{2,1,0:T(4,128)(2,1)}), bf16[160,4,128]{2,1,0:T(4,128)(2,1)S(1)}, u32[]{:S(2)}, u32[]{:S(2)}) async-start(bf16[160,4,128]{2,1,0:T(4,128)(2,1)} %shard_map.154), calls=%async_computation.3 | async-start | bytes 327680 | tf_op jit(solution)/shard_map/all_to_all | solution.py:519
  71.6 2.4 %shard_map.155 = (bf16[8,2048]{1,0:T(8,128)(2,1)S(1)}, bf16[8,2048]{1,0:T(8,128)(2,1)S(1)}) custom-call(bf16[16,80,128]{2,1,0:T(8,128)(2,1)S(1)} %all_to_all.21.r, bf16[1,4,32,128,128]{4,3,2,1,0:T(8,128)(2,1)} %tiles.5, s32[1,4,32]{2,1,0:T(4,128)S(1)} %get-tuple-element.27.dst_in.dst_hbm, s32[1,4,32]{2,1,0:T(4,128)S(1)} %get-tuple-element.28.src_in.src_hbm, ...), custom_call_target="tpu_custom_call" | custom-call | flops 33554432 | bytes 2097152 | tf_op jit(solution)/shard_map/pallas_call | solution.py:646
  74.0 0.4 collective-permute-start.3
  74.4 1.4 %collective-permute-start.4 = (bf16[8,2048]{1,0:T(8,128)(2,1)S(1)}, bf16[8,2048]{1,0:T(8,128)(2,1)S(1)}, u32[]{:S(2)}, u32[]{:S(2)}) collective-permute-start(bf16[8,2048]{1,0:T(8,128)(2,1)S(1)} %get-tuple-element.38), channel_id=1, source_target_pairs={{0,16},{16,32},{32,48},{48,64},{64,80},{80,96},{96,112},{112,128},... | collective-permute-start | bytes 98312 | tf_op jit(solution)/shard_map/ppermute | solution.py:513
  75.8 2.5 %shard_map.151 = (f32[8,2048]{1,0:T(8,128)S(1)}, bf16[16,2048]{1,0:T(8,128)(2,1)}) custom-call(bf16[16,80,128]{2,1,0:T(8,128)(2,1)S(1)} %all_to_all.21.r, bf16[1,4,32,128,128]{4,3,2,1,0:T(8,128)(2,1)} %tiles.5, s32[1,4,32]{2,1,0:T(4,128)S(1)} %get-tuple-element.27.dst_in.dst_hbm, s32[1,4,32]{2,1,0:T(4,128)S(1)} %get-tuple-element.28.src_in.src_hbm, ...), custom_call_target="tpu_custom_call" | custom-call | flops 16777216 | bytes 1048576 | tf_op jit(solution)/shard_map/pallas_call | solution.py:657
  78.3 1.6 %collective-permute-done.3.after = bf16[8,2048]{1,0:T(8,128)(2,1)S(1)} collective-permute-done((bf16[8,2048]{1,0:T(8,128)(2,1)S(1)}, bf16[8,2048]{1,0:T(8,128)(2,1)S(1)}, u32[]{:S(2)}, u32[]{:S(2)}) %collective-permute-start.3) | collective-permute-done | bytes 32800 | tf_op jit(solution)/shard_map/ppermute | solution.py:513
  79.9 0.0 collective-permute-done.4.before
  79.9 1.8 %all-to-all-done.3.recv = bf16[160,4,128]{2,1,0:T(4,128)(2,1)S(1)} async-done(((bf16[160,4,128]{2,1,0:T(4,128)(2,1)}), bf16[160,4,128]{2,1,0:T(4,128)(2,1)S(1)}, u32[]{:S(2)}, u32[]{:S(2)}) %all-to-all-start.3) | async-done | bytes 163872 | tf_op jit(solution)/shard_map/all_to_all | solution.py:519
  81.6 1.1 %shard_map.156 = (bf16[8,2048]{1,0:T(8,128)(2,1)}, f32[16,128]{1,0:T(8,128)}, f32[16,128]{1,0:T(8,128)}, f32[1,16]{1,0:T(1,128)}) custom-call(bf16[160,4,128]{2,1,0:T(4,128)(2,1)S(1)} %all-to-all-done.3.recv, s32[8,128]{1,0:T(8,128)S(1)} %get-tuple-element.35.index, f32[8,2048]{1,0:T(8,128)S(1)} %get-tuple-element.36.own, ...), custom_call_target="tpu_custom_call" | custom-call | tf_op jit(solution)/shard_map/pallas_call | solution.py:666
Async XLA Ops:
  0.6 26.8 %copy-start = (bf16[8,2048]{1,0:T(8,128)(2,1)S(1)}, bf16[8,2048]{1,0:T(8,128)(2,1)}, u32[]{:S(2)}) copy-start(bf16[8,2048]{1,0:T(8,128)(2,1)} %feat.1) | copy-start | bytes 98308
  0.6 26.8 %copy-start.2 = (bf16[128,16]{0,1:T(8,128)(2,1)S(1)}, bf16[128,16]{0,1:T(8,128)(2,1)}, u32[]{:S(2)}) copy-start(bf16[128,16]{0,1:T(8,128)(2,1)} %param.18) | copy-start | bytes 12292
  0.7 26.8 %copy-start.3 = (bf16[128,16]{0,1:T(8,128)(2,1)S(1)}, bf16[128,16]{0,1:T(8,128)(2,1)}, u32[]{:S(2)}) copy-start(bf16[128,16]{0,1:T(8,128)(2,1)} %param.19) | copy-start | bytes 12292
  0.7 26.8 %copy-start.4 = (f32[16]{0:T(128)S(1)}, f32[16]{0:T(128)}, u32[]{:S(2)}) copy-start(f32[16]{0:T(128)} %param.20) | copy-start | bytes 196
  0.7 26.8 %copy-start.1 = (bf16[16,2048]{1,0:T(8,128)(2,1)S(1)}, bf16[16,2048]{1,0:T(8,128)(2,1)}, u32[]{:S(2)}) copy-start(bf16[16,2048]{1,0:T(8,128)(2,1)} %cot.1) | copy-start | bytes 196612
  2.8 24.7 %all-to-all-start = ((bf16[32,2,128]{2,1,0:T(2,128)(2,1)}), bf16[32,2,128]{2,1,0:T(2,128)(2,1)S(1)}, u32[]{:S(2)}, u32[]{:S(2)}) async-start(bf16[32,2,128]{2,1,0:T(2,128)(2,1)} %get-tuple-element.24), calls=%async_computation | async-start | bytes 32768 | tf_op jit(solution)/shard_map/all_to_all | solution.py:519
  21.1 3.7 %collective-permute-start = (bf16[8,2048]{1,0:T(8,128)(2,1)}, bf16[8,2048]{1,0:T(8,128)(2,1)S(1)}, u32[]{:S(2)}, u32[]{:S(2)}) collective-permute-start(bf16[8,2048]{1,0:T(8,128)(2,1)} %feat.1), channel_id=1, source_target_pairs={{0,16},{16,32},{32,48},{48,64},{64,80},{80,96},{96,112},{112,128},... | collective-permute-start | bytes 98312 | tf_op jit(solution)/shard_map/ppermute | solution.py:513
  22.6 3.6 %collective-permute-start.1 = (bf16[8,2048]{1,0:T(8,128)(2,1)}, bf16[8,2048]{1,0:T(8,128)(2,1)S(1)}, u32[]{:S(2)}, u32[]{:S(2)}) collective-permute-start(bf16[8,2048]{1,0:T(8,128)(2,1)} %feat.1), channel_id=1, source_target_pairs={{0,496},{16,0},{32,16},{48,32},{64,48},{80,64},{96,80},{112,96},{1... | collective-permute-start | bytes 98312 | tf_op jit(solution)/shard_map/ppermute | solution.py:513
  52.2 6.9 %collective-permute-start.2 = (f32[16,128]{1,0:T(8,128)S(1)}, f32[16,128]{1,0:T(8,128)S(1)}, u32[]{:S(2)}, u32[]{:S(2)}) collective-permute-start(f32[16,128]{1,0:T(8,128)S(1)} %get-tuple-element.34), channel_id=1, source_target_pairs={{0,16},{16,0},{32,48},{48,32},{64,80},{80,64},{96,112},{112,96},{1... | collective-permute-start | bytes 24584 | tf_op jit(solution)/shard_map/ppermute | solution.py:627
  59.8 21.8 %all-to-all-start.3 = ((bf16[160,4,128]{2,1,0:T(4,128)(2,1)}), bf16[160,4,128]{2,1,0:T(4,128)(2,1)S(1)}, u32[]{:S(2)}, u32[]{:S(2)}) async-start(bf16[160,4,128]{2,1,0:T(4,128)(2,1)} %shard_map.154), calls=%async_computation.3 | async-start | bytes 327680 | tf_op jit(solution)/shard_map/all_to_all | solution.py:519
  74.0 5.8 %collective-permute-start.3 = (bf16[8,2048]{1,0:T(8,128)(2,1)S(1)}, bf16[8,2048]{1,0:T(8,128)(2,1)S(1)}, u32[]{:S(2)}, u32[]{:S(2)}) collective-permute-start(bf16[8,2048]{1,0:T(8,128)(2,1)S(1)} %get-tuple-element.37), channel_id=1, source_target_pairs={{0,496},{16,0},{32,16},{48,32},{64,48},{80,64},{96,80},{112,96},{1... | collective-permute-start | bytes 98312 | tf_op jit(solution)/shard_map/ppermute | solution.py:513
  74.4 5.4 %collective-permute-start.4 = (bf16[8,2048]{1,0:T(8,128)(2,1)S(1)}, bf16[8,2048]{1,0:T(8,128)(2,1)S(1)}, u32[]{:S(2)}, u32[]{:S(2)}) collective-permute-start(bf16[8,2048]{1,0:T(8,128)(2,1)S(1)} %get-tuple-element.38), channel_id=1, source_target_pairs={{0,16},{16,32},{32,48},{48,64},{64,80},{80,96},{96,112},{112,128},... | collective-permute-start | bytes 98312 | tf_op jit(solution)/shard_map/ppermute | solution.py:513

commit v4 on v3

--- a/solution.py
+++ b/solution.py
@@ -23,8 +23,8 @@
 RET = 5
 FWD_ROWS = 80
 BWD_ROWS = 80
-FIRST_ROW = 20
-FIRST_COL = 11
+ROW_OUT, ROW_BACK = 20, 16
+COL_OUT, COL_BACK = 11, 10
 F32, BF16 = jnp.float32, jnp.bfloat16
 NT = (((1,), (1,)), ((), ()))
 TN = (((0,), (0,)), ((), ()))
@@ -44,12 +44,12 @@
     return lax.dot_general(a, b, dims, preferred_element_type=F32)
 
 
-def row_at(p):
-    return (p - FIRST_ROW) % NROW
-
-
-def col_at(c):
-    return (c - FIRST_COL) % NCOL
+def row_at(p, first):
+    return (p - first) % NROW
+
+
+def col_at(c, first):
+    return (c - first) % NCOL
 
 
 def iota(shape, dim):
@@ -146,8 +146,16 @@
     return out
 
 
-def gather_kernel(feat_hbm, rows_hbm, counts_hbm, out, index, feat, rows, counts, scr, sems):
-    wait_all(start_all((rows_hbm, counts_hbm, feat_hbm), (rows, counts, feat), sems))
+def gather_kernel(
+    feat_hbm, rows_hbm, counts_hbm, dst_hbm, src_hbm, count_hbm,
+    out, index, feat, dst_out, src_out, count_out, rows, counts, scr, sems,
+):
+    copies = start_all(
+        (rows_hbm, counts_hbm, feat_hbm, dst_hbm, src_hbm, count_hbm),
+        (rows, counts, feat, dst_out, src_out, count_out),
+        sems,
+    )
+    wait_all(copies[:3])
     cnt = jnp.broadcast_to(counts[...], (NROW, NROW))
     cnt = jnp.where(iota((NROW, NROW), 0) == iota((NROW, NROW), 1), cnt, 0)
     cnt = jnp.sum(cnt, axis=1, keepdims=True)
@@ -173,7 +181,8 @@
         groups.append(g)
     rows2 = compact(groups).astype(BF16)
     for p in range(NROW):
-        out[row_at(p)] = rows2[2 * p : 2 * p + 2]
+        out[row_at(p, ROW_OUT)] = rows2[2 * p : 2 * p + 2]
+    wait_all(copies[3:])
 
 
 def store_source(lo, hi, k, x):
@@ -209,21 +218,16 @@
 
 
 def own_kernel(
-    feat_hbm, tiles, dst_hbm, src_hbm, count_hbm, part, near, far, dst_out, src_out, count_out,
-    feat, dst, src, count, held, lo, hi, sems, own_sems, near_sems, far_sems,
+    feat, dst_in, src_in, count_in, tiles, part, near, far,
+    dst, src, count, held, lo, hi, sems, own_sems, near_sems, far_sems,
 ):
-    copies = start_all(
-        (count_hbm, dst_hbm, src_hbm, feat_hbm, dst_hbm, src_hbm, count_hbm),
-        (count, dst, src, feat, dst_out, src_out, count_out),
-        sems,
-    )
+    copies = start_all((count_in, dst_in, src_in), (count, dst, src), sems)
     work = ((held, [0], own_sems), (near, [1, 2], near_sems), (far, [3], far_sems))
     for place, groups, place_sems in work:
         start_chunks(tiles, place, groups, count, place_sems, 0, 1)
-    copies[0].wait()
+    wait_all(copies)
     for place, groups, place_sems in work:
         start_chunks(tiles, place, groups, count, place_sems, 1, NCHUNK)
-    wait_all(copies[1:4])
     for k in range(RT):
         store_source(lo, hi, k, tile_of(feat, k).astype(F32))
     zero_source(lo, hi, RT)
@@ -244,7 +248,6 @@
                 return carry
 
             lax.fori_loop(0, steps(count[0, g]), arrived, 0)
-    wait_all(copies[4:])
 
 
 def near_kernel(prev, foll, before, near, dst_in, src_in, count_in, part, dst, src, count, lo, hi, sems):
@@ -273,7 +276,7 @@
     lo, hi, acc, sems,
 ):
     copies = start_all((count_hbm, dst_hbm, src_hbm), (count, dst, src), sems)
-    rows = jnp.concatenate([recv[row_at(p)].astype(F32) for p in range(NROW)], axis=0).astype(BF16)
+    rows = jnp.concatenate([recv[row_at(p, ROW_OUT)].astype(F32) for p in range(NROW)], axis=0).astype(BF16)
     for k, x in enumerate(spread_out(rows)):
         store_source(lo, hi, k, x)
     zero_source(lo, hi, NB)
@@ -299,7 +302,7 @@
     block = block.astype(BF16)
     for d in range(RT):
         both = jnp.concatenate([acc[d], tile_of(feat, d).astype(F32)], axis=0)
-        at = col_at(d)
+        at = col_at(d, COL_OUT)
         buf[at, 0:16] = both.astype(BF16)
         buf[at, 16:32] = tile_of(cot, d)
         buf[at, 32:48] = wst[...]
@@ -308,12 +311,12 @@
 
 
 def dense_kernel(r, out):
-    wst = jnp.concatenate([r[col_at(c), 32:48] for c in range(NCOL)], axis=0)
-    wnt = jnp.concatenate([r[col_at(c), 48:64] for c in range(NCOL)], axis=0)
-    cot = jnp.concatenate([r[col_at(c), 16:32] for c in range(NCOL)], axis=0).astype(F32)
-    bias = jnp.concatenate([r[col_at(c), 64:80] for c in range(NCOL)], axis=0).astype(F32)
+    wst = jnp.concatenate([r[col_at(c, COL_OUT), 32:48] for c in range(NCOL)], axis=0)
+    wnt = jnp.concatenate([r[col_at(c, COL_OUT), 48:64] for c in range(NCOL)], axis=0)
+    cot = jnp.concatenate([r[col_at(c, COL_OUT), 16:32] for c in range(NCOL)], axis=0).astype(F32)
+    bias = jnp.concatenate([r[col_at(c, COL_OUT), 64:80] for c in range(NCOL)], axis=0).astype(F32)
     bias = bias[:, 0:1] + bias[:, 1:2] + bias[:, 2:3]
-    heads = [r[col_at(c), 0:16].astype(F32) for c in range(NCOL)]
+    heads = [r[col_at(c, COL_OUT), 0:16].astype(F32) for c in range(NCOL)]
     agg = jnp.concatenate([h[:FEAT] for h in heads], axis=0).astype(BF16)
     feats = jnp.concatenate([h[FEAT:] for h in heads], axis=0).astype(BF16)
     pre = dot(wst, feats) + dot(wnt, agg) + bias
@@ -337,11 +340,12 @@
         bsum = jnp.where((lane >= BMAX) & (lane < BMAX + HLOC), bsum, 0.0)
         bhi = bsum.astype(BF16).astype(F32)
         bsum = jnp.where(sub == 0, bhi, jnp.where(sub == 1, bsum - bhi, 0.0))
-        out[col_at(c), 0:16] = jnp.concatenate([agg_grad[f], own_hi[f]], axis=0).astype(BF16)
-        out[col_at(c), 16:32] = hidden[h]
-        out[col_at(c), 32:48] = gs[h]
-        out[col_at(c), 48:64] = gn[h]
-        out[col_at(c), 64:80] = jnp.concatenate([own_lo[f], bsum], axis=0).astype(BF16)
+        at = col_at(c, COL_BACK)
+        out[at, 0:16] = jnp.concatenate([agg_grad[f], own_hi[f]], axis=0).astype(BF16)
+        out[at, 16:32] = hidden[h]
+        out[at, 32:48] = gs[h]
+        out[at, 48:64] = gn[h]
+        out[at, 64:80] = jnp.concatenate([own_lo[f], bsum], axis=0).astype(BF16)
 
 
 def weights_kernel(r, kept, given, bsum):
@@ -378,7 +382,7 @@
 
 def load_grads(r, lo, hi):
     for d in range(RT):
-        store_source(lo, hi, d, r[col_at(d), 0:16].astype(F32)[:FEAT])
+        store_source(lo, hi, d, r[col_at(d, COL_BACK), 0:16].astype(F32)[:FEAT])
     zero_source(lo, hi, RT)
 
 
@@ -403,7 +407,7 @@
     mine = (kept[...] + got[...]).astype(BF16)
     extra = jnp.broadcast_to(bsum[...], (2, TILE))
     for p in range(NROW):
-        at = RET * row_at(p)
+        at = RET * row_at(p, ROW_BACK)
         out[at] = jnp.concatenate([far[p].astype(F32), extra], axis=0).astype(BF16)
         for i in range(4):
             out[at + 1 + i] = mine[4 * i : 4 * i + 4]
@@ -446,7 +450,7 @@
     acc = scratch[6]
     for k in range(RT):
         cols = slice(k * TILE, (k + 1) * TILE)
-        at = col_at(k)
+        at = col_at(k, COL_BACK)
         tail = r[at, 64:80].astype(F32)
         own[:, cols] = acc[k] + r[at, 0:16].astype(F32)[FEAT:] + tail[:FEAT]
         hidden[:, cols] = r[at, 16:32]
@@ -455,7 +459,7 @@
 def final_kernel(recv, index, own, after, before, grad, gs, gn, gb, *, scale):
     place = iota((TILE, TILE), 0)
     lefts, rights = [], []
-    heads = [recv[RET * row_at(p)].astype(F32) for p in range(NROW)]
+    heads = [recv[RET * row_at(p, ROW_BACK)].astype(F32) for p in range(NROW)]
     rows = jnp.concatenate([h[:2] for h in heads], axis=0).astype(BF16)
     bsum = heads[0]
     for h in heads[1:]:
@@ -465,9 +469,9 @@
     for half in range(2):
         quarters = []
         for i in range(4):
-            q = recv[RET * row_at(half) + 1 + i].astype(F32)
+            q = recv[RET * row_at(half, ROW_BACK) + 1 + i].astype(F32)
             for p in range(half + 2, NROW, 2):
-                q = q + recv[RET * row_at(p) + 1 + i].astype(F32)
+                q = q + recv[RET * row_at(p, ROW_BACK) + 1 + i].astype(F32)
             quarters.append(q)
         halves.append(jnp.concatenate(quarters, axis=0) * scale)
     for k, x in enumerate(spread_out(rows)):
@@ -538,46 +542,48 @@
     tiles = in_hbm(tile_values)
     previous = shifted(features, 1)
     following = shifted(features, -1)
-    outgoing, index = call(
+    outgoing, index, feat, *here = call(
         gather_kernel,
-        (sds((NROW, 2, TILE), BF16), sds((NB, TILE), jnp.int32)),
-        [HB] * 3,
-        (VM, VM),
+        (
+            sds((NROW, 2, TILE), BF16),
+            sds((NB, TILE), jnp.int32),
+            sds((FEAT, NODES_LOC), BF16),
+            sds((1, 4, 32), jnp.int32),
+            sds((1, 4, 32), jnp.int32),
+            sds((1, 4), jnp.int32),
+        ),
+        [HB] * 6,
+        (VM,) * 6,
         [
-            pltpu.VMEM((FEAT, NODES_LOC), BF16),
             pltpu.VMEM((1, NROW, BMAX), jnp.int32),
             pltpu.VMEM((1, NROW), jnp.int32),
             pltpu.VMEM((NROW, TILE), jnp.int32),
-            pltpu.SemaphoreType.DMA((3,)),
+            pltpu.SemaphoreType.DMA((6,)),
         ],
         flops=2 * TILE * TILE * NROW * BMAX,
-    )(in_hbm(features), in_hbm(send_rows), in_hbm(send_count))
-    incoming = swap(outgoing, "row", FIRST_ROW)
-    part, near, kept, *here = call(
+    )(in_hbm(features), in_hbm(send_rows), in_hbm(send_count), *tables)
+    incoming = swap(outgoing, "row", ROW_OUT)
+    part, near, kept = call(
         own_kernel,
         (
             sds((RT, FEAT, TILE), F32),
             sds((2, 32, TILE, TILE), BF16),
             sds((1, 32, TILE, TILE), BF16),
-            sds((1, 4, 32), jnp.int32),
-            sds((1, 4, 32), jnp.int32),
-            sds((1, 4), jnp.int32),
         ),
-        [HB] * 5,
-        (VM,) * 6,
+        [VM] * 4 + [HB],
+        (VM,) * 3,
         [
-            pltpu.VMEM((FEAT, NODES_LOC), BF16),
             *TABLES,
             held(1),
             *sources(RT),
-            pltpu.SemaphoreType.DMA((7,)),
+            pltpu.SemaphoreType.DMA((3,)),
             pltpu.SemaphoreType.DMA((1, NCHUNK)),
             pltpu.SemaphoreType.DMA((2, NCHUNK)),
             pltpu.SemaphoreType.DMA((1, NCHUNK)),
         ],
         flops=2 * 16 * TILE * TILE * 32,
         nbytes=4 << 20,
-    )(in_hbm(features), tiles, *tables)
+    )(feat, *here, tiles)
     part = call(
         near_kernel,
         sds((RT, FEAT, TILE), F32),
@@ -603,7 +609,7 @@
     )(
         incoming,
         part,
-        features,
+        feat,
         cotangent,
         w_self.T,
         w_neigh.T,
@@ -611,7 +617,7 @@
         kept,
         *here,
     )
-    by_node = swap(buf, "col", FIRST_COL)
+    by_node = swap(buf, "col", COL_OUT)
     sent = call(
         dense_kernel,
         sds((NCOL, BWD_ROWS, TILE), BF16),
@@ -619,7 +625,7 @@
         VM,
         flops=2 * D_IN * HID * TILE * 6,
     )(by_node)
-    back = swap(sent, "col", FIRST_COL)
+    back = swap(sent, "col", COL_BACK)
     half = sds((HLOC, TILE), F32)
     kept_half, given_half, bsum = call(
         weights_kernel, (half, half, sds((1, TILE), F32)), [VM], (VM, VM, VM)
@@ -642,7 +648,7 @@
     returning = call(pack_kernel, sds((NROW * RET, 4, TILE), BF16), [VM] * 4, VM)(
         far, bsum, kept_half, got_half
     )
-    returned = swap(returning, "row", FIRST_ROW)
+    returned = swap(returning, "row", ROW_BACK)
     to_previous, to_following = call(
         back_near_kernel,
         (sds((FEAT, NODES_LOC), BF16),) * 2,

time: 83.2 us -> 81.5 us (0.980)
  waiting for transfers between devices: 4.68 us -> 2.49 us
  starting transfers between devices: 38.8 us -> 40.3 us
  blocking collectives: 23.1 us -> 22.2 us
    all_to_all x2, waiting for transfers between devices: 1.79 us -> 0.01 us  [swap(): return lax.all_to_all(x, axis, 0, 0, axis_index_groups=[group], tiled=True)]
    all_to_all x2, starting transfers between devices: 30.2 us -> 31 us  [swap(): return lax.all_to_all(x, axis, 0, 0, axis_index_groups=[group], tiled=True)]
  transfers between devices with their start and end apart: 7 -> 7, of which waited for: 3 -> 2; matrix products, arithmetic and copies ran while one was open for 0% -> 0% of each run, Pallas kernels for 12% -> 12%
where the time goes in v4:
time: 81.5 us; the launch traced here: 81 us
  starting transfers between devices  40.3 us (49%)
  blocking collectives  22.2 us (27%)
  Pallas kernels  15.2 us (19%)
  waiting for transfers between devices  2.49 us (3%)
    all_to_all x2, starting transfers between devices, swap(): return lax.all_to_all(x, axis, 0, 0, axis_index_groups=[group], tiled=True)  31 us
    all_to_all x2, blocking collectives, swap(): return lax.all_to_all(x, axis, 0, 0, axis_index_groups=[group], tiled=True)  22.2 us
    ppermute x1, starting transfers between devices, per_device(): lax.ppermute(given_half, 'row', [(i, i ^ 1) for i in range(NROW)])  5.69 us
    ppermute x4, starting transfers between devices, shifted(): lax.ppermute(shard, 'row', [(i, (i + by) % NROW) for i in range(NROW)])  3.52 us
    pallas_call x1, Pallas kernels, per_device(): call(back_own_kernel, (sds((FEAT, NODES_LOC), F32), sds((HLOC, NODES_LOC)...  2.73 us
    ppermute x4, waiting for transfers between devices, shifted(): lax.ppermute(shard, 'row', [(i, (i + by) % NROW) for i in range(NROW)])  2.48 us
    pallas_call x1, Pallas kernels, per_device(): call(own_kernel, (sds((RT, FEAT, TILE), F32), sds((2, 32, TILE, TILE), BF...  2.25 us
    pallas_call x1, Pallas kernels, per_device(): call(back_near_kernel, (sds((FEAT, NODES_LOC), BF16),) * 2, [VM, HB] + [V...  2.16 us
  transfers between devices with their start and end apart: 7, of which 2 were waited for; matrix products, arithmetic and copies ran while one was open for 0% of the time, Pallas kernels for 12%

profile of v4, /device:TPU:1, one launch (start us, length us, event | category | flops | bytes accessed | tf_op | source)
XLA Modules:
  0.0 81.0 jit_solution(8876874575182572858)
XLA Ops:
  0.6 0.0 copy-start
  0.6 0.0 copy-start.3
  0.7 0.0 copy-start.2
  0.7 0.0 copy-start.1
  0.7 2.1 %shard_map.146 = (bf16[32,2,128]{2,1,0:T(2,128)(2,1)}, s32[8,128]{1,0:T(8,128)S(1)}, bf16[8,2048]{1,0:T(8,128)(2,1)S(1)}, s32[1,4,32]{2,1,0:T(4,128)S(1)}, s32[1,4,32]{2,1,0:T(4,128)S(1)}, /*index=5*/s32[1,4]{1,0:T(1,128)S(1)}) custom-call(bf16[8,2048]{1,0:T(8,128)(2,1)} %feat_hbm.1, s32[1,32,32]{2,1,0:T(8,128)} %rows_hbm.1, s32[1,32]{1,0:T(1,128)} %counts_hbm.1, ...), custom_call_target="tpu_custom_call" | custom-call | flops 33554432 | tf_op jit(solution)/shard_map/pallas_call | solution.py:545
  2.8 18.4 %all-to-all-start = ((bf16[32,2,128]{2,1,0:T(2,128)(2,1)}), bf16[32,2,128]{2,1,0:T(2,128)(2,1)S(1)}, u32[]{:S(2)}, u32[]{:S(2)}) async-start(bf16[32,2,128]{2,1,0:T(2,128)(2,1)} %get-tuple-element.25), calls=%async_computation | async-start | bytes 32768 | tf_op jit(solution)/shard_map/all_to_all | solution.py:523
  21.1 0.4 collective-permute-start.1
  21.5 1.4 %collective-permute-start = (bf16[8,2048]{1,0:T(8,128)(2,1)}, bf16[8,2048]{1,0:T(8,128)(2,1)S(1)}, u32[]{:S(2)}, u32[]{:S(2)}) collective-permute-start(bf16[8,2048]{1,0:T(8,128)(2,1)} %feat_hbm.1), channel_id=1, source_target_pairs={{0,16},{16,32},{32,48},{48,64},{64,80},{80,96},{96,112},{112,128},... | collective-permute-start | bytes 98312 | tf_op jit(solution)/shard_map/ppermute | solution.py:517
  22.9 2.3 %shard_map.147 = (f32[16,8,128]{2,1,0:T(8,128)S(1)}, bf16[2,32,128,128]{3,2,1,0:T(8,128)(2,1)S(1)}, bf16[1,32,128,128]{3,2,1,0:T(8,128)(2,1)S(1)}) custom-call(bf16[8,2048]{1,0:T(8,128)(2,1)S(1)} %get-tuple-element.26.feat, s32[1,4,32]{2,1,0:T(4,128)S(1)} %get-tuple-element.27.dst_in.dst_hbm, s32[1,4,32]{2,1,0:T(4,128)S(1)} %get-tuple-element.28.src_in.src_hbm, ...), custom_call_target="tpu_custom_call" | custom-call | flops 16777216 | bytes 4194304 | tf_op jit(solution)/shard_map/pallas_call | solution.py:566
  25.2 0.1 collective-permute-done.1.foll
  25.3 0.0 collective-permute-done.prev
  25.3 1.1 %shard_map.148.part = f32[16,8,128]{2,1,0:T(8,128)S(1)} custom-call(bf16[8,2048]{1,0:T(8,128)(2,1)S(1)} %collective-permute-done.prev, bf16[8,2048]{1,0:T(8,128)(2,1)S(1)} %collective-permute-done.1.foll, f32[16,8,128]{2,1,0:T(8,128)S(1)} %get-tuple-element.30.before, bf16[2,32,128,128]{3,2,1,0:T(8,128)(2,1)S(1)} %get-tuple-element.31.near, ...), custom_call_target="tpu_custom_call" | custom-call | flops 33554432 | bytes 2097152 | tf_op jit(solution)/shard_map/pallas_call | solution.py:587
  26.4 0.0 all-to-all-done.recv
  26.5 0.0 copy-done
  26.5 0.0 copy-done.3
  26.5 0.0 copy-done.2
  26.5 0.0 copy-done.1
  26.5 1.1 %shard_map.149 = bf16[16,80,128]{2,1,0:T(8,128)(2,1)S(1)} custom-call(bf16[32,2,128]{2,1,0:T(2,128)(2,1)S(1)} %all-to-all-done.recv, f32[16,8,128]{2,1,0:T(8,128)S(1)} %shard_map.148.part, bf16[8,2048]{1,0:T(8,128)(2,1)S(1)} %get-tuple-element.26.feat, bf16[16,2048]{1,0:T(8,128)(2,1)S(1)} %copy-done, bf16[16,128]{1,0:T(8,128)(2,1)S(1)} %bitcast.6, ...), custom_call_target="tpu_custom_call" | custom-call | flops 16777216 | bytes 1048576 | tf_op jit(solution)/shard_map/pallas_call | solution.py:596
  27.6 12.2 %all_to_all.20.r = bf16[16,80,128]{2,1,0:T(8,128)(2,1)S(1)} all-to-all(bf16[16,80,128]{2,1,0:T(8,128)(2,1)S(1)} %shard_map.149), channel_id=1, replica_groups={{11,12,13,14,15,0,1,2,3,4,5,6,7,8,9,10},{27,28,29,30,31,16,17,18,19,20,..., dimensions={0} | all-to-all | bytes 655360 | tf_op jit(solution)/shard_map/all_to_all | solution.py:523
  39.8 0.4 shard_map.150
  40.3 10.0 %all_to_all.21.r = bf16[16,80,128]{2,1,0:T(8,128)(2,1)S(1)} all-to-all(bf16[16,80,128]{2,1,0:T(8,128)(2,1)S(1)} %shard_map.150), channel_id=1, replica_groups={{10,11,12,13,14,15,0,1,2,3,4,5,6,7,8,9},{26,27,28,29,30,31,16,17,18,19,..., dimensions={0} | all-to-all | bytes 655360 | tf_op jit(solution)/shard_map/all_to_all | solution.py:523
  50.3 0.1 shard_map.153
  50.4 5.7 %collective-permute-start.2 = (f32[16,128]{1,0:T(8,128)S(1)}, f32[16,128]{1,0:T(8,128)S(1)}, u32[]{:S(2)}, u32[]{:S(2)}) collective-permute-start(f32[16,128]{1,0:T(8,128)S(1)} %get-tuple-element.36), channel_id=1, source_target_pairs={{0,16},{16,0},{32,48},{48,32},{64,80},{80,64},{96,112},{112,96},{1... | collective-permute-start | bytes 24584 | tf_op jit(solution)/shard_map/ppermute | solution.py:633
  56.1 1.4 %shard_map.152.far = bf16[32,2,128]{2,1,0:T(2,128)(2,1)S(1)} custom-call(bf16[16,80,128]{2,1,0:T(8,128)(2,1)S(1)} %all_to_all.21.r, bf16[1,32,128,128]{3,2,1,0:T(8,128)(2,1)S(1)} %get-tuple-element.32.kept, s32[1,4,32]{2,1,0:T(4,128)S(1)} %get-tuple-element.27.dst_in.dst_hbm, s32[1,4,32]{2,1,0:T(4,128)S(1)} %get-tuple-element.28.src_in.src_hbm, ...), custom_call_target="tpu_custom_call" | custom-call | flops 16777216 | bytes 1048576 | tf_op jit(solution)/shard_map/pallas_call | solution.py:634
  57.5 0.0 collective-permute-done.2.got
  57.5 0.7 shard_map.154
  58.2 12.7 %all-to-all-start.3 = ((bf16[160,4,128]{2,1,0:T(4,128)(2,1)}), bf16[160,4,128]{2,1,0:T(4,128)(2,1)S(1)}, u32[]{:S(2)}, u32[]{:S(2)}) async-start(bf16[160,4,128]{2,1,0:T(4,128)(2,1)} %shard_map.154), calls=%async_computation.3 | async-start | bytes 327680 | tf_op jit(solution)/shard_map/all_to_all | solution.py:523
  70.9 2.2 %shard_map.155 = (bf16[8,2048]{1,0:T(8,128)(2,1)S(1)}, bf16[8,2048]{1,0:T(8,128)(2,1)S(1)}) custom-call(bf16[16,80,128]{2,1,0:T(8,128)(2,1)S(1)} %all_to_all.21.r, bf16[1,4,32,128,128]{4,3,2,1,0:T(8,128)(2,1)} %tiles.5, s32[1,4,32]{2,1,0:T(4,128)S(1)} %get-tuple-element.27.dst_in.dst_hbm, s32[1,4,32]{2,1,0:T(4,128)S(1)} %get-tuple-element.28.src_in.src_hbm, ...), custom_call_target="tpu_custom_call" | custom-call | flops 33554432 | bytes 2097152 | tf_op jit(solution)/shard_map/pallas_call | solution.py:652
  73.1 0.1 collective-permute-start.3
  73.2 1.6 %collective-permute-start.4 = (bf16[8,2048]{1,0:T(8,128)(2,1)S(1)}, bf16[8,2048]{1,0:T(8,128)(2,1)S(1)}, u32[]{:S(2)}, u32[]{:S(2)}) collective-permute-start(bf16[8,2048]{1,0:T(8,128)(2,1)S(1)} %get-tuple-element.40), channel_id=1, source_target_pairs={{0,16},{16,32},{32,48},{48,64},{64,80},{80,96},{96,112},{112,128},... | collective-permute-start | bytes 98312 | tf_op jit(solution)/shard_map/ppermute | solution.py:517
  74.8 2.7 %shard_map.151 = (f32[8,2048]{1,0:T(8,128)S(1)}, bf16[16,2048]{1,0:T(8,128)(2,1)}) custom-call(bf16[16,80,128]{2,1,0:T(8,128)(2,1)S(1)} %all_to_all.21.r, bf16[1,4,32,128,128]{4,3,2,1,0:T(8,128)(2,1)} %tiles.5, s32[1,4,32]{2,1,0:T(4,128)S(1)} %get-tuple-element.27.dst_in.dst_hbm, s32[1,4,32]{2,1,0:T(4,128)S(1)} %get-tuple-element.28.src_in.src_hbm, ...), custom_call_target="tpu_custom_call" | custom-call | flops 16777216 | bytes 1048576 | tf_op jit(solution)/shard_map/pallas_call | solution.py:663
  77.6 2.3 %collective-permute-done.3.after = bf16[8,2048]{1,0:T(8,128)(2,1)S(1)} collective-permute-done((bf16[8,2048]{1,0:T(8,128)(2,1)S(1)}, bf16[8,2048]{1,0:T(8,128)(2,1)S(1)}, u32[]{:S(2)}, u32[]{:S(2)}) %collective-permute-start.3) | collective-permute-done | bytes 32800 | tf_op jit(solution)/shard_map/ppermute | solution.py:517
  79.9 0.0 collective-permute-done.4.before
  79.9 0.0 all-to-all-done.3.recv
  79.9 1.1 %shard_map.156 = (bf16[8,2048]{1,0:T(8,128)(2,1)}, f32[16,128]{1,0:T(8,128)}, f32[16,128]{1,0:T(8,128)}, f32[1,16]{1,0:T(1,128)}) custom-call(bf16[160,4,128]{2,1,0:T(4,128)(2,1)S(1)} %all-to-all-done.3.recv, s32[8,128]{1,0:T(8,128)S(1)} %get-tuple-element.37.index, f32[8,2048]{1,0:T(8,128)S(1)} %get-tuple-element.38.own, ...), custom_call_target="tpu_custom_call" | custom-call | tf_op jit(solution)/shard_map/pallas_call | solution.py:672
Async XLA Ops:
  0.6 25.8 %copy-start = (bf16[16,2048]{1,0:T(8,128)(2,1)S(1)}, bf16[16,2048]{1,0:T(8,128)(2,1)}, u32[]{:S(2)}) copy-start(bf16[16,2048]{1,0:T(8,128)(2,1)} %cot.1) | copy-start | bytes 196612
  0.6 25.8 %copy-start.3 = (f32[16]{0:T(128)S(1)}, f32[16]{0:T(128)}, u32[]{:S(2)}) copy-start(f32[16]{0:T(128)} %param.20) | copy-start | bytes 196
  0.7 25.8 %copy-start.2 = (bf16[128,16]{0,1:T(8,128)(2,1)S(1)}, bf16[128,16]{0,1:T(8,128)(2,1)}, u32[]{:S(2)}) copy-start(bf16[128,16]{0,1:T(8,128)(2,1)} %param.19) | copy-start | bytes 12292
  0.7 25.8 %copy-start.1 = (bf16[128,16]{0,1:T(8,128)(2,1)S(1)}, bf16[128,16]{0,1:T(8,128)(2,1)}, u32[]{:S(2)}) copy-start(bf16[128,16]{0,1:T(8,128)(2,1)} %param.18) | copy-start | bytes 12292
  2.8 23.7 %all-to-all-start = ((bf16[32,2,128]{2,1,0:T(2,128)(2,1)}), bf16[32,2,128]{2,1,0:T(2,128)(2,1)S(1)}, u32[]{:S(2)}, u32[]{:S(2)}) async-start(bf16[32,2,128]{2,1,0:T(2,128)(2,1)} %get-tuple-element.25), calls=%async_computation | async-start | bytes 32768 | tf_op jit(solution)/shard_map/all_to_all | solution.py:523
  21.1 4.2 %collective-permute-start.1 = (bf16[8,2048]{1,0:T(8,128)(2,1)}, bf16[8,2048]{1,0:T(8,128)(2,1)S(1)}, u32[]{:S(2)}, u32[]{:S(2)}) collective-permute-start(bf16[8,2048]{1,0:T(8,128)(2,1)} %feat_hbm.1), channel_id=1, source_target_pairs={{0,496},{16,0},{32,16},{48,32},{64,48},{80,64},{96,80},{112,96},{1... | collective-permute-start | bytes 98312 | tf_op jit(solution)/shard_map/ppermute | solution.py:517
  21.5 3.8 %collective-permute-start = (bf16[8,2048]{1,0:T(8,128)(2,1)}, bf16[8,2048]{1,0:T(8,128)(2,1)S(1)}, u32[]{:S(2)}, u32[]{:S(2)}) collective-permute-start(bf16[8,2048]{1,0:T(8,128)(2,1)} %feat_hbm.1), channel_id=1, source_target_pairs={{0,16},{16,32},{32,48},{48,64},{64,80},{80,96},{96,112},{112,128},... | collective-permute-start | bytes 98312 | tf_op jit(solution)/shard_map/ppermute | solution.py:517
  50.4 7.1 %collective-permute-start.2 = (f32[16,128]{1,0:T(8,128)S(1)}, f32[16,128]{1,0:T(8,128)S(1)}, u32[]{:S(2)}, u32[]{:S(2)}) collective-permute-start(f32[16,128]{1,0:T(8,128)S(1)} %get-tuple-element.36), channel_id=1, source_target_pairs={{0,16},{16,0},{32,48},{48,32},{64,80},{80,64},{96,112},{112,96},{1... | collective-permute-start | bytes 24584 | tf_op jit(solution)/shard_map/ppermute | solution.py:633
  58.2 21.7 %all-to-all-start.3 = ((bf16[160,4,128]{2,1,0:T(4,128)(2,1)}), bf16[160,4,128]{2,1,0:T(4,128)(2,1)S(1)}, u32[]{:S(2)}, u32[]{:S(2)}) async-start(bf16[160,4,128]{2,1,0:T(4,128)(2,1)} %shard_map.154), calls=%async_computation.3 | async-start | bytes 327680 | tf_op jit(solution)/shard_map/all_to_all | solution.py:523
  73.1 6.8 %collective-permute-start.3 = (bf16[8,2048]{1,0:T(8,128)(2,1)S(1)}, bf16[8,2048]{1,0:T(8,128)(2,1)S(1)}, u32[]{:S(2)}, u32[]{:S(2)}) collective-permute-start(bf16[8,2048]{1,0:T(8,128)(2,1)S(1)} %get-tuple-element.39), channel_id=1, source_target_pairs={{0,496},{16,0},{32,16},{48,32},{64,48},{80,64},{96,80},{112,96},{1... | collective-permute-start | bytes 98312 | tf_op jit(solution)/shard_map/ppermute | solution.py:517
  73.2 6.7 %collective-permute-start.4 = (bf16[8,2048]{1,0:T(8,128)(2,1)S(1)}, bf16[8,2048]{1,0:T(8,128)(2,1)S(1)}, u32[]{:S(2)}, u32[]{:S(2)}) collective-permute-start(bf16[8,2048]{1,0:T(8,128)(2,1)S(1)} %get-tuple-element.40), channel_id=1, source_target_pairs={{0,16},{16,32},{32,48},{48,64},{64,80},{80,96},{96,112},{112,128},... | collective-permute-start | bytes 98312 | tf_op jit(solution)/shard_map/ppermute | solution.py:517

commit v5 on v4

--- a/solution.py
+++ b/solution.py
@@ -23,7 +23,7 @@
 RET = 5
 FWD_ROWS = 80
 BWD_ROWS = 80
-ROW_OUT, ROW_BACK = 20, 16
+ROW_OUT, ROW_BACK = 22, 16
 COL_OUT, COL_BACK = 11, 10
 F32, BF16 = jnp.float32, jnp.bfloat16
 NT = (((1,), (1,)), ((), ()))
@@ -373,8 +373,9 @@
         db = jnp.where(second < n, dst[0, g, second], none)
         ka = jnp.where(first < n, src[0, g, first] + base, base)
         kb = jnp.where(second < n, src[0, g, second] + base, base)
-        res = dot(lo[da], tile_at(first), NT) + dot(hi[db], tile_at(second), NT)
-        done.append((res, ka, kb))
+        left = jnp.concatenate([lo[da], hi[db]], axis=1)
+        right = jnp.concatenate([tile_at(first), tile_at(second)], axis=1)
+        done.append((dot(left, right, NT), ka, kb))
     for res, ka, kb in done:
         acc[ka] += res[:FEAT]
         acc[kb] += res[FEAT:]

time: 81.5 us -> 81.3 us (level)
  starting transfers between devices: 40.3 us -> 38.3 us
  blocking collectives: 22.2 us -> 23.6 us
  Pallas kernels: 15.2 us -> 16.1 us
    ppermute x1, starting transfers between devices: 5.69 us -> 4.05 us  [per_device(): lax.ppermute(given_half, 'row', [(i, i ^ 1) for i in range(NROW)])]
    all_to_all x2, blocking collectives: 22.2 us -> 23.6 us  [swap(): return lax.all_to_all(x, axis, 0, 0, axis_index_groups=[group], tiled=True)]
  transfers between devices with their start and end apart: 7 -> 7, of which waited for: 2 -> 1; matrix products, arithmetic and copies ran while one was open for 0% -> 0% of each run, Pallas kernels for 12% -> 13%
where the time goes in v5:
time: 81.3 us; the launch traced here: 81.2 us
  starting transfers between devices  38.3 us (47%)
  blocking collectives  23.6 us (29%)
  Pallas kernels  16.1 us (20%)
  waiting for transfers between devices  2.37 us (3%)
  between operations  0.83 us (1%)
    all_to_all x2, starting transfers between devices, swap(): return lax.all_to_all(x, axis, 0, 0, axis_index_groups=[group], tiled=True)  30.7 us
    all_to_all x2, blocking collectives, swap(): return lax.all_to_all(x, axis, 0, 0, axis_index_groups=[group], tiled=True)  23.6 us
    ppermute x1, starting transfers between devices, per_device(): lax.ppermute(given_half, 'row', [(i, i ^ 1) for i in range(NROW)])  4.05 us
    ppermute x4, starting transfers between devices, shifted(): lax.ppermute(shard, 'row', [(i, (i + by) % NROW) for i in range(NROW)])  3.51 us
    pallas_call x1, Pallas kernels, per_device(): call(back_near_kernel, (sds((FEAT, NODES_LOC), BF16),) * 2, [VM, HB] + [V...  2.44 us
    pallas_call x1, Pallas kernels, per_device(): call(back_own_kernel, (sds((FEAT, NODES_LOC), F32), sds((HLOC, NODES_LOC)...  2.42 us
    ppermute x4, waiting for transfers between devices, shifted(): lax.ppermute(shard, 'row', [(i, (i + by) % NROW) for i in range(NROW)])  2.37 us
    pallas_call x1, Pallas kernels, per_device(): call(own_kernel, (sds((RT, FEAT, TILE), F32), sds((2, 32, TILE, TILE), BF...  2.27 us
  transfers between devices with their start and end apart: 7, of which 1 were waited for; matrix products, arithmetic and copies ran while one was open for 0% of the time, Pallas kernels for 13%

profile of v5, /device:TPU:1, one launch (start us, length us, event | category | flops | bytes accessed | tf_op | source)
XLA Modules:
  0.0 81.2 jit_solution(14029463027937230793)
XLA Ops:
  0.6 0.0 copy-start
  0.6 0.0 copy-start.3
  0.7 0.0 copy-start.2
  0.7 0.0 copy-start.1
  0.7 2.1 %shard_map.146 = (bf16[32,2,128]{2,1,0:T(2,128)(2,1)}, s32[8,128]{1,0:T(8,128)S(1)}, bf16[8,2048]{1,0:T(8,128)(2,1)S(1)}, s32[1,4,32]{2,1,0:T(4,128)S(1)}, s32[1,4,32]{2,1,0:T(4,128)S(1)}, /*index=5*/s32[1,4]{1,0:T(1,128)S(1)}) custom-call(bf16[8,2048]{1,0:T(8,128)(2,1)} %feat_hbm.1, s32[1,32,32]{2,1,0:T(8,128)} %rows_hbm.1, s32[1,32]{1,0:T(1,128)} %counts_hbm.1, ...), custom_call_target="tpu_custom_call" | custom-call | flops 33554432 | tf_op jit(solution)/shard_map/pallas_call | solution.py:546
  2.8 17.5 %all-to-all-start = ((bf16[32,2,128]{2,1,0:T(2,128)(2,1)}), bf16[32,2,128]{2,1,0:T(2,128)(2,1)S(1)}, u32[]{:S(2)}, u32[]{:S(2)}) async-start(bf16[32,2,128]{2,1,0:T(2,128)(2,1)} %get-tuple-element.25), calls=%async_computation | async-start | bytes 32768 | tf_op jit(solution)/shard_map/all_to_all | solution.py:524
  20.2 0.4 collective-permute-start.1
  20.6 1.4 %collective-permute-start = (bf16[8,2048]{1,0:T(8,128)(2,1)}, bf16[8,2048]{1,0:T(8,128)(2,1)S(1)}, u32[]{:S(2)}, u32[]{:S(2)}) collective-permute-start(bf16[8,2048]{1,0:T(8,128)(2,1)} %feat_hbm.1), channel_id=1, source_target_pairs={{0,16},{16,32},{32,48},{48,64},{64,80},{80,96},{96,112},{112,128},... | collective-permute-start | bytes 98312 | tf_op jit(solution)/shard_map/ppermute | solution.py:518
  22.0 2.3 %shard_map.147 = (f32[16,8,128]{2,1,0:T(8,128)S(1)}, bf16[2,32,128,128]{3,2,1,0:T(8,128)(2,1)S(1)}, bf16[1,32,128,128]{3,2,1,0:T(8,128)(2,1)S(1)}) custom-call(bf16[8,2048]{1,0:T(8,128)(2,1)S(1)} %get-tuple-element.26.feat, s32[1,4,32]{2,1,0:T(4,128)S(1)} %get-tuple-element.27.dst_in.dst_hbm, s32[1,4,32]{2,1,0:T(4,128)S(1)} %get-tuple-element.28.src_in.src_hbm, ...), custom_call_target="tpu_custom_call" | custom-call | flops 16777216 | bytes 4194304 | tf_op jit(solution)/shard_map/pallas_call | solution.py:567
  24.3 0.0 collective-permute-done.1.foll
  24.3 0.0 collective-permute-done.prev
  24.3 1.5 %shard_map.148.part = f32[16,8,128]{2,1,0:T(8,128)S(1)} custom-call(bf16[8,2048]{1,0:T(8,128)(2,1)S(1)} %collective-permute-done.prev, bf16[8,2048]{1,0:T(8,128)(2,1)S(1)} %collective-permute-done.1.foll, f32[16,8,128]{2,1,0:T(8,128)S(1)} %get-tuple-element.30.before, bf16[2,32,128,128]{3,2,1,0:T(8,128)(2,1)S(1)} %get-tuple-element.31.near, ...), custom_call_target="tpu_custom_call" | custom-call | flops 33554432 | bytes 2097152 | tf_op jit(solution)/shard_map/pallas_call | solution.py:588
  25.8 0.0 all-to-all-done.recv
  25.8 0.0 copy-done
  25.8 0.0 copy-done.3
  25.8 0.0 copy-done.2
  25.8 0.0 copy-done.1
  25.8 1.4 %shard_map.149 = bf16[16,80,128]{2,1,0:T(8,128)(2,1)S(1)} custom-call(bf16[32,2,128]{2,1,0:T(2,128)(2,1)S(1)} %all-to-all-done.recv, f32[16,8,128]{2,1,0:T(8,128)S(1)} %shard_map.148.part, bf16[8,2048]{1,0:T(8,128)(2,1)S(1)} %get-tuple-element.26.feat, bf16[16,2048]{1,0:T(8,128)(2,1)S(1)} %copy-done, bf16[16,128]{1,0:T(8,128)(2,1)S(1)} %bitcast.6, ...), custom_call_target="tpu_custom_call" | custom-call | flops 16777216 | bytes 1048576 | tf_op jit(solution)/shard_map/pallas_call | solution.py:597
  27.2 12.8 %all_to_all.20.r = bf16[16,80,128]{2,1,0:T(8,128)(2,1)S(1)} all-to-all(bf16[16,80,128]{2,1,0:T(8,128)(2,1)S(1)} %shard_map.149), channel_id=1, replica_groups={{11,12,13,14,15,0,1,2,3,4,5,6,7,8,9,10},{27,28,29,30,31,16,17,18,19,20,..., dimensions={0} | all-to-all | bytes 655360 | tf_op jit(solution)/shard_map/all_to_all | solution.py:524
  40.1 0.4 shard_map.150
  40.5 10.8 %all_to_all.21.r = bf16[16,80,128]{2,1,0:T(8,128)(2,1)S(1)} all-to-all(bf16[16,80,128]{2,1,0:T(8,128)(2,1)S(1)} %shard_map.150), channel_id=1, replica_groups={{10,11,12,13,14,15,0,1,2,3,4,5,6,7,8,9},{26,27,28,29,30,31,16,17,18,19,..., dimensions={0} | all-to-all | bytes 655360 | tf_op jit(solution)/shard_map/all_to_all | solution.py:524
  51.3 0.1 shard_map.153
  51.4 4.0 %collective-permute-start.2 = (f32[16,128]{1,0:T(8,128)S(1)}, f32[16,128]{1,0:T(8,128)S(1)}, u32[]{:S(2)}, u32[]{:S(2)}) collective-permute-start(f32[16,128]{1,0:T(8,128)S(1)} %get-tuple-element.36), channel_id=1, source_target_pairs={{0,16},{16,0},{32,48},{48,32},{64,80},{80,64},{96,112},{112,96},{1... | collective-permute-start | bytes 24584 | tf_op jit(solution)/shard_map/ppermute | solution.py:634
  55.5 1.7 %shard_map.152.far = bf16[32,2,128]{2,1,0:T(2,128)(2,1)S(1)} custom-call(bf16[16,80,128]{2,1,0:T(8,128)(2,1)S(1)} %all_to_all.21.r, bf16[1,32,128,128]{3,2,1,0:T(8,128)(2,1)S(1)} %get-tuple-element.32.kept, s32[1,4,32]{2,1,0:T(4,128)S(1)} %get-tuple-element.27.dst_in.dst_hbm, s32[1,4,32]{2,1,0:T(4,128)S(1)} %get-tuple-element.28.src_in.src_hbm, ...), custom_call_target="tpu_custom_call" | custom-call | flops 16777216 | bytes 1048576 | tf_op jit(solution)/shard_map/pallas_call | solution.py:635
  57.1 0.0 collective-permute-done.2.got
  57.1 0.7 shard_map.154
  57.9 13.3 %all-to-all-start.3 = ((bf16[160,4,128]{2,1,0:T(4,128)(2,1)}), bf16[160,4,128]{2,1,0:T(4,128)(2,1)S(1)}, u32[]{:S(2)}, u32[]{:S(2)}) async-start(bf16[160,4,128]{2,1,0:T(4,128)(2,1)} %shard_map.154), calls=%async_computation.3 | async-start | bytes 327680 | tf_op jit(solution)/shard_map/all_to_all | solution.py:524
  71.1 2.4 %shard_map.155 = (bf16[8,2048]{1,0:T(8,128)(2,1)S(1)}, bf16[8,2048]{1,0:T(8,128)(2,1)S(1)}) custom-call(bf16[16,80,128]{2,1,0:T(8,128)(2,1)S(1)} %all_to_all.21.r, bf16[1,4,32,128,128]{4,3,2,1,0:T(8,128)(2,1)} %tiles.5, s32[1,4,32]{2,1,0:T(4,128)S(1)} %get-tuple-element.27.dst_in.dst_hbm, s32[1,4,32]{2,1,0:T(4,128)S(1)} %get-tuple-element.28.src_in.src_hbm, ...), custom_call_target="tpu_custom_call" | custom-call | flops 33554432 | bytes 2097152 | tf_op jit(solution)/shard_map/pallas_call | solution.py:653
  73.6 0.0 collective-permute-start.3
  73.6 1.7 %collective-permute-start.4 = (bf16[8,2048]{1,0:T(8,128)(2,1)S(1)}, bf16[8,2048]{1,0:T(8,128)(2,1)S(1)}, u32[]{:S(2)}, u32[]{:S(2)}) collective-permute-start(bf16[8,2048]{1,0:T(8,128)(2,1)S(1)} %get-tuple-element.40), channel_id=1, source_target_pairs={{0,16},{16,32},{32,48},{48,64},{64,80},{80,96},{96,112},{112,128},... | collective-permute-start | bytes 98312 | tf_op jit(solution)/shard_map/ppermute | solution.py:518
  75.3 2.4 %shard_map.151 = (f32[8,2048]{1,0:T(8,128)S(1)}, bf16[16,2048]{1,0:T(8,128)(2,1)}) custom-call(bf16[16,80,128]{2,1,0:T(8,128)(2,1)S(1)} %all_to_all.21.r, bf16[1,4,32,128,128]{4,3,2,1,0:T(8,128)(2,1)} %tiles.5, s32[1,4,32]{2,1,0:T(4,128)S(1)} %get-tuple-element.27.dst_in.dst_hbm, s32[1,4,32]{2,1,0:T(4,128)S(1)} %get-tuple-element.28.src_in.src_hbm, ...), custom_call_target="tpu_custom_call" | custom-call | flops 16777216 | bytes 1048576 | tf_op jit(solution)/shard_map/pallas_call | solution.py:664
  77.8 2.4 %collective-permute-done.3.after = bf16[8,2048]{1,0:T(8,128)(2,1)S(1)} collective-permute-done((bf16[8,2048]{1,0:T(8,128)(2,1)S(1)}, bf16[8,2048]{1,0:T(8,128)(2,1)S(1)}, u32[]{:S(2)}, u32[]{:S(2)}) %collective-permute-start.3) | collective-permute-done | bytes 32800 | tf_op jit(solution)/shard_map/ppermute | solution.py:518
  80.1 0.0 collective-permute-done.4.before
  80.1 0.0 all-to-all-done.3.recv
  80.1 1.1 %shard_map.156 = (bf16[8,2048]{1,0:T(8,128)(2,1)}, f32[16,128]{1,0:T(8,128)}, f32[16,128]{1,0:T(8,128)}, f32[1,16]{1,0:T(1,128)}) custom-call(bf16[160,4,128]{2,1,0:T(4,128)(2,1)S(1)} %all-to-all-done.3.recv, s32[8,128]{1,0:T(8,128)S(1)} %get-tuple-element.37.index, f32[8,2048]{1,0:T(8,128)S(1)} %get-tuple-element.38.own, ...), custom_call_target="tpu_custom_call" | custom-call | tf_op jit(solution)/shard_map/pallas_call | solution.py:673
Async XLA Ops:
  0.6 25.1 %copy-start = (bf16[16,2048]{1,0:T(8,128)(2,1)S(1)}, bf16[16,2048]{1,0:T(8,128)(2,1)}, u32[]{:S(2)}) copy-start(bf16[16,2048]{1,0:T(8,128)(2,1)} %cot.1) | copy-start | bytes 196612
  0.6 25.1 %copy-start.3 = (f32[16]{0:T(128)S(1)}, f32[16]{0:T(128)}, u32[]{:S(2)}) copy-start(f32[16]{0:T(128)} %param.20) | copy-start | bytes 196
  0.7 25.1 %copy-start.2 = (bf16[128,16]{0,1:T(8,128)(2,1)S(1)}, bf16[128,16]{0,1:T(8,128)(2,1)}, u32[]{:S(2)}) copy-start(bf16[128,16]{0,1:T(8,128)(2,1)} %param.19) | copy-start | bytes 12292
  0.7 25.1 %copy-start.1 = (bf16[128,16]{0,1:T(8,128)(2,1)S(1)}, bf16[128,16]{0,1:T(8,128)(2,1)}, u32[]{:S(2)}) copy-start(bf16[128,16]{0,1:T(8,128)(2,1)} %param.18) | copy-start | bytes 12292
  2.8 23.0 %all-to-all-start = ((bf16[32,2,128]{2,1,0:T(2,128)(2,1)}), bf16[32,2,128]{2,1,0:T(2,128)(2,1)S(1)}, u32[]{:S(2)}, u32[]{:S(2)}) async-start(bf16[32,2,128]{2,1,0:T(2,128)(2,1)} %get-tuple-element.25), calls=%async_computation | async-start | bytes 32768 | tf_op jit(solution)/shard_map/all_to_all | solution.py:524
  20.2 4.0 %collective-permute-start.1 = (bf16[8,2048]{1,0:T(8,128)(2,1)}, bf16[8,2048]{1,0:T(8,128)(2,1)S(1)}, u32[]{:S(2)}, u32[]{:S(2)}) collective-permute-start(bf16[8,2048]{1,0:T(8,128)(2,1)} %feat_hbm.1), channel_id=1, source_target_pairs={{0,496},{16,0},{32,16},{48,32},{64,48},{80,64},{96,80},{112,96},{1... | collective-permute-start | bytes 98312 | tf_op jit(solution)/shard_map/ppermute | solution.py:518
  20.6 3.7 %collective-permute-start = (bf16[8,2048]{1,0:T(8,128)(2,1)}, bf16[8,2048]{1,0:T(8,128)(2,1)S(1)}, u32[]{:S(2)}, u32[]{:S(2)}) collective-permute-start(bf16[8,2048]{1,0:T(8,128)(2,1)} %feat_hbm.1), channel_id=1, source_target_pairs={{0,16},{16,32},{32,48},{48,64},{64,80},{80,96},{96,112},{112,128},... | collective-permute-start | bytes 98312 | tf_op jit(solution)/shard_map/ppermute | solution.py:518
  51.4 5.7 %collective-permute-start.2 = (f32[16,128]{1,0:T(8,128)S(1)}, f32[16,128]{1,0:T(8,128)S(1)}, u32[]{:S(2)}, u32[]{:S(2)}) collective-permute-start(f32[16,128]{1,0:T(8,128)S(1)} %get-tuple-element.36), channel_id=1, source_target_pairs={{0,16},{16,0},{32,48},{48,32},{64,80},{80,64},{96,112},{112,96},{1... | collective-permute-start | bytes 24584 | tf_op jit(solution)/shard_map/ppermute | solution.py:634
  57.9 22.3 %all-to-all-start.3 = ((bf16[160,4,128]{2,1,0:T(4,128)(2,1)}), bf16[160,4,128]{2,1,0:T(4,128)(2,1)S(1)}, u32[]{:S(2)}, u32[]{:S(2)}) async-start(bf16[160,4,128]{2,1,0:T(4,128)(2,1)} %shard_map.154), calls=%async_computation.3 | async-start | bytes 327680 | tf_op jit(solution)/shard_map/all_to_all | solution.py:524
  73.6 6.5 %collective-permute-start.3 = (bf16[8,2048]{1,0:T(8,128)(2,1)S(1)}, bf16[8,2048]{1,0:T(8,128)(2,1)S(1)}, u32[]{:S(2)}, u32[]{:S(2)}) collective-permute-start(bf16[8,2048]{1,0:T(8,128)(2,1)S(1)} %get-tuple-element.39), channel_id=1, source_target_pairs={{0,496},{16,0},{32,16},{48,32},{64,48},{80,64},{96,80},{112,96},{1... | collective-permute-start | bytes 98312 | tf_op jit(solution)/shard_map/ppermute | solution.py:518
  73.6 6.5 %collective-permute-start.4 = (bf16[8,2048]{1,0:T(8,128)(2,1)S(1)}, bf16[8,2048]{1,0:T(8,128)(2,1)S(1)}, u32[]{:S(2)}, u32[]{:S(2)}) collective-permute-start(bf16[8,2048]{1,0:T(8,128)(2,1)S(1)} %get-tuple-element.40), channel_id=1, source_target_pairs={{0,16},{16,32},{32,48},{48,64},{64,80},{80,96},{96,112},{112,128},... | collective-permute-start | bytes 98312 | tf_op jit(solution)/shard_map/ppermute | solution.py:518

commit v6 on v5

--- a/solution.py
+++ b/solution.py
@@ -387,11 +387,17 @@
     zero_source(lo, hi, RT)
 
 
-def back_far_kernel(r, kept, dst_hbm, src_hbm, count_hbm, out, dst, src, count, lo, hi, acc, sems):
+def back_far_kernel(
+    r, kept, dst_hbm, src_hbm, count_hbm, tiles, out, near, dst, src, count, lo, hi, acc, sems,
+    near_sems,
+):
     copies = start_all((count_hbm, dst_hbm, src_hbm), (count, dst, src), sems)
+    start_chunks(tiles, near, [1, 2], count, near_sems, 0, 1)
+    copies[0].wait()
+    start_chunks(tiles, near, [1, 2], count, near_sems, 1, NCHUNK)
     load_grads(r, lo, hi)
     acc[...] = jnp.zeros_like(acc)
-    wait_all(copies)
+    wait_all(copies[1:])
     n = count[0, 3]
 
     def step(it, carry):
@@ -402,6 +408,13 @@
     rows = compact([acc[k] for k in range(NB)]).astype(BF16)
     for p in range(NROW):
         out[p] = rows[2 * p : 2 * p + 2]
+    for slot, g in enumerate([1, 2]):
+
+        def arrived(it, carry):
+            chunk_copy(tiles, near, g, it, slot, near_sems).wait()
+            return carry
+
+        lax.fori_loop(0, steps(count[0, g]), arrived, 0)
 
 
 def pack_kernel(far, bsum, kept, got, out):
@@ -437,9 +450,23 @@
         lax.fori_loop(0, steps(n), step, 0)
 
 
-def back_near_kernel(r, tiles, dst_hbm, src_hbm, count_hbm, prev, foll, *scratch):
-    back_groups([1, 2], r, tiles, dst_hbm, src_hbm, count_hbm, *scratch)
-    acc = scratch[6]
+def back_near_kernel(
+    r, near, dst_hbm, src_hbm, count_hbm, prev, foll, dst, src, count, lo, hi, acc, sems
+):
+    copies = start_all((count_hbm, dst_hbm, src_hbm), (count, dst, src), sems)
+    load_grads(r, lo, hi)
+    acc[...] = jnp.zeros_like(acc)
+    wait_all(copies)
+    for slot, g in enumerate([1, 2]):
+        n = count[0, g]
+
+        def step(it, carry):
+            backward_step(
+                it, g, slot * RT, RT, lo, hi, lambda i: near[slot, i], dst, src, n, acc
+            )
+            return carry
+
+        lax.fori_loop(0, steps(n), step, 0)
     for k in range(RT):
         cols = slice(k * TILE, (k + 1) * TILE)
         prev[:, cols] = acc[k].astype(BF16)
@@ -632,20 +659,21 @@
         weights_kernel, (half, half, sds((1, TILE), F32)), [VM], (VM, VM, VM)
     )(back)
     got_half = lax.ppermute(given_half, "row", [(i, i ^ 1) for i in range(NROW)])
-    far = call(
+    far, near_back = call(
         back_far_kernel,
-        sds((NROW, 2, TILE), BF16),
-        [VM] * 5,
-        VM,
+        (sds((NROW, 2, TILE), BF16), sds((2, 32, TILE, TILE), BF16)),
+        [VM] * 5 + [HB],
+        (VM, VM),
         [
             *TABLES,
             *sources(RT),
             pltpu.VMEM((NB, FEAT, TILE), F32),
             pltpu.SemaphoreType.DMA((3,)),
+            pltpu.SemaphoreType.DMA((2, NCHUNK)),
         ],
         flops=2 * 16 * TILE * TILE * 32,
         nbytes=1 << 20,
-    )(back, kept, *here)
+    )(back, kept, *here, tiles)
     returning = call(pack_kernel, sds((NROW * RET, 4, TILE), BF16), [VM] * 4, VM)(
         far, bsum, kept_half, got_half
     )
@@ -653,12 +681,17 @@
     to_previous, to_following = call(
         back_near_kernel,
         (sds((FEAT, NODES_LOC), BF16),) * 2,
-        [VM, HB] + [VM] * 3,
+        [VM] * 5,
         (VM, VM),
-        back_scratch(2),
+        [
+            *TABLES,
+            *sources(RT),
+            pltpu.VMEM((2 * RT, FEAT, TILE), F32),
+            pltpu.SemaphoreType.DMA((3,)),
+        ],
         flops=2 * 16 * TILE * TILE * 64,
         nbytes=2 << 20,
-    )(back, tiles, *here)
+    )(back, near_back, *here)
     after = shifted(to_previous, -1)
     before = shifted(to_following, 1)
     own, hidden = call(

time: 81.3 us -> 81.4 us (level)
  waiting for transfers between devices: 2.37 us -> 4.41 us
  blocking collectives: 23.6 us -> 22.5 us
  Pallas kernels: 16.1 us -> 15.2 us
    ppermute x4, waiting for transfers between devices: 2.37 us -> 4.4 us  [shifted(): lax.ppermute(shard, 'row', [(i, (i + by) % NROW) for i in range(NROW)])]
    all_to_all x2, blocking collectives: 23.6 us -> 22.5 us  [swap(): return lax.all_to_all(x, axis, 0, 0, axis_index_groups=[group], tiled=True)]
    ppermute x1, starting transfers between devices: 4.05 us -> 5.13 us  [per_device(): lax.ppermute(given_half, 'row', [(i, i ^ 1) for i in range(NROW)])]
    all_to_all x2, starting transfers between devices: 30.7 us -> 29.6 us  [swap(): return lax.all_to_all(x, axis, 0, 0, axis_index_groups=[group], tiled=True)]
  transfers between devices with their start and end apart: 7 -> 7, of which waited for: 1 -> 2; matrix products, arithmetic and copies ran while one was open for 0% -> 0% of each run, Pallas kernels for 13% -> 12%
where the time goes in v6:
time: 81.4 us; the launch traced here: 80.9 us
  starting transfers between devices  38 us (47%)
  blocking collectives  22.5 us (28%)
  Pallas kernels  15.2 us (19%)
  waiting for transfers between devices  4.41 us (5%)
    all_to_all x2, starting transfers between devices, swap(): return lax.all_to_all(x, axis, 0, 0, axis_index_groups=[group], tiled=True)  29.6 us
    all_to_all x2, blocking collectives, swap(): return lax.all_to_all(x, axis, 0, 0, axis_index_groups=[group], tiled=True)  22.5 us
    ppermute x1, starting transfers between devices, per_device(): lax.ppermute(given_half, 'row', [(i, i ^ 1) for i in range(NROW)])  5.13 us
    ppermute x4, waiting for transfers between devices, shifted(): lax.ppermute(shard, 'row', [(i, (i + by) % NROW) for i in range(NROW)])  4.4 us
    ppermute x4, starting transfers between devices, shifted(): lax.ppermute(shard, 'row', [(i, (i + by) % NROW) for i in range(NROW)])  3.2 us
    pallas_call x1, Pallas kernels, per_device(): call(back_own_kernel, (sds((FEAT, NODES_LOC), F32), sds((HLOC, NODES_LOC)...  2.42 us
    pallas_call x1, Pallas kernels, per_device(): call(own_kernel, (sds((RT, FEAT, TILE), F32), sds((2, 32, TILE, TILE), BF...  2.18 us
    pallas_call x1, Pallas kernels, per_device(): call(gather_kernel, (sds((NROW, 2, TILE), BF16), sds((NB, TILE), jnp.int3...  2.06 us
  transfers between devices with their start and end apart: 7, of which 2 were waited for; matrix products, arithmetic and copies ran while one was open for 0% of the time, Pallas kernels for 12%

profile of v6, /device:TPU:1, one launch (start us, length us, event | category | flops | bytes accessed | tf_op | source)
XLA Modules:
  0.0 80.9 jit_solution(14255759302723638830)
XLA Ops:
  0.6 2.1 %shard_map.146 = (bf16[32,2,128]{2,1,0:T(2,128)(2,1)}, s32[8,128]{1,0:T(8,128)S(1)}, bf16[8,2048]{1,0:T(8,128)(2,1)S(1)}, s32[1,4,32]{2,1,0:T(4,128)S(1)}, s32[1,4,32]{2,1,0:T(4,128)S(1)}, /*index=5*/s32[1,4]{1,0:T(1,128)S(1)}) custom-call(bf16[8,2048]{1,0:T(8,128)(2,1)} %feat_hbm.1, s32[1,32,32]{2,1,0:T(8,128)} %rows_hbm.1, s32[1,32]{1,0:T(1,128)} %counts_hbm.1, ...), custom_call_target="tpu_custom_call" | custom-call | flops 33554432 | tf_op jit(solution)/shard_map/pallas_call | solution.py:573
  2.7 17.5 %all-to-all-start = ((bf16[32,2,128]{2,1,0:T(2,128)(2,1)}), bf16[32,2,128]{2,1,0:T(2,128)(2,1)S(1)}, u32[]{:S(2)}, u32[]{:S(2)}) async-start(bf16[32,2,128]{2,1,0:T(2,128)(2,1)} %get-tuple-element.27), calls=%async_computation | async-start | bytes 32768 | tf_op jit(solution)/shard_map/all_to_all | solution.py:551
  20.2 1.4 %collective-permute-start = (bf16[8,2048]{1,0:T(8,128)(2,1)}, bf16[8,2048]{1,0:T(8,128)(2,1)S(1)}, u32[]{:S(2)}, u32[]{:S(2)}) collective-permute-start(bf16[8,2048]{1,0:T(8,128)(2,1)} %feat_hbm.1), channel_id=1, source_target_pairs={{0,16},{16,32},{32,48},{48,64},{64,80},{80,96},{96,112},{112,128},... | collective-permute-start | bytes 98312 | tf_op jit(solution)/shard_map/ppermute | solution.py:545
  21.6 0.0 collective-permute-start.1
  21.6 2.2 %shard_map.147 = (f32[16,8,128]{2,1,0:T(8,128)S(1)}, bf16[2,32,128,128]{3,2,1,0:T(8,128)(2,1)S(1)}, bf16[1,32,128,128]{3,2,1,0:T(8,128)(2,1)S(1)}) custom-call(bf16[8,2048]{1,0:T(8,128)(2,1)S(1)} %get-tuple-element.28.feat, s32[1,4,32]{2,1,0:T(4,128)S(1)} %get-tuple-element.29.dst_in.dst_hbm, s32[1,4,32]{2,1,0:T(4,128)S(1)} %get-tuple-element.30.src_in.src_hbm, ...), custom_call_target="tpu_custom_call" | custom-call | flops 16777216 | bytes 4194304 | tf_op jit(solution)/shard_map/pallas_call | solution.py:594
  23.8 0.0 copy-start
  23.8 0.0 copy-start.1
  23.8 0.0 copy-start.2
  23.8 0.0 copy-start.3
  23.8 0.0 collective-permute-done.prev
  23.9 1.4 %collective-permute-done.1.foll = bf16[8,2048]{1,0:T(8,128)(2,1)S(1)} collective-permute-done((bf16[8,2048]{1,0:T(8,128)(2,1)}, bf16[8,2048]{1,0:T(8,128)(2,1)S(1)}, u32[]{:S(2)}, u32[]{:S(2)}) %collective-permute-start.1) | collective-permute-done | bytes 32800 | tf_op jit(solution)/shard_map/ppermute | solution.py:545
  25.3 1.6 %shard_map.148.part = f32[16,8,128]{2,1,0:T(8,128)S(1)} custom-call(bf16[8,2048]{1,0:T(8,128)(2,1)S(1)} %collective-permute-done.prev, bf16[8,2048]{1,0:T(8,128)(2,1)S(1)} %collective-permute-done.1.foll, f32[16,8,128]{2,1,0:T(8,128)S(1)} %get-tuple-element.32.before, bf16[2,32,128,128]{3,2,1,0:T(8,128)(2,1)S(1)} %get-tuple-element.33.near, ...), custom_call_target="tpu_custom_call" | custom-call | flops 33554432 | bytes 2097152 | tf_op jit(solution)/shard_map/pallas_call | solution.py:615
  26.9 0.0 all-to-all-done.recv
  26.9 0.0 copy-done
  26.9 0.0 copy-done.1
  26.9 0.0 copy-done.2
  26.9 0.0 copy-done.3
  26.9 0.9 %shard_map.149 = bf16[16,80,128]{2,1,0:T(8,128)(2,1)S(1)} custom-call(bf16[32,2,128]{2,1,0:T(2,128)(2,1)S(1)} %all-to-all-done.recv, f32[16,8,128]{2,1,0:T(8,128)S(1)} %shard_map.148.part, bf16[8,2048]{1,0:T(8,128)(2,1)S(1)} %get-tuple-element.28.feat, bf16[16,2048]{1,0:T(8,128)(2,1)S(1)} %copy-done, bf16[16,128]{1,0:T(8,128)(2,1)S(1)} %bitcast.6, ...), custom_call_target="tpu_custom_call" | custom-call | flops 16777216 | bytes 1048576 | tf_op jit(solution)/shard_map/pallas_call | solution.py:624
  27.9 12.6 %all_to_all.20.r = bf16[16,80,128]{2,1,0:T(8,128)(2,1)S(1)} all-to-all(bf16[16,80,128]{2,1,0:T(8,128)(2,1)S(1)} %shard_map.149), channel_id=1, replica_groups={{11,12,13,14,15,0,1,2,3,4,5,6,7,8,9,10},{27,28,29,30,31,16,17,18,19,20,..., dimensions={0} | all-to-all | bytes 655360 | tf_op jit(solution)/shard_map/all_to_all | solution.py:551
  40.5 0.4 shard_map.150
  40.9 9.9 %all_to_all.21.r = bf16[16,80,128]{2,1,0:T(8,128)(2,1)S(1)} all-to-all(bf16[16,80,128]{2,1,0:T(8,128)(2,1)S(1)} %shard_map.150), channel_id=1, replica_groups={{10,11,12,13,14,15,0,1,2,3,4,5,6,7,8,9},{26,27,28,29,30,31,16,17,18,19,..., dimensions={0} | all-to-all | bytes 655360 | tf_op jit(solution)/shard_map/all_to_all | solution.py:551
  50.8 0.1 shard_map.153
  50.9 5.1 %collective-permute-start.2 = (f32[16,128]{1,0:T(8,128)S(1)}, f32[16,128]{1,0:T(8,128)S(1)}, u32[]{:S(2)}, u32[]{:S(2)}) collective-permute-start(f32[16,128]{1,0:T(8,128)S(1)} %get-tuple-element.39), channel_id=1, source_target_pairs={{0,16},{16,0},{32,48},{48,32},{64,80},{80,64},{96,112},{112,96},{1... | collective-permute-start | bytes 24584 | tf_op jit(solution)/shard_map/ppermute | solution.py:661
  56.1 1.9 %shard_map.152 = (bf16[32,2,128]{2,1,0:T(2,128)(2,1)S(1)}, bf16[2,32,128,128]{3,2,1,0:T(8,128)(2,1)S(1)}) custom-call(bf16[16,80,128]{2,1,0:T(8,128)(2,1)S(1)} %all_to_all.21.r, bf16[1,32,128,128]{3,2,1,0:T(8,128)(2,1)S(1)} %get-tuple-element.34.kept, s32[1,4,32]{2,1,0:T(4,128)S(1)} %get-tuple-element.29.dst_in.dst_hbm, ...), custom_call_target="tpu_custom_call" | custom-call | flops 16777216 | bytes 1048576 | tf_op jit(solution)/shard_map/pallas_call | solution.py:662
  57.9 0.0 collective-permute-done.2.got
  57.9 0.7 shard_map.154
  58.6 12.2 %all-to-all-start.3 = ((bf16[160,4,128]{2,1,0:T(4,128)(2,1)}), bf16[160,4,128]{2,1,0:T(4,128)(2,1)S(1)}, u32[]{:S(2)}, u32[]{:S(2)}) async-start(bf16[160,4,128]{2,1,0:T(4,128)(2,1)} %shard_map.154), calls=%async_computation.3 | async-start | bytes 327680 | tf_op jit(solution)/shard_map/all_to_all | solution.py:551
  70.9 1.8 %shard_map.155 = (bf16[8,2048]{1,0:T(8,128)(2,1)S(1)}, bf16[8,2048]{1,0:T(8,128)(2,1)S(1)}) custom-call(bf16[16,80,128]{2,1,0:T(8,128)(2,1)S(1)} %all_to_all.21.r, bf16[2,32,128,128]{3,2,1,0:T(8,128)(2,1)S(1)} %get-tuple-element.42.near, s32[1,4,32]{2,1,0:T(4,128)S(1)} %get-tuple-element.29.dst_in.dst_hbm, s32[1,4,32]{2,1,0:T(4,128)S(1)} %get-tuple-element.30.src_in.src_hbm, ...), custom_call_target="tpu_custom_call" | custom-call | flops 33554432 | bytes 2097152 | tf_op jit(solution)/shard_map/pallas_call | solution.py:681
  72.7 0.2 collective-permute-start.3
  72.9 1.6 %collective-permute-start.4 = (bf16[8,2048]{1,0:T(8,128)(2,1)S(1)}, bf16[8,2048]{1,0:T(8,128)(2,1)S(1)}, u32[]{:S(2)}, u32[]{:S(2)}) collective-permute-start(bf16[8,2048]{1,0:T(8,128)(2,1)S(1)} %get-tuple-element.44), channel_id=1, source_target_pairs={{0,16},{16,32},{32,48},{48,64},{64,80},{80,96},{96,112},{112,128},... | collective-permute-start | bytes 98312 | tf_op jit(solution)/shard_map/ppermute | solution.py:545
  74.4 2.4 %shard_map.151 = (f32[8,2048]{1,0:T(8,128)S(1)}, bf16[16,2048]{1,0:T(8,128)(2,1)}) custom-call(bf16[16,80,128]{2,1,0:T(8,128)(2,1)S(1)} %all_to_all.21.r, bf16[1,4,32,128,128]{4,3,2,1,0:T(8,128)(2,1)} %tiles.5, s32[1,4,32]{2,1,0:T(4,128)S(1)} %get-tuple-element.29.dst_in.dst_hbm, s32[1,4,32]{2,1,0:T(4,128)S(1)} %get-tuple-element.30.src_in.src_hbm, ...), custom_call_target="tpu_custom_call" | custom-call | flops 16777216 | bytes 1048576 | tf_op jit(solution)/shard_map/pallas_call | solution.py:697
  76.9 3.0 %collective-permute-done.3.after = bf16[8,2048]{1,0:T(8,128)(2,1)S(1)} collective-permute-done((bf16[8,2048]{1,0:T(8,128)(2,1)S(1)}, bf16[8,2048]{1,0:T(8,128)(2,1)S(1)}, u32[]{:S(2)}, u32[]{:S(2)}) %collective-permute-start.3) | collective-permute-done | bytes 32800 | tf_op jit(solution)/shard_map/ppermute | solution.py:545
  79.8 0.0 collective-permute-done.4.before
  79.9 0.0 all-to-all-done.3.recv
  79.9 1.1 %shard_map.156 = (bf16[8,2048]{1,0:T(8,128)(2,1)}, f32[16,128]{1,0:T(8,128)}, f32[16,128]{1,0:T(8,128)}, f32[1,16]{1,0:T(1,128)}) custom-call(bf16[160,4,128]{2,1,0:T(4,128)(2,1)S(1)} %all-to-all-done.3.recv, s32[8,128]{1,0:T(8,128)S(1)} %get-tuple-element.40.index, f32[8,2048]{1,0:T(8,128)S(1)} %get-tuple-element.41.own, ...), custom_call_target="tpu_custom_call" | custom-call | tf_op jit(solution)/shard_map/pallas_call | solution.py:706
Async XLA Ops:
  2.7 24.2 %all-to-all-start = ((bf16[32,2,128]{2,1,0:T(2,128)(2,1)}), bf16[32,2,128]{2,1,0:T(2,128)(2,1)S(1)}, u32[]{:S(2)}, u32[]{:S(2)}) async-start(bf16[32,2,128]{2,1,0:T(2,128)(2,1)} %get-tuple-element.27), calls=%async_computation | async-start | bytes 32768 | tf_op jit(solution)/shard_map/all_to_all | solution.py:551
  20.2 3.7 %collective-permute-start = (bf16[8,2048]{1,0:T(8,128)(2,1)}, bf16[8,2048]{1,0:T(8,128)(2,1)S(1)}, u32[]{:S(2)}, u32[]{:S(2)}) collective-permute-start(bf16[8,2048]{1,0:T(8,128)(2,1)} %feat_hbm.1), channel_id=1, source_target_pairs={{0,16},{16,32},{32,48},{48,64},{64,80},{80,96},{96,112},{112,128},... | collective-permute-start | bytes 98312 | tf_op jit(solution)/shard_map/ppermute | solution.py:545
  21.6 3.7 %collective-permute-start.1 = (bf16[8,2048]{1,0:T(8,128)(2,1)}, bf16[8,2048]{1,0:T(8,128)(2,1)S(1)}, u32[]{:S(2)}, u32[]{:S(2)}) collective-permute-start(bf16[8,2048]{1,0:T(8,128)(2,1)} %feat_hbm.1), channel_id=1, source_target_pairs={{0,496},{16,0},{32,16},{48,32},{64,48},{80,64},{96,80},{112,96},{1... | collective-permute-start | bytes 98312 | tf_op jit(solution)/shard_map/ppermute | solution.py:545
  23.8 3.1 %copy-start = (bf16[16,2048]{1,0:T(8,128)(2,1)S(1)}, bf16[16,2048]{1,0:T(8,128)(2,1)}, u32[]{:S(2)}) copy-start(bf16[16,2048]{1,0:T(8,128)(2,1)} %cot.1) | copy-start | bytes 196612
  23.8 3.1 %copy-start.1 = (bf16[128,16]{0,1:T(8,128)(2,1)S(1)}, bf16[128,16]{0,1:T(8,128)(2,1)}, u32[]{:S(2)}) copy-start(bf16[128,16]{0,1:T(8,128)(2,1)} %param.18) | copy-start | bytes 12292
  23.8 3.1 %copy-start.2 = (bf16[128,16]{0,1:T(8,128)(2,1)S(1)}, bf16[128,16]{0,1:T(8,128)(2,1)}, u32[]{:S(2)}) copy-start(bf16[128,16]{0,1:T(8,128)(2,1)} %param.19) | copy-start | bytes 12292
  23.8 3.1 %copy-start.3 = (f32[16]{0:T(128)S(1)}, f32[16]{0:T(128)}, u32[]{:S(2)}) copy-start(f32[16]{0:T(128)} %param.20) | copy-start | bytes 196
  50.9 7.0 %collective-permute-start.2 = (f32[16,128]{1,0:T(8,128)S(1)}, f32[16,128]{1,0:T(8,128)S(1)}, u32[]{:S(2)}, u32[]{:S(2)}) collective-permute-start(f32[16,128]{1,0:T(8,128)S(1)} %get-tuple-element.39), channel_id=1, source_target_pairs={{0,16},{16,0},{32,48},{48,32},{64,80},{80,64},{96,112},{112,96},{1... | collective-permute-start | bytes 24584 | tf_op jit(solution)/shard_map/ppermute | solution.py:661
  58.6 21.2 %all-to-all-start.3 = ((bf16[160,4,128]{2,1,0:T(4,128)(2,1)}), bf16[160,4,128]{2,1,0:T(4,128)(2,1)S(1)}, u32[]{:S(2)}, u32[]{:S(2)}) async-start(bf16[160,4,128]{2,1,0:T(4,128)(2,1)} %shard_map.154), calls=%async_computation.3 | async-start | bytes 327680 | tf_op jit(solution)/shard_map/all_to_all | solution.py:551
  72.7 7.2 %collective-permute-start.3 = (bf16[8,2048]{1,0:T(8,128)(2,1)S(1)}, bf16[8,2048]{1,0:T(8,128)(2,1)S(1)}, u32[]{:S(2)}, u32[]{:S(2)}) collective-permute-start(bf16[8,2048]{1,0:T(8,128)(2,1)S(1)} %get-tuple-element.43), channel_id=1, source_target_pairs={{0,496},{16,0},{32,16},{48,32},{64,48},{80,64},{96,80},{112,96},{1... | collective-permute-start | bytes 98312 | tf_op jit(solution)/shard_map/ppermute | solution.py:545
  72.9 7.0 %collective-permute-start.4 = (bf16[8,2048]{1,0:T(8,128)(2,1)S(1)}, bf16[8,2048]{1,0:T(8,128)(2,1)S(1)}, u32[]{:S(2)}, u32[]{:S(2)}) collective-permute-start(bf16[8,2048]{1,0:T(8,128)(2,1)S(1)} %get-tuple-element.44), channel_id=1, source_target_pairs={{0,16},{16,32},{32,48},{48,64},{64,80},{80,96},{96,112},{112,128},... | collective-permute-start | bytes 98312 | tf_op jit(solution)/shard_map/ppermute | solution.py:545

commit v7 on v5

--- a/solution.py
+++ b/solution.py
@@ -23,8 +23,8 @@
 RET = 5
 FWD_ROWS = 80
 BWD_ROWS = 80
-ROW_OUT, ROW_BACK = 22, 16
-COL_OUT, COL_BACK = 11, 10
+ROW_OUT, ROW_BACK = 22, 14
+COL_OUT, COL_BACK = 10, 10
 F32, BF16 = jnp.float32, jnp.bfloat16
 NT = (((1,), (1,)), ((), ()))
 TN = (((0,), (0,)), ((), ()))

time: 81.3 us -> 80.6 us (level)
  waiting for transfers between devices: 2.37 us -> 4.92 us
  blocking collectives: 23.6 us -> 21.7 us
  Pallas kernels: 16.1 us -> 14.6 us
    all_to_all x2, starting transfers between devices: 30.7 us -> 28.5 us  [swap(): return lax.all_to_all(x, axis, 0, 0, axis_index_groups=[group], tiled=True)]
    ppermute x1, starting transfers between devices: 4.05 us -> 6.01 us  [per_device(): lax.ppermute(given_half, 'row', [(i, i ^ 1) for i in range(NROW)])]
    all_to_all x2, blocking collectives: 23.6 us -> 21.7 us  [swap(): return lax.all_to_all(x, axis, 0, 0, axis_index_groups=[group], tiled=True)]
    all_to_all x2, waiting for transfers between devices: 0.01 us -> 1.89 us  [swap(): return lax.all_to_all(x, axis, 0, 0, axis_index_groups=[group], tiled=True)]
  transfers between devices with their start and end apart: 7 -> 7, of which waited for: 1 -> 3; matrix products, arithmetic and copies ran while one was open for 0% -> 0% of each run, Pallas kernels for 13% -> 11%
where the time goes in v7:
time: 80.6 us; the launch traced here: 80.1 us
  starting transfers between devices  38.1 us (47%)
  blocking collectives  21.7 us (27%)
  Pallas kernels  14.6 us (18%)
  waiting for transfers between devices  4.92 us (6%)
  between operations  0.81 us (1%)
    all_to_all x2, starting transfers between devices, swap(): return lax.all_to_all(x, axis, 0, 0, axis_index_groups=[group], tiled=True)  28.5 us
    all_to_all x2, blocking collectives, swap(): return lax.all_to_all(x, axis, 0, 0, axis_index_groups=[group], tiled=True)  21.7 us
    ppermute x1, starting transfers between devices, per_device(): lax.ppermute(given_half, 'row', [(i, i ^ 1) for i in range(NROW)])  6.01 us
    ppermute x4, starting transfers between devices, shifted(): lax.ppermute(shard, 'row', [(i, (i + by) % NROW) for i in range(NROW)])  3.52 us
    ppermute x4, waiting for transfers between devices, shifted(): lax.ppermute(shard, 'row', [(i, (i + by) % NROW) for i in range(NROW)])  3.02 us
    pallas_call x1, Pallas kernels, per_device(): call(back_own_kernel, (sds((FEAT, NODES_LOC), F32), sds((HLOC, NODES_LOC)...  2.42 us
    pallas_call x1, Pallas kernels, per_device(): call(gather_kernel, (sds((NROW, 2, TILE), BF16), sds((NB, TILE), jnp.int3...  2.1 us
    pallas_call x1, Pallas kernels, per_device(): call(own_kernel, (sds((RT, FEAT, TILE), F32), sds((2, 32, TILE, TILE), BF...  2.04 us
  transfers between devices with their start and end apart: 7, of which 3 were waited for; matrix products, arithmetic and copies ran while one was open for 0% of the time, Pallas kernels for 11%

profile of v7, /device:TPU:1, one launch (start us, length us, event | category | flops | bytes accessed | tf_op | source)
XLA Modules:
  0.0 80.1 jit_solution(16564472428693722585)
XLA Ops:
  0.6 0.0 copy-start
  0.6 0.0 copy-start.3
  0.7 0.0 copy-start.2
  0.7 0.0 copy-start.1
  0.7 2.1 %shard_map.146 = (bf16[32,2,128]{2,1,0:T(2,128)(2,1)}, s32[8,128]{1,0:T(8,128)S(1)}, bf16[8,2048]{1,0:T(8,128)(2,1)S(1)}, s32[1,4,32]{2,1,0:T(4,128)S(1)}, s32[1,4,32]{2,1,0:T(4,128)S(1)}, /*index=5*/s32[1,4]{1,0:T(1,128)S(1)}) custom-call(bf16[8,2048]{1,0:T(8,128)(2,1)} %feat_hbm.1, s32[1,32,32]{2,1,0:T(8,128)} %rows_hbm.1, s32[1,32]{1,0:T(1,128)} %counts_hbm.1, ...), custom_call_target="tpu_custom_call" | custom-call | flops 33554432 | tf_op jit(solution)/shard_map/pallas_call | solution.py:546
  2.8 17.5 %all-to-all-start = ((bf16[32,2,128]{2,1,0:T(2,128)(2,1)}), bf16[32,2,128]{2,1,0:T(2,128)(2,1)S(1)}, u32[]{:S(2)}, u32[]{:S(2)}) async-start(bf16[32,2,128]{2,1,0:T(2,128)(2,1)} %get-tuple-element.25), calls=%async_computation | async-start | bytes 32768 | tf_op jit(solution)/shard_map/all_to_all | solution.py:524
  20.2 0.4 collective-permute-start.1
  20.6 1.4 %collective-permute-start = (bf16[8,2048]{1,0:T(8,128)(2,1)}, bf16[8,2048]{1,0:T(8,128)(2,1)S(1)}, u32[]{:S(2)}, u32[]{:S(2)}) collective-permute-start(bf16[8,2048]{1,0:T(8,128)(2,1)} %feat_hbm.1), channel_id=1, source_target_pairs={{0,16},{16,32},{32,48},{48,64},{64,80},{80,96},{96,112},{112,128},... | collective-permute-start | bytes 98312 | tf_op jit(solution)/shard_map/ppermute | solution.py:518
  22.0 2.0 %shard_map.147 = (f32[16,8,128]{2,1,0:T(8,128)S(1)}, bf16[2,32,128,128]{3,2,1,0:T(8,128)(2,1)S(1)}, bf16[1,32,128,128]{3,2,1,0:T(8,128)(2,1)S(1)}) custom-call(bf16[8,2048]{1,0:T(8,128)(2,1)S(1)} %get-tuple-element.26.feat, s32[1,4,32]{2,1,0:T(4,128)S(1)} %get-tuple-element.27.dst_in.dst_hbm, s32[1,4,32]{2,1,0:T(4,128)S(1)} %get-tuple-element.28.src_in.src_hbm, ...), custom_call_target="tpu_custom_call" | custom-call | flops 16777216 | bytes 4194304 | tf_op jit(solution)/shard_map/pallas_call | solution.py:567
  24.0 0.1 collective-permute-done.1.foll
  24.1 0.0 collective-permute-done.prev
  24.1 1.1 %shard_map.148.part = f32[16,8,128]{2,1,0:T(8,128)S(1)} custom-call(bf16[8,2048]{1,0:T(8,128)(2,1)S(1)} %collective-permute-done.prev, bf16[8,2048]{1,0:T(8,128)(2,1)S(1)} %collective-permute-done.1.foll, f32[16,8,128]{2,1,0:T(8,128)S(1)} %get-tuple-element.30.before, bf16[2,32,128,128]{3,2,1,0:T(8,128)(2,1)S(1)} %get-tuple-element.31.near, ...), custom_call_target="tpu_custom_call" | custom-call | flops 33554432 | bytes 2097152 | tf_op jit(solution)/shard_map/pallas_call | solution.py:588
  25.2 0.0 all-to-all-done.recv
  25.2 0.0 copy-done
  25.3 0.0 copy-done.3
  25.3 0.0 copy-done.2
  25.3 0.0 copy-done.1
  25.3 1.2 %shard_map.149 = bf16[16,80,128]{2,1,0:T(8,128)(2,1)S(1)} custom-call(bf16[32,2,128]{2,1,0:T(2,128)(2,1)S(1)} %all-to-all-done.recv, f32[16,8,128]{2,1,0:T(8,128)S(1)} %shard_map.148.part, bf16[8,2048]{1,0:T(8,128)(2,1)S(1)} %get-tuple-element.26.feat, bf16[16,2048]{1,0:T(8,128)(2,1)S(1)} %copy-done, bf16[16,128]{1,0:T(8,128)(2,1)S(1)} %bitcast.6, ...), custom_call_target="tpu_custom_call" | custom-call | flops 16777216 | bytes 1048576 | tf_op jit(solution)/shard_map/pallas_call | solution.py:597
  26.5 11.6 %all_to_all.20.r = bf16[16,80,128]{2,1,0:T(8,128)(2,1)S(1)} all-to-all(bf16[16,80,128]{2,1,0:T(8,128)(2,1)S(1)} %shard_map.149), channel_id=1, replica_groups={{10,11,12,13,14,15,0,1,2,3,4,5,6,7,8,9},{26,27,28,29,30,31,16,17,18,19,..., dimensions={0} | all-to-all | bytes 655360 | tf_op jit(solution)/shard_map/all_to_all | solution.py:524
  38.1 0.4 shard_map.150
  38.6 10.1 %all_to_all.21.r = bf16[16,80,128]{2,1,0:T(8,128)(2,1)S(1)} all-to-all(bf16[16,80,128]{2,1,0:T(8,128)(2,1)S(1)} %shard_map.150), channel_id=1, replica_groups={{10,11,12,13,14,15,0,1,2,3,4,5,6,7,8,9},{26,27,28,29,30,31,16,17,18,19,..., dimensions={0} | all-to-all | bytes 655360 | tf_op jit(solution)/shard_map/all_to_all | solution.py:524
  48.7 0.1 shard_map.153
  48.8 6.0 %collective-permute-start.2 = (f32[16,128]{1,0:T(8,128)S(1)}, f32[16,128]{1,0:T(8,128)S(1)}, u32[]{:S(2)}, u32[]{:S(2)}) collective-permute-start(f32[16,128]{1,0:T(8,128)S(1)} %get-tuple-element.36), channel_id=1, source_target_pairs={{0,16},{16,0},{32,48},{48,32},{64,80},{80,64},{96,112},{112,96},{1... | collective-permute-start | bytes 24584 | tf_op jit(solution)/shard_map/ppermute | solution.py:634
  54.8 1.5 %shard_map.152.far = bf16[32,2,128]{2,1,0:T(2,128)(2,1)S(1)} custom-call(bf16[16,80,128]{2,1,0:T(8,128)(2,1)S(1)} %all_to_all.21.r, bf16[1,32,128,128]{3,2,1,0:T(8,128)(2,1)S(1)} %get-tuple-element.32.kept, s32[1,4,32]{2,1,0:T(4,128)S(1)} %get-tuple-element.27.dst_in.dst_hbm, s32[1,4,32]{2,1,0:T(4,128)S(1)} %get-tuple-element.28.src_in.src_hbm, ...), custom_call_target="tpu_custom_call" | custom-call | flops 16777216 | bytes 1048576 | tf_op jit(solution)/shard_map/pallas_call | solution.py:635
  56.3 0.0 collective-permute-done.2.got
  56.3 0.7 shard_map.154
  57.0 11.1 %all-to-all-start.3 = ((bf16[160,4,128]{2,1,0:T(4,128)(2,1)}), bf16[160,4,128]{2,1,0:T(4,128)(2,1)S(1)}, u32[]{:S(2)}, u32[]{:S(2)}) async-start(bf16[160,4,128]{2,1,0:T(4,128)(2,1)} %shard_map.154), calls=%async_computation.3 | async-start | bytes 327680 | tf_op jit(solution)/shard_map/all_to_all | solution.py:524
  68.1 1.8 %shard_map.155 = (bf16[8,2048]{1,0:T(8,128)(2,1)S(1)}, bf16[8,2048]{1,0:T(8,128)(2,1)S(1)}) custom-call(bf16[16,80,128]{2,1,0:T(8,128)(2,1)S(1)} %all_to_all.21.r, bf16[1,4,32,128,128]{4,3,2,1,0:T(8,128)(2,1)} %tiles.5, s32[1,4,32]{2,1,0:T(4,128)S(1)} %get-tuple-element.27.dst_in.dst_hbm, s32[1,4,32]{2,1,0:T(4,128)S(1)} %get-tuple-element.28.src_in.src_hbm, ...), custom_call_target="tpu_custom_call" | custom-call | flops 33554432 | bytes 2097152 | tf_op jit(solution)/shard_map/pallas_call | solution.py:653
  69.9 0.8 collective-permute-start.3
  70.7 1.0 %collective-permute-start.4 = (bf16[8,2048]{1,0:T(8,128)(2,1)S(1)}, bf16[8,2048]{1,0:T(8,128)(2,1)S(1)}, u32[]{:S(2)}, u32[]{:S(2)}) collective-permute-start(bf16[8,2048]{1,0:T(8,128)(2,1)S(1)} %get-tuple-element.40), channel_id=1, source_target_pairs={{0,16},{16,32},{32,48},{48,64},{64,80},{80,96},{96,112},{112,128},... | collective-permute-start | bytes 98312 | tf_op jit(solution)/shard_map/ppermute | solution.py:518
  71.7 2.4 %shard_map.151 = (f32[8,2048]{1,0:T(8,128)S(1)}, bf16[16,2048]{1,0:T(8,128)(2,1)}) custom-call(bf16[16,80,128]{2,1,0:T(8,128)(2,1)S(1)} %all_to_all.21.r, bf16[1,4,32,128,128]{4,3,2,1,0:T(8,128)(2,1)} %tiles.5, s32[1,4,32]{2,1,0:T(4,128)S(1)} %get-tuple-element.27.dst_in.dst_hbm, s32[1,4,32]{2,1,0:T(4,128)S(1)} %get-tuple-element.28.src_in.src_hbm, ...), custom_call_target="tpu_custom_call" | custom-call | flops 16777216 | bytes 1048576 | tf_op jit(solution)/shard_map/pallas_call | solution.py:664
  74.1 3.0 %collective-permute-done.3.after = bf16[8,2048]{1,0:T(8,128)(2,1)S(1)} collective-permute-done((bf16[8,2048]{1,0:T(8,128)(2,1)S(1)}, bf16[8,2048]{1,0:T(8,128)(2,1)S(1)}, u32[]{:S(2)}, u32[]{:S(2)}) %collective-permute-start.3) | collective-permute-done | bytes 32800 | tf_op jit(solution)/shard_map/ppermute | solution.py:518
  77.1 0.0 collective-permute-done.4.before
  77.1 1.9 %all-to-all-done.3.recv = bf16[160,4,128]{2,1,0:T(4,128)(2,1)S(1)} async-done(((bf16[160,4,128]{2,1,0:T(4,128)(2,1)}), bf16[160,4,128]{2,1,0:T(4,128)(2,1)S(1)}, u32[]{:S(2)}, u32[]{:S(2)}) %all-to-all-start.3) | async-done | bytes 163872 | tf_op jit(solution)/shard_map/all_to_all | solution.py:524
  79.0 1.1 %shard_map.156 = (bf16[8,2048]{1,0:T(8,128)(2,1)}, f32[16,128]{1,0:T(8,128)}, f32[16,128]{1,0:T(8,128)}, f32[1,16]{1,0:T(1,128)}) custom-call(bf16[160,4,128]{2,1,0:T(4,128)(2,1)S(1)} %all-to-all-done.3.recv, s32[8,128]{1,0:T(8,128)S(1)} %get-tuple-element.37.index, f32[8,2048]{1,0:T(8,128)S(1)} %get-tuple-element.38.own, ...), custom_call_target="tpu_custom_call" | custom-call | tf_op jit(solution)/shard_map/pallas_call | solution.py:673
Async XLA Ops:
  0.6 24.6 %copy-start = (bf16[16,2048]{1,0:T(8,128)(2,1)S(1)}, bf16[16,2048]{1,0:T(8,128)(2,1)}, u32[]{:S(2)}) copy-start(bf16[16,2048]{1,0:T(8,128)(2,1)} %cot.1) | copy-start | bytes 196612
  0.6 24.6 %copy-start.3 = (f32[16]{0:T(128)S(1)}, f32[16]{0:T(128)}, u32[]{:S(2)}) copy-start(f32[16]{0:T(128)} %param.20) | copy-start | bytes 196
  0.7 24.6 %copy-start.2 = (bf16[128,16]{0,1:T(8,128)(2,1)S(1)}, bf16[128,16]{0,1:T(8,128)(2,1)}, u32[]{:S(2)}) copy-start(bf16[128,16]{0,1:T(8,128)(2,1)} %param.19) | copy-start | bytes 12292
  0.7 24.6 %copy-start.1 = (bf16[128,16]{0,1:T(8,128)(2,1)S(1)}, bf16[128,16]{0,1:T(8,128)(2,1)}, u32[]{:S(2)}) copy-start(bf16[128,16]{0,1:T(8,128)(2,1)} %param.18) | copy-start | bytes 12292
  2.8 22.5 %all-to-all-start = ((bf16[32,2,128]{2,1,0:T(2,128)(2,1)}), bf16[32,2,128]{2,1,0:T(2,128)(2,1)S(1)}, u32[]{:S(2)}, u32[]{:S(2)}) async-start(bf16[32,2,128]{2,1,0:T(2,128)(2,1)} %get-tuple-element.25), calls=%async_computation | async-start | bytes 32768 | tf_op jit(solution)/shard_map/all_to_all | solution.py:524
  20.2 3.9 %collective-permute-start.1 = (bf16[8,2048]{1,0:T(8,128)(2,1)}, bf16[8,2048]{1,0:T(8,128)(2,1)S(1)}, u32[]{:S(2)}, u32[]{:S(2)}) collective-permute-start(bf16[8,2048]{1,0:T(8,128)(2,1)} %feat_hbm.1), channel_id=1, source_target_pairs={{0,496},{16,0},{32,16},{48,32},{64,48},{80,64},{96,80},{112,96},{1... | collective-permute-start | bytes 98312 | tf_op jit(solution)/shard_map/ppermute | solution.py:518
  20.6 3.5 %collective-permute-start = (bf16[8,2048]{1,0:T(8,128)(2,1)}, bf16[8,2048]{1,0:T(8,128)(2,1)S(1)}, u32[]{:S(2)}, u32[]{:S(2)}) collective-permute-start(bf16[8,2048]{1,0:T(8,128)(2,1)} %feat_hbm.1), channel_id=1, source_target_pairs={{0,16},{16,32},{32,48},{48,64},{64,80},{80,96},{96,112},{112,128},... | collective-permute-start | bytes 98312 | tf_op jit(solution)/shard_map/ppermute | solution.py:518
  48.8 7.5 %collective-permute-start.2 = (f32[16,128]{1,0:T(8,128)S(1)}, f32[16,128]{1,0:T(8,128)S(1)}, u32[]{:S(2)}, u32[]{:S(2)}) collective-permute-start(f32[16,128]{1,0:T(8,128)S(1)} %get-tuple-element.36), channel_id=1, source_target_pairs={{0,16},{16,0},{32,48},{48,32},{64,80},{80,64},{96,112},{112,96},{1... | collective-permute-start | bytes 24584 | tf_op jit(solution)/shard_map/ppermute | solution.py:634
  57.0 22.0 %all-to-all-start.3 = ((bf16[160,4,128]{2,1,0:T(4,128)(2,1)}), bf16[160,4,128]{2,1,0:T(4,128)(2,1)S(1)}, u32[]{:S(2)}, u32[]{:S(2)}) async-start(bf16[160,4,128]{2,1,0:T(4,128)(2,1)} %shard_map.154), calls=%async_computation.3 | async-start | bytes 327680 | tf_op jit(solution)/shard_map/all_to_all | solution.py:524
  69.9 7.2 %collective-permute-start.3 = (bf16[8,2048]{1,0:T(8,128)(2,1)S(1)}, bf16[8,2048]{1,0:T(8,128)(2,1)S(1)}, u32[]{:S(2)}, u32[]{:S(2)}) collective-permute-start(bf16[8,2048]{1,0:T(8,128)(2,1)S(1)} %get-tuple-element.39), channel_id=1, source_target_pairs={{0,496},{16,0},{32,16},{48,32},{64,48},{80,64},{96,80},{112,96},{1... | collective-permute-start | bytes 98312 | tf_op jit(solution)/shard_map/ppermute | solution.py:518
  70.7 6.4 %collective-permute-start.4 = (bf16[8,2048]{1,0:T(8,128)(2,1)S(1)}, bf16[8,2048]{1,0:T(8,128)(2,1)S(1)}, u32[]{:S(2)}, u32[]{:S(2)}) collective-permute-start(bf16[8,2048]{1,0:T(8,128)(2,1)S(1)} %get-tuple-element.40), channel_id=1, source_target_pairs={{0,16},{16,32},{32,48},{48,64},{64,80},{80,96},{96,112},{112,128},... | collective-permute-start | bytes 98312 | tf_op jit(solution)/shard_map/ppermute | solution.py:518
